TPU v7x, 128 devices: a whole 4x4x4 slice. The times are simulated.
128 devices in a mesh: obs: 4 (over z), td: 32 (over y, x, core).
Axes of the slice: x: 4, y: 4, z: 4, core: 2. Of those that a mesh axis runs over, the one named last changes fastest.
Arguments:
- timestreams: bfloat16 [4, 512, 32768], P('obs', 'td'), may hold values from -6 to 6
- filter_taps: bfloat16 [4, 512, 8, 129], P('obs', 'td'), may hold values from -0.5 to 0.5
- scan_bounds: int32 [4, 32], P('obs'), may hold values from 0 to 32768, as said below
- tile_index: int32 [4, 256], P('obs', 'td'), may hold values from 0 to 15
- det_weights: bfloat16 [4, 512], P('obs'), may hold values from 0.29882812 to 3
- positions: float32 [2, 512], replicated, may hold values from -1 to 1
- wafer_group: int32 [512], replicated, may hold values from 0 to 7, as said below
Outputs:
- filtered_residual: float32 [4, 512, 32768], P('obs', 'td')
- sky_map: float32 [16, 128, 128], P(None, ('obs', 'td'))
Inputs may be any that keep to these rules, and one draw needn't show every extreme that they name: `scan_bounds`: each row is strictly increasing, starts with 0 and ends with 32768. `wafer_group`: every wafer group holds the same number of detectors.
All inputs are finite; a program needn't handle non-finite values.
Results may differ from a plain program's by a relative error of at most 0.009.
Values may be sent and summed in bfloat16 or wider, within the bound.
No kernel may reach another device: no remote copies, remote signals or barrier semaphores. Data moves between devices by JAX's collectives and lax.ppermute only.
A program may use at most 128 MiB of HBM per device.

v0:
```python
import jax
import jax.numpy as jnp
from jax import lax
from jax.sharding import PartitionSpec as P

TAPS = 129
BANDS = 8
TILE = 128
WAFERS = 8
POLY = 6
TILES = 16


prior_weight = 1.0


def toeplitz(band_taps):
    leading = band_taps.shape[:-1]
    half = TAPS // 2
    padded = jnp.concatenate(
        [
            jnp.zeros(leading + (TILE - half,), band_taps.dtype),
            band_taps,
            jnp.zeros(leading + (3 * TILE - TAPS + half,), band_taps.dtype),
        ],
        axis=-1,
    )
    repeated = jnp.tile(padded, (1,) * len(leading) + (TILE,))
    repeated = repeated[..., : TILE * (4 * TILE - 1)].reshape(leading + (TILE, 4 * TILE - 1))
    return repeated[..., : 3 * TILE]


def windows_of(signal):
    blocks = jnp.pad(signal, ((0, 0), (0, 0), (TILE, TILE)))
    blocks = blocks.reshape(signal.shape[0], signal.shape[1], -1, TILE)
    return jnp.concatenate([blocks[:, :, :-2], blocks[:, :, 1:-1], blocks[:, :, 2:]], axis=-1)


def forward_filter(signal, filter_taps):
    windows = windows_of(signal)
    per_band = windows.shape[2] // BANDS
    pieces = []
    for band_idx in range(BANDS):
        kernel = toeplitz(filter_taps[:, :, band_idx])
        band_part = windows[:, :, band_idx * per_band : (band_idx + 1) * per_band]
        pieces.append(
            jnp.einsum("odnj,odij->odni", band_part, kernel, preferred_element_type=jnp.float32)
        )
    return jnp.concatenate(pieces, axis=2).reshape(signal.shape)


def adjoint_filter(signal, filter_taps):
    blocks = signal.reshape(signal.shape[0], signal.shape[1], -1, TILE)
    per_band = blocks.shape[2] // BANDS
    pieces = []
    for band_idx in range(BANDS):
        kernel = toeplitz(filter_taps[:, :, band_idx])
        band_part = blocks[:, :, band_idx * per_band : (band_idx + 1) * per_band]
        pieces.append(
            jnp.einsum("odni,odij->odnj", band_part, kernel, preferred_element_type=jnp.float32)
        )
    spread = jnp.concatenate(pieces, axis=2)
    zero_block = jnp.zeros(spread.shape[:2] + (1, TILE), jnp.float32)
    from_next = jnp.concatenate([spread[:, :, 1:, :TILE], zero_block], axis=2)
    from_prev = jnp.concatenate([zero_block, spread[:, :, :-1, 2 * TILE :]], axis=2)
    summed = spread[:, :, :, TILE : 2 * TILE] + from_next + from_prev
    return summed.reshape(signal.shape)


def make_basis(positions, wafer_group):
    x_pos = positions[0]
    y_pos = positions[1]
    monomials = jnp.stack(
        [jnp.ones_like(x_pos), x_pos, y_pos, x_pos * x_pos, x_pos * y_pos, y_pos * y_pos]
    )
    member = (wafer_group[None, :] == jnp.arange(WAFERS, dtype=jnp.int32)[:, None]).astype(
        jnp.float32
    )
    basis_b = (member[:, None, :] * monomials[None]).reshape(WAFERS * POLY, -1).astype(jnp.bfloat16)
    basis_f = basis_b.astype(jnp.float32)
    gram_matrix = jnp.dot(basis_f, basis_f.T, precision=lax.Precision.HIGHEST)
    factor = jnp.linalg.cholesky(gram_matrix)
    lower_inv = lax.linalg.triangular_solve(
        factor, jnp.eye(WAFERS * POLY, dtype=jnp.float32), left_side=True, lower=True
    )
    inverse = jnp.dot(lower_inv.T, lower_inv, precision=lax.Precision.HIGHEST)
    return (basis_b, basis_f, inverse)


def remove_poly(gathered, basis):
    basis_b, basis_f, inverse = basis
    coef_raw = jnp.einsum("md,nds->nms", basis_b, gathered, preferred_element_type=jnp.float32)
    coefficients = jnp.einsum("mq,nqs->nms", inverse, coef_raw, precision=lax.Precision.HIGHEST)
    coef_high = coefficients.astype(jnp.bfloat16)
    coef_low = (coefficients - coef_high.astype(jnp.float32)).astype(jnp.bfloat16)
    fitted = jnp.einsum("md,nms->nds", basis_b, coef_high, preferred_element_type=jnp.float32)
    fitted = fitted + jnp.einsum(
        "md,nms->nds", basis_b, coef_low, preferred_element_type=jnp.float32
    )
    return (gathered.astype(jnp.float32) - fitted).astype(jnp.bfloat16)


def scan_flags(bounds, offset, length):
    sample = offset + jnp.arange(length, dtype=jnp.int32)
    passed = jnp.sum((bounds[:, :, None] <= sample[None, None, :]).astype(jnp.int32), axis=1)
    return (passed % 2).astype(jnp.float32)


def bin_maps(cleaned, in_scan, det_weights, tile_index):
    obs_count, det_count, samples = cleaned.shape
    groups = det_count // TILE
    block_count = samples // TILE
    masked = cleaned * in_scan[:, None, :].astype(jnp.bfloat16)
    shaped = masked.reshape(obs_count, groups, TILE, block_count, TILE)
    weight_rows = det_weights.reshape(obs_count, groups, TILE)
    block_sums = jnp.einsum(
        "oqr,oqrbc->obrc", weight_rows, shaped, preferred_element_type=jnp.float32
    )
    row_weight = jnp.sum(weight_rows.astype(jnp.float32), axis=1)
    one_hot = (tile_index[:, :, None] == jnp.arange(TILES, dtype=jnp.int32)[None, None, :]).astype(
        jnp.float32
    )
    weighted_sum = jnp.einsum("obt,obrc->trc", one_hot, block_sums, precision=lax.Precision.HIGHEST)
    scan_blocks = in_scan.reshape(obs_count, block_count, TILE)
    hit_weight = jnp.einsum(
        "obt,or,obc->trc", one_hot, row_weight, scan_blocks, precision=lax.Precision.HIGHEST
    )
    return (weighted_sum, hit_weight, one_hot)


def rescan_residual(cleaned, in_scan, sky_b, one_hot):
    obs_count, det_count, samples = cleaned.shape
    groups = det_count // TILE
    block_count = samples // TILE
    selected = jnp.einsum(
        "obt,trc->orbc", one_hot.astype(jnp.bfloat16), sky_b, preferred_element_type=jnp.float32
    )
    shaped = cleaned.astype(jnp.float32).reshape(obs_count, groups, TILE, block_count, TILE)
    deviation = shaped - selected[:, None]
    flags = in_scan.reshape(obs_count, 1, 1, block_count, TILE)
    return (flags * deviation).astype(jnp.bfloat16).reshape(obs_count, det_count, samples)


def local(timestreams, filter_taps, scan_bounds, tile_index, det_weights, positions, wafer_group):
    filtered = forward_filter(timestreams, filter_taps).astype(jnp.bfloat16)
    basis = make_basis(positions, wafer_group)
    cleaned = remove_poly(
        lax.all_to_all(filtered, "td", split_axis=2, concat_axis=1, tiled=True), basis
    )
    slab_len = cleaned.shape[2]
    offset = lax.axis_index("td") * slab_len
    in_scan = scan_flags(scan_bounds, offset, slab_len)
    weighted_sum, hit_weight, one_hot = bin_maps(cleaned, in_scan, det_weights, tile_index)
    own_rows = TILE // lax.axis_size(("obs", "td"))
    row_start = lax.axis_index(("obs", "td")) * own_rows
    stacked = jnp.stack([weighted_sum, hit_weight])
    totals = lax.psum(stacked, ("obs", "td"))
    hits = totals[1]
    whole_map = totals[0] / (hits + prior_weight)
    sky_own = lax.dynamic_slice_in_dim(whole_map, row_start, own_rows, 1)
    sky_b = whole_map.astype(jnp.bfloat16)
    residual = rescan_residual(cleaned, in_scan, sky_b, one_hot)
    returned = lax.all_to_all(residual, "td", split_axis=1, concat_axis=2, tiled=True)
    return (adjoint_filter(returned, filter_taps), sky_own)


def solution(mesh):
    placed = (
        P("obs", "td", None),
        P("obs", "td", None, None),
        P("obs", None),
        P("obs", "td"),
        P("obs", None),
        P(),
        P(),
    )
    return jax.shard_map(
        local,
        mesh=mesh,
        in_specs=placed,
        out_specs=(P("obs", "td", None), P(None, ("obs", "td"), None)),
        check_vma=False,
    )
```

profile of v0, /device:TPU:1, one launch (start us, length us, event | category | flops | bytes accessed | tf_op | source)
XLA Modules:
  0.0 620.7 jit_solution(3578517123573770558)
XLA Ops:
  9.0 2.0 tile.50
  10.9 1.6 slice-done
  12.5 4.9 reshape.624
  18.1 2.0 fusion.90
  20.2 2.0 tile.53
  22.2 1.6 slice-done.1
  23.8 4.9 reshape.627
  28.9 2.0 tile.56
  30.9 1.6 slice-done.2
  32.4 5.0 reshape.630
  37.6 2.0 tile.59
  39.5 1.6 slice-done.3
  41.1 4.9 reshape.633
  46.2 2.0 tile.62
  48.2 1.6 slice-done.4
  49.7 5.5 reshape.636
  55.4 2.0 tile.65
  57.3 1.6 slice-done.5
  58.9 4.9 reshape.639
  64.0 2.0 tile.68
  66.0 1.6 slice-done.6
  67.6 4.9 reshape.642
  72.6 2.0 tile.71
  76.2 5.1 reshape.645
  81.3 2.2 pad_maximum_fusion
  91.5 25.1 %copy.66 = bf16[1,16,32768]{1,0,2:T(2,128)(2,1)} copy(bf16[1,16,32768]{2,1,0:T(8,128)(2,1)S(1)} %convert_element_type.195) | data formatting | bytes 2097152 | tf_op jit(solution)/shard_map/convert_element_type | solution.py:145
  117.2 179.2 %reduce.12 = bf16[32768,16]{1,0:T(8,128)(2,1)} reduce(bf16[32768,1,16]{2,1,0:T(2,128)(2,1)} %bitcast.377, bf16[]{:T(256)} %broadcast.361), dimensions={1}, to_apply=%bitcast.360.reduce_sub_computation | reduce | bytes 2097154
  296.3 11.2 %reshape.670 = bf16[32,2,8192]{2,1,0:T(2,128)(2,1)} reshape(bf16[32768,16]{1,0:T(8,128)(2,1)} %reduce.12) | data formatting | bytes 2097152
  307.6 8.7 %all-to-all-start = ((bf16[32,2,8192]{2,1,0:T(2,128)(2,1)}), bf16[32,2,8192]{2,1,0:T(2,128)(2,1)S(1)}, u32[]{:S(2)}, u32[]{:S(2)}) async-start(bf16[32,2,8192]{2,1,0:T(2,128)(2,1)} %reshape.670), calls=%async_computation | async-start | bytes 2097152 | tf_op jit(solution)/shard_map/all_to_all | solution.py:148
  316.9 4.4 cholesky.17
  322.6 3.7 custom-call.6
  327.4 6.1 all-to-all-done
  333.5 19.3 %reshape.671 = bf16[32768,1,16]{2,1,0:T(2,128)(2,1)} reshape(bf16[32,2,8192]{2,1,0:T(2,128)(2,1)S(1)} %all-to-all-done) | data formatting | bytes 2097152
  352.8 29.6 %copy.67 = bf16[1,16,32768]{2,1,0:T(8,128)(2,1)S(1)} copy(bf16[1,16,32768]{1,0,2:T(2,128)(2,1)} %bitcast.378) | data formatting | bytes 2097152 | tf_op jit(solution)/shard_map/all_to_all | solution.py:148
  385.0 2.5 copy.68
  387.6 2.9 copy.71
  390.5 3.5 broadcast_multiply_fusion
  399.1 148.9 %all-reduce.5.cloned.1.call-done = f32[2,16,128,128]{3,1,2,0:T(8,128)} async-done(((f32[2,16,128,128]{3,1,2,0:T(8,128)}), f32[2,16,128,128]{3,1,2,0:T(8,128)}) %all-reduce.5.cloned.1.call-update) | async-done | bytes 2097168 | tf_op jit(solution)/shard_map/psum | solution.py:157
  548.0 1.7 fusion.58
  550.2 1.7 sub.24
  551.9 2.1 sub.25
  554.0 2.5 multiply_convert_fusion
  556.5 5.0 copy.73
  561.5 7.8 %reduce.13 = bf16[512,1024]{1,0:T(8,128)(2,1)} reduce(bf16[512,1,1024]{2,1,0:T(2,128)(2,1)S(1)} %bitcast.380, bf16[]{:T(256)} %broadcast.361), dimensions={1}, to_apply=%bitcast.362.reduce_sub_computation | reduce | bytes 2097154
  569.3 2.6 reshape.672
  571.9 6.9 %all-to-all-start.1 = ((bf16[32,2,8192]{2,1,0:T(2,128)(2,1)}), bf16[32,2,8192]{2,1,0:T(2,128)(2,1)}, u32[]{:S(2)}, u32[]{:S(2)}) async-start(bf16[32,2,8192]{2,1,0:T(2,128)(2,1)} %reshape.672), calls=%async_computation.1 | async-start | bytes 2097152 | tf_op jit(solution)/shard_map/all_to_all | solution.py:163
  579.4 16.4 %all-to-all-done.1 = bf16[32,2,8192]{2,1,0:T(2,128)(2,1)} async-done(((bf16[32,2,8192]{2,1,0:T(2,128)(2,1)}), bf16[32,2,8192]{2,1,0:T(2,128)(2,1)}, u32[]{:S(2)}, u32[]{:S(2)}) %all-to-all-start.1) | async-done | bytes 1048608 | tf_op jit(solution)/shard_map/all_to_all | solution.py:163
  595.9 4.3 reshape.673
  (135 shorter events, 38.3 us)
Async XLA Ops:
  10.9 1.6 slice-start
  12.5 4.9 copy-start.16
  22.2 1.6 slice-start.1
  30.9 1.6 slice-start.2
  39.5 1.6 slice-start.3
  48.2 1.6 slice-start.4
  57.3 1.6 slice-start.5
  66.0 1.6 slice-start.6
  74.6 1.6 slice-start.7
  81.3 2.2 copy-start
  83.5 1.6 copy-start.2
  83.5 2.3 copy-start.4
  85.1 1.7 copy-start.6
  85.8 1.7 copy-start.8
  86.8 1.7 copy-start.10
  87.5 1.7 copy-start.12
  88.6 1.7 copy-start.14
  307.5 9.0 %copy-start.17 = (f32[2,512]{1,0:T(2,128)S(1)}, f32[2,512]{1,0:T(2,128)}, u32[]{:S(2)}) copy-start(f32[2,512]{1,0:T(2,128)} %param.12) | copy-start | bytes 12292
  307.5 9.1 %copy-start.19 = (s32[512]{0:T(512)S(1)}, s32[512]{0:T(512)}, u32[]{:S(2)}) copy-start(s32[512]{0:T(512)} %param.13) | copy-start | bytes 6148
  307.5 18.7 %copy-start.21 = (s32[1,32]{1,0:T(1,128)S(1)}, s32[1,32]{1,0:T(1,128)}, u32[]{:S(2)}) copy-start(s32[1,32]{1,0:T(1,128)} %param.9) | copy-start | bytes 388
  307.5 18.8 %copy-start.20 = (bf16[1,512]{1,0:T(2,128)(2,1)S(1)}, bf16[1,512]{1,0:T(2,128)(2,1)}, u32[]{:S(2)}) copy-start(bf16[1,512]{1,0:T(2,128)(2,1)} %param.11) | copy-start | bytes 3076
  307.5 18.9 %copy-start.18 = (s32[1,8]{1,0:T(1,128)S(1)}, s32[1,8]{1,0:T(1,128)}, u32[]{:S(2)}) copy-start(s32[1,8]{1,0:T(1,128)} %param.10) | copy-start | bytes 100
  307.6 25.9 %all-to-all-start = ((bf16[32,2,8192]{2,1,0:T(2,128)(2,1)}), bf16[32,2,8192]{2,1,0:T(2,128)(2,1)S(1)}, u32[]{:S(2)}, u32[]{:S(2)}) async-start(bf16[32,2,8192]{2,1,0:T(2,128)(2,1)} %reshape.670), calls=%async_computation | async-start | bytes 2097152 | tf_op jit(solution)/shard_map/all_to_all | solution.py:148
  316.3 231.7 %all-reduce.5.cloned.1.call-start = ((), (), s32[]{:S(2)}) async-start(), calls=%async_computation.2 | async-start | bytes 4194304 | tf_op jit(solution)/shard_map/psum | solution.py:157
  571.9 24.0 %all-to-all-start.1 = ((bf16[32,2,8192]{2,1,0:T(2,128)(2,1)}), bf16[32,2,8192]{2,1,0:T(2,128)(2,1)}, u32[]{:S(2)}, u32[]{:S(2)}) async-start(bf16[32,2,8192]{2,1,0:T(2,128)(2,1)} %reshape.672), calls=%async_computation.1 | async-start | bytes 2097152 | tf_op jit(solution)/shard_map/all_to_all | solution.py:163
  600.6 3.1 copy-start.1
  603.7 1.6 copy-start.3
  603.7 2.2 copy-start.5
  605.3 1.7 copy-start.7
  605.9 1.7 copy-start.9
  607.0 1.7 copy-start.11
  607.6 1.7 copy-start.13
  608.7 1.7 copy-start.15
Sparse Core Ops, SparseCore 0:
  399.2 148.7 all-reduce.4
where the time goes:
time: 631 us; the launch traced here: 621 us
  other arithmetic  207 us (33%)
  local copies, waits for them, and re-layouts  197 us (31%)
  waiting for transfers between devices  172 us (27%)
  starting transfers between devices  15.9 us (3%)
  between operations  15.1 us (2%)
  matrix products  14.9 us (2%)
    unnamed x5, other arithmetic  188 us
    psum x1, waiting for transfers between devices, local(): totals = lax.psum(stacked, ('obs', 'td'))  149 us
    unnamed x51, local copies, waits for them, and re-layouts  45.1 us
    reshape x8, local copies, waits for them, and re-layouts, toeplitz(): repeated[..., :TILE * (4 * TILE - 1)]  40.1 us
    all_to_all x2, local copies, waits for them, and re-layouts, local(): lax.all_to_all(filtered, 'td', split_axis=2, concat_axis=1, tiled=True)  30.2 us
    convert_element_type x2, local copies, waits for them, and re-layouts, local(): filtered = forward_filter(timestreams, filter_taps).astype(jnp.bfloat16)  25.6 us
    another operation x16, local copies, waits for them, and re-layouts, toeplitz(): repeated = jnp.tile(padded, (1,) * len(leading) + (TILE,))  16.9 us
    all_to_all x1, waiting for transfers between devices, local(): lax.all_to_all(residual, 'td', split_axis=1, concat_axis=2, tiled=True)  16.4 us
  transfers between devices with their start and end apart: 3, of which 3 were waited for; matrix products, arithmetic and copies ran while one was open for 2% of the time, Pallas kernels for 0%

commit v1 on v0

v1 whole, which is shorter than its diff:
```python
import functools

import jax
import jax.numpy as jnp
from jax import lax
from jax.experimental import pallas as pl
from jax.experimental.pallas import tpu as pltpu
from jax.sharding import Mesh
from jax.sharding import PartitionSpec as P

TAPS = 129
BANDS = 8
TILE = 128
WAFERS = 8
POLY = 6
NINT = 16
OBS = 4
DET = 512
SAMP = 32768
TILES = 16

QUADS = 4
GROUPS = 8
ROWS = 16
BLOCKS = SAMP // TILE
SLABS = QUADS * GROUPS
SLAB_BLOCKS = BLOCKS // SLABS
BAND_BLOCKS = BLOCKS // BANDS
HALF = TILE // 2
GROUP_AXES = ("obs", "q")
SLAB_AXES = ("q", "g")
ALL_AXES = ("obs", "q", "g")

prior_weight = 1.0
VMEM_LIMIT = 48 * 1024 * 1024


def vmem():
    return pl.BlockSpec(memory_space=pltpu.VMEM)


def smem():
    return pl.BlockSpec(memory_space=pltpu.SMEM)


def call(kernel, out_shape, in_specs, out_specs, scratch=(), flops=0, bytes_accessed=0):
    return pl.pallas_call(
        kernel,
        out_shape=out_shape,
        in_specs=in_specs,
        out_specs=out_specs,
        scratch_shapes=list(scratch),
        compiler_params=pltpu.CompilerParams(vmem_limit_bytes=VMEM_LIMIT),
        cost_estimate=pl.CostEstimate(flops=flops, bytes_accessed=bytes_accessed, transcendentals=0),
    )


def lane_ids(shape):
    return lax.broadcasted_iota(jnp.int32, shape, len(shape) - 1)


def row_ids(shape):
    return lax.broadcasted_iota(jnp.int32, shape, len(shape) - 2)


def circulant(row):
    return pltpu.roll(jnp.broadcast_to(row, (TILE, TILE)), 0, 1, stride=1, stride_axis=0)


def forward_kernel(x_ref, taps_ref, y_ref, shifted, summed, first, last):
    taps = taps_ref[...].astype(jnp.float32)
    head = taps[:, :, :TILE].reshape(ROWS * BANDS, TILE).astype(jnp.bfloat16)
    reverse = (row_ids((TILE, TILE)) == ((TILE - lane_ids((TILE, TILE))) & (TILE - 1))).astype(
        jnp.float32
    )
    first[...] = jnp.dot(head, reverse.astype(jnp.bfloat16), preferred_element_type=jnp.float32)
    last[...] = jnp.broadcast_to(taps[:, :, TILE:], (ROWS, BANDS, TILE)).reshape(
        ROWS * BANDS, TILE
    )
    low = lane_ids((ROWS, TILE)) < HALF

    def shift_slab(slab, before):
        for inner in range(SLAB_BLOCKS):
            block = slab * SLAB_BLOCKS + inner
            start = pl.multiple_of(block * TILE, TILE)
            here = pltpu.roll(x_ref[0, :, pl.ds(start, TILE)].astype(jnp.float32), HALF, 1)
            shifted[pl.ds(pl.multiple_of(block * ROWS, ROWS), ROWS), :] = jnp.where(
                low, before, here
            )
            before = here
        return before

    before = lax.fori_loop(0, SLABS, shift_slab, jnp.zeros((ROWS, TILE), jnp.float32))
    shifted[BLOCKS * ROWS :, :] = jnp.where(low, before, 0.0)

    rows, lanes = row_ids((TILE, TILE)), lane_ids((TILE, TILE))
    in_first = lanes <= rows
    on_diag = lanes == rows

    def one_detector(det, carry):
        for band in range(BANDS):
            pair = det * BANDS + band
            turned = circulant(first[pl.ds(pair, 1), :])
            end = jnp.broadcast_to(last[pl.ds(pair, 1), :], (TILE, TILE))
            upper = jnp.where(in_first, turned, 0.0)
            lower = jnp.where(in_first, jnp.where(on_diag, end, 0.0), turned)
            kernel = jnp.concatenate([upper, lower], axis=0).astype(jnp.bfloat16)
            base = band * BAND_BLOCKS * ROWS + det
            one = shifted[pl.ds(base, BAND_BLOCKS, stride=ROWS), :]
            two = shifted[pl.ds(base + ROWS, BAND_BLOCKS, stride=ROWS), :]
            window = jnp.concatenate([one, two], axis=1).astype(jnp.bfloat16)
            summed[pl.ds(base, BAND_BLOCKS, stride=ROWS), :] = jnp.dot(
                window, kernel, preferred_element_type=jnp.float32
            )
        return carry

    lax.fori_loop(0, ROWS, one_detector, 0)

    def write_slab(slab, carry):
        for inner in range(SLAB_BLOCKS):
            block = slab * SLAB_BLOCKS + inner
            part = summed[pl.ds(pl.multiple_of(block * ROWS, ROWS), ROWS), :]
            y_ref[slab, :, inner * TILE : (inner + 1) * TILE] = part.astype(jnp.bfloat16)
        return carry

    lax.fori_loop(0, SLABS, write_slab, 0)


def clean_kernel(data_ref, basis_ref, basis_t_ref, inverse_ref, out_ref):
    data = data_ref[...].reshape(DET, SLAB_BLOCKS * TILE)
    raw = jnp.dot(basis_ref[...], data, preferred_element_type=jnp.float32)
    coef = jnp.dot(
        inverse_ref[...],
        raw,
        precision=lax.Precision.HIGHEST,
        preferred_element_type=jnp.float32,
    )
    high = coef.astype(jnp.bfloat16)
    rest = (coef - high.astype(jnp.float32)).astype(jnp.bfloat16)
    both = jnp.concatenate([high, rest], axis=0)
    fitted = jnp.dot(basis_t_ref[...], both, preferred_element_type=jnp.float32)
    out = (data.astype(jnp.float32) - fitted).astype(jnp.bfloat16)
    out_ref[...] = out.reshape(out_ref.shape)


def write_flags(flags, bounds_ref, obs):
    for part in range(BANDS):
        sample = (
            (row_ids((BAND_BLOCKS, TILE)) + part * BAND_BLOCKS) * TILE
            + lane_ids((BAND_BLOCKS, TILE))
        )
        passed = jnp.zeros((BAND_BLOCKS, TILE), jnp.int32)
        for bound in range(2 * NINT):
            passed = passed + (bounds_ref[obs, bound] <= sample).astype(jnp.int32)
        flags[part * BAND_BLOCKS : (part + 1) * BAND_BLOCKS, :] = (passed & 1).astype(jnp.float32)


def hits_kernel(bounds_ref, tiles_ref, weight_ref, out_ref, flags):
    sums = []
    for obs in range(OBS):
        write_flags(flags, bounds_ref, obs)
        chosen = row_ids((TILES, BLOCKS)) == tiles_ref[obs : obs + 1, :]
        sums.append(
            jnp.dot(
                chosen.astype(jnp.bfloat16),
                flags[...].astype(jnp.bfloat16),
                preferred_element_type=jnp.float32,
            )
        )
    for tile in range(TILES):
        total = jnp.zeros((ROWS, TILE), jnp.float32)
        for obs in range(OBS):
            total = total + weight_ref[obs] * sums[obs][tile : tile + 1, :]
        out_ref[tile] = total


def bin_kernel(bounds_ref, tiles_ref, data_ref, weight_ref, out_ref, flags):
    write_flags(flags, bounds_ref, 0)
    out_ref[...] = jnp.zeros_like(out_ref)

    def add_slab(slab, carry):
        for inner in range(SLAB_BLOCKS):
            block = slab * SLAB_BLOCKS + inner
            part = data_ref[slab, :, inner * TILE : (inner + 1) * TILE].astype(jnp.float32)
            tile = tiles_ref[block]
            out_ref[tile] = out_ref[tile] + part * flags[pl.ds(block, 1), :]
        return carry

    lax.fori_loop(0, SLABS, add_slab, 0)
    for tile in range(TILES):
        out_ref[tile] = out_ref[tile] * weight_ref[...]


def adjoint_kernel(
    bounds_ref, tiles_ref, data_ref, sky_ref, taps_ref, out_ref, flags, resid, same, after, first, last
):
    write_flags(flags, bounds_ref, 0)
    taps = taps_ref[...].astype(jnp.float32)
    first[...] = taps[:, :, :TILE].reshape(ROWS * BANDS, TILE)
    last[...] = jnp.broadcast_to(taps[:, :, TILE:], (ROWS, BANDS, TILE)).reshape(
        ROWS * BANDS, TILE
    )

    def residual_slab(slab, carry):
        for inner in range(SLAB_BLOCKS):
            block = slab * SLAB_BLOCKS + inner
            part = data_ref[slab, :, inner * TILE : (inner + 1) * TILE].astype(jnp.float32)
            sky = sky_ref[tiles_ref[block]].astype(jnp.bfloat16).astype(jnp.float32)
            value = flags[pl.ds(block, 1), :] * (part - sky)
            resid[pl.ds(pl.multiple_of(block * ROWS, ROWS), ROWS), :] = value
        return carry

    lax.fori_loop(0, SLABS, residual_slab, 0)

    rows, lanes = row_ids((TILE, TILE)), lane_ids((TILE, TILE))
    in_first = lanes >= rows
    on_diag = lanes == rows
    after[:ROWS, :] = jnp.zeros((ROWS, TILE), jnp.float32)

    def one_detector(det, carry):
        for band in range(BANDS):
            pair = det * BANDS + band
            turned = circulant(first[pl.ds(pair, 1), :])
            end = jnp.broadcast_to(last[pl.ds(pair, 1), :], (TILE, TILE))
            upper = jnp.where(in_first, turned, 0.0)
            lower = jnp.where(in_first, jnp.where(on_diag, end, 0.0), turned)
            kernel = jnp.concatenate([upper, lower], axis=1).astype(jnp.bfloat16)
            base = band * BAND_BLOCKS * ROWS + det
            part = resid[pl.ds(base, BAND_BLOCKS, stride=ROWS), :].astype(jnp.bfloat16)
            spread = jnp.dot(part, kernel, preferred_element_type=jnp.float32)
            same[pl.ds(base, BAND_BLOCKS, stride=ROWS), :] = spread[:, :TILE]
            after[pl.ds(base + ROWS, BAND_BLOCKS, stride=ROWS), :] = spread[:, TILE:]
        return carry

    lax.fori_loop(0, ROWS, one_detector, 0)
    same[BLOCKS * ROWS :, :] = jnp.zeros((ROWS, TILE), jnp.float32)
    low = lane_ids((ROWS, TILE)) < HALF

    def joined(block):
        start = pl.multiple_of(block * ROWS, ROWS)
        return pltpu.roll(same[pl.ds(start, ROWS), :] + after[pl.ds(start, ROWS), :], HALF, 1)

    def write_slab(slab, here):
        for inner in range(SLAB_BLOCKS):
            block = slab * SLAB_BLOCKS + inner
            following = joined(block + 1)
            out_ref[0, :, pl.ds(pl.multiple_of(block * TILE, TILE), TILE)] = jnp.where(
                low, here, following
            )
            here = following
        return here

    lax.fori_loop(0, SLABS, write_slab, joined(0))


def make_basis(positions, wafer_group):
    x_pos = positions[0]
    y_pos = positions[1]
    monomials = jnp.stack(
        [jnp.ones_like(x_pos), x_pos, y_pos, x_pos * x_pos, x_pos * y_pos, y_pos * y_pos]
    )
    member = (wafer_group[None, :] == jnp.arange(WAFERS, dtype=jnp.int32)[:, None]).astype(
        jnp.float32
    )
    basis_b = (member[:, None, :] * monomials[None]).reshape(WAFERS * POLY, -1).astype(jnp.bfloat16)
    basis_f = basis_b.astype(jnp.float32)
    gram_matrix = jnp.dot(basis_f, basis_f.T, precision=lax.Precision.HIGHEST)
    factor = jnp.linalg.cholesky(gram_matrix)
    lower_inv = lax.linalg.triangular_solve(
        factor, jnp.eye(WAFERS * POLY, dtype=jnp.float32), left_side=True, lower=True
    )
    inverse = jnp.dot(lower_inv.T, lower_inv, precision=lax.Precision.HIGHEST)
    return (basis_b, inverse)


def exchange(value, axis):
    size = lax.axis_size(axis)
    return [
        lax.ppermute(value, axis, [(src, (src + step) % size) for src in range(size)])
        for step in range(1, size)
    ]


def local(timestreams, filter_taps, scan_bounds, tile_index, det_weights, positions, wafer_group):
    f32 = jnp.float32
    shape = jax.ShapeDtypeStruct
    obs = lax.axis_index("obs")
    group = lax.axis_index("g")
    slab = lax.axis_index(SLAB_AXES)
    taps = filter_taps.reshape(ROWS, BANDS, TAPS)
    own_weights = lax.dynamic_slice_in_dim(det_weights[0], slab * ROWS, ROWS).astype(f32)
    own_bound = lax.dynamic_slice_in_dim(scan_bounds[0], slab, 1).astype(f32)
    pieces = [tile_index[0].astype(f32), own_bound, own_weights]
    used = SLAB_BLOCKS + 1 + ROWS
    meta = jnp.concatenate(pieces + [jnp.zeros((TILE - used,), f32)]).reshape(1, TILE)
    meta = lax.all_gather(meta, ALL_AXES, axis=0, tiled=True).reshape(OBS, SLABS, TILE)
    all_tiles = meta[:, :, :SLAB_BLOCKS].reshape(OBS, BLOCKS).astype(jnp.int32)
    all_bounds = meta[:, :, SLAB_BLOCKS].astype(jnp.int32)
    all_weights = meta[:, :, SLAB_BLOCKS + 1 : used].reshape(OBS, QUADS, GROUPS, ROWS)
    row_weights = jnp.sum(lax.dynamic_index_in_dim(all_weights, group, 2, keepdims=False), axis=1)
    own_tiles = lax.dynamic_index_in_dim(all_tiles, obs, 0, keepdims=False)

    filtered = call(
        forward_kernel,
        shape((SLABS, ROWS, SLAB_BLOCKS * TILE), jnp.bfloat16),
        [vmem(), vmem()],
        vmem(),
        [
            pltpu.VMEM(((BLOCKS + 1) * ROWS, TILE), f32),
            pltpu.VMEM((BLOCKS * ROWS, TILE), f32),
            pltpu.VMEM((ROWS * BANDS, TILE), f32),
            pltpu.VMEM((ROWS * BANDS, TILE), f32),
        ],
    )(timestreams, taps)
    basis, inverse = make_basis(positions, wafer_group)
    gathered = lax.all_to_all(filtered, SLAB_AXES, split_axis=0, concat_axis=0, tiled=True)
    cleaned = call(
        clean_kernel,
        shape((SLABS, ROWS, SLAB_BLOCKS * TILE), jnp.bfloat16),
        [vmem()] * 4,
        vmem(),
    )(gathered, basis, jnp.concatenate([basis, basis], axis=0).T, inverse)
    returned = lax.all_to_all(cleaned, SLAB_AXES, split_axis=0, concat_axis=0, tiled=True)

    hits = call(
        hits_kernel,
        shape((TILES, ROWS, TILE), f32),
        [smem(), vmem(), vmem()],
        vmem(),
        [pltpu.VMEM((BLOCKS, TILE), f32)],
    )(all_bounds, all_tiles, jnp.broadcast_to(row_weights[:, :, None], (OBS, ROWS, TILE)))
    part = call(
        bin_kernel,
        shape((TILES, ROWS, TILE), f32),
        [smem(), smem(), vmem(), vmem()],
        vmem(),
        [pltpu.VMEM((BLOCKS, TILE), f32)],
    )(scan_bounds, own_tiles, returned, jnp.broadcast_to(own_weights[:, None], (ROWS, TILE)))
    part = sum(exchange(part, "obs"), part)
    part = sum(exchange(part, "q"), part)
    sky = part / (hits + prior_weight)
    row = lax.axis_index(GROUP_AXES)
    sky_row = lax.dynamic_slice_in_dim(sky, row, 1, 1)
    moves = [
        ((o * QUADS + q) * GROUPS + g, g * ROWS + o * QUADS + q)
        for o in range(OBS)
        for q in range(QUADS)
        for g in range(GROUPS)
    ]
    sky_own = lax.ppermute(sky_row, ALL_AXES, moves)
    out = call(
        adjoint_kernel,
        shape((1, ROWS, SAMP), f32),
        [smem(), smem(), vmem(), vmem(), vmem()],
        vmem(),
        [
            pltpu.VMEM((BLOCKS, TILE), f32),
            pltpu.VMEM((BLOCKS * ROWS, TILE), f32),
            pltpu.VMEM(((BLOCKS + 1) * ROWS, TILE), f32),
            pltpu.VMEM(((BLOCKS + 1) * ROWS, TILE), f32),
            pltpu.VMEM((ROWS * BANDS, TILE), f32),
            pltpu.VMEM((ROWS * BANDS, TILE), f32),
        ],
    )(scan_bounds, own_tiles, returned, sky, taps)
    return (out, sky_own)


def solution(mesh):
    split = Mesh(mesh.devices.reshape(OBS, QUADS, GROUPS), ALL_AXES)
    placed = (
        P("obs", SLAB_AXES, None),
        P("obs", SLAB_AXES, None, None),
        P("obs", None),
        P("obs", SLAB_AXES),
        P("obs", None),
        P(),
        P(),
    )
    return jax.shard_map(
        local,
        mesh=split,
        in_specs=placed,
        out_specs=(P("obs", SLAB_AXES, None), P(None, ALL_AXES, None)),
        check_vma=False,
    )
```

time: 631 us -> 123 us (0.19); the launches traced: 621 us -> 121 us
  other arithmetic: 207 us -> 11.8 us
  local copies, waits for them, and re-layouts: 197 us -> 3.37 us
  waiting for transfers between devices: 172 us -> 13.2 us
  blocking collectives: 0 us -> 37.8 us
  Pallas kernels: 0 us -> 26.7 us
  matrix products: 14.9 us -> 0.55 us
  between operations: 15.1 us -> 0.91 us
  starting transfers between devices: 15.9 us -> 26.5 us
    unnamed x5 -> x1, other arithmetic: 188 us -> 0.72 us
    psum x1 -> x0, waiting for transfers between devices: 149 us -> none  [local(): totals = lax.psum(stacked, ('obs', 'td'))]
    reshape x11 -> x1, local copies, waits for them, and re-layouts: 43.7 us -> 0.08 us  [local(): meta[:, :, SLAB_BLOCKS + 1:used].reshape(OBS, QUADS, GROUPS, ROWS)]
    unnamed x51 -> x16, local copies, waits for them, and re-layouts: 45.1 us -> 2.77 us
    all_gather x0 -> x1, blocking collectives: none -> 37.8 us  [local(): lax.all_gather(meta, ALL_AXES, axis=0, tiled=True).reshape(OBS, SLABS, TILE)]
    convert_element_type x5 -> x1, local copies, waits for them, and re-layouts: 36 us -> 0.1 us  [local(): all_tiles = meta[:, :, :SLAB_BLOCKS].reshape(OBS, BLOCKS).astype(jnp.int32)]
    all_to_all x3 -> x0, local copies, waits for them, and re-layouts: 31.8 us -> none  [the longest x2 30.2 us: local(): lax.all_to_all(filtered, 'td', split_axis=2, concat_axis=1, tiled=True)]
    pallas_call x0 -> x5, Pallas kernels: none -> 26.7 us  [the longest x1 11.4 us: local(): call(adjoint_kernel, shape((1, ROWS, SAMP), f32), [smem(), smem(), vmem()...]
  transfers between devices with their start and end apart: 3 -> 9, of which waited for: 3 -> 6; matrix products, arithmetic and copies ran while one was open for 2% -> 11% of each run, Pallas kernels for 0% -> 11%
where the time goes in v1:
time: 123 us; the launch traced here: 121 us
  blocking collectives  37.8 us (31%)
  Pallas kernels  26.7 us (22%)
  starting transfers between devices  26.5 us (22%)
  waiting for transfers between devices  13.2 us (11%)
  other arithmetic  11.8 us (10%)
  local copies, waits for them, and re-layouts  3.37 us (3%)
    all_gather x1, blocking collectives, local(): lax.all_gather(meta, ALL_AXES, axis=0, tiled=True).reshape(OBS, SLABS, TILE)  37.8 us
    pallas_call x1, Pallas kernels, local(): call(adjoint_kernel, shape((1, ROWS, SAMP), f32), [smem(), smem(), vmem()...  11.4 us
    pallas_call x1, Pallas kernels, local(): call(forward_kernel, shape((SLABS, ROWS, SLAB_BLOCKS * TILE), jnp.bfloat1...  9.29 us
    all_to_all x1, starting transfers between devices, local(): lax.all_to_all(filtered, SLAB_AXES, split_axis=0, concat_axis=0, tiled=True)  8.58 us
    ppermute x6, starting transfers between devices, exchange(): lax.ppermute(value, axis, [(src, (src + step) % size) for src in range(si...  8.06 us
    all_to_all x1, waiting for transfers between devices, local(): lax.all_to_all(filtered, SLAB_AXES, split_axis=0, concat_axis=0, tiled=True)  6.69 us
    ppermute x6, waiting for transfers between devices, exchange(): lax.ppermute(value, axis, [(src, (src + step) % size) for src in range(si...  6.5 us
    ppermute x1, starting transfers between devices, local(): sky_own = lax.ppermute(sky_row, ALL_AXES, moves)  5.86 us
  transfers between devices with their start and end apart: 9, of which 6 were waited for; matrix products, arithmetic and copies ran while one was open for 11% of the time, Pallas kernels for 11%

profile of v1, /device:TPU:1, one launch (start us, length us, event | category | flops | bytes accessed | tf_op | source)
XLA Modules:
  0.0 120.8 jit_solution(4522078309505130852)
XLA Ops:
  0.6 1.2 %copy-done = bf16[1,16,32768]{2,1,0:T(8,128)(2,1)S(1)} copy-done((bf16[1,16,32768]{2,1,0:T(8,128)(2,1)S(1)}, bf16[1,16,32768]{2,1,0:T(8,128)(2,1)}, u32[]{:S(2)}) %copy-start) | copy-done | bytes 1048600
  1.9 0.8 copy-done.1
  2.7 9.3 %shard_map.86 = bf16[32,16,1024]{2,1,0:T(8,128)(2,1)} custom-call(bf16[1,16,32768]{2,1,0:T(8,128)(2,1)S(1)} %copy-done, bf16[16,8,129]{2,1,0:T(8,128)(2,1)S(1)} %bitcast.31), custom_call_target="tpu_custom_call" | custom-call | tf_op jit(solution)/shard_map/pallas_call | solution.py:303
  12.0 8.6 %all-to-all-start = ((bf16[32,16,1024]{2,1,0:T(8,128)(2,1)}), bf16[32,16,1024]{2,1,0:T(8,128)(2,1)S(1)}, u32[]{:S(2)}, u32[]{:S(2)}) async-start(bf16[32,16,1024]{2,1,0:T(8,128)(2,1)} %shard_map.86), calls=%async_computation | async-start | bytes 2097152 | tf_op jit(solution)/shard_map/all_to_all | solution.py:316
  20.7 0.1 fusion.8
  20.8 0.1 copy.17
  21.0 0.1 copy.19
  21.1 4.4 %cholesky.17 = f32[48,48]{1,0:T(8,128)S(1)} custom-call(f32[48,48]{1,0:T(8,128)S(1)} %fusion.3), custom_call_target="Cholesky" | custom-call | tf_op jit(solution)/shard_map/jit(cholesky)/cholesky | solution.py:268
  25.5 0.6 compare_reduce_fusion
  26.1 0.7 fusion
  26.8 3.7 %custom-call.6 = f32[1,48,48]{1,2,0:T(8,128)S(1)} custom-call(f32[1,48,48]{2,1,0:T(8,128)S(1)} %fusion), custom_call_target="InvertDiagBlocksLowerTriangular" | custom-call | tf_op jit(solution)/shard_map/triangular_solve | solution.py:269
  30.5 0.1 maximum_bitcast_fusion.basis_t_ref
  30.6 0.2 fusion.1
  30.8 0.2 fusion.9.inverse_ref
  31.0 0.0 copy-start.3
  31.1 0.0 copy-start.6
  31.1 6.7 %all-to-all-done.data_ref = bf16[32,16,1024]{2,1,0:T(8,128)(2,1)S(1)} async-done(((bf16[32,16,1024]{2,1,0:T(8,128)(2,1)}), bf16[32,16,1024]{2,1,0:T(8,128)(2,1)S(1)}, u32[]{:S(2)}, u32[]{:S(2)}) %all-to-all-start) | async-done | bytes 1048608 | tf_op jit(solution)/shard_map/all_to_all | solution.py:316
  37.8 1.8 %shard_map.87 = bf16[32,16,1024]{2,1,0:T(8,128)(2,1)} custom-call(bf16[32,16,1024]{2,1,0:T(8,128)(2,1)S(1)} %all-to-all-done.data_ref, bf16[48,512]{1,0:T(8,128)(2,1)S(1)} %convert_element_type.56.basis_ref, bf16[512,96]{1,0:T(8,128)(2,1)S(1)} %maximum_bitcast_fusion.basis_t_ref, f32[48,48]{1,0:T(8,128)S(1)} %fusion.9.inverse_ref), custom_call_target="tpu_custom_call" | custom-call | tf_op jit(solution)/shard_map/pallas_call | solution.py:317
  39.5 4.0 %all-to-all-start.1 = ((bf16[32,16,1024]{2,1,0:T(8,128)(2,1)}), bf16[32,16,1024]{2,1,0:T(8,128)(2,1)S(1)}, u32[]{:S(2)}, u32[]{:S(2)}) async-start(bf16[32,16,1024]{2,1,0:T(8,128)(2,1)} %shard_map.87), calls=%async_computation.1 | async-start | bytes 2097152 | tf_op jit(solution)/shard_map/all_to_all | solution.py:323
  43.5 0.0 copy-start.2
  43.6 0.6 fusion.7
  44.2 0.7 fusion.6
  44.9 0.7 maximum_bitcast_fusion.1
  45.6 37.8 %all-gather.1 = f32[128,1,128]{2,1,0:T(1,128)S(1)} all-gather(f32[1,1,128]{2,1,0:T(1,128)S(1)} %maximum_bitcast_fusion.1), channel_id=2, replica_groups=mesh['obs'=4,'q'=4,'g'=8] {'obs','q','g'}, dimensions={0}, use_global_device_ids=true | all-gather | bytes 66048 | tf_op jit(solution)/shard_map/all_gather | solution.py:296
  83.4 0.1 convert_element_type.53.tiles_ref
  83.5 0.0 all-to-all-done.1.data_ref
  83.5 0.1 broadcast_in_dim.9.weight_ref
  83.6 1.8 %shard_map.88 = f32[16,16,128]{2,1,0:T(8,128)S(1)} custom-call(s32[1,32]{1,0:T(1,128)S(1)} %copy-done.3, s32[256]{0:T(256)S(1)} %bitcast.33, bf16[32,16,1024]{2,1,0:T(8,128)(2,1)S(1)} %all-to-all-done.1.data_ref, f32[16,128]{1,0:T(8,128)S(1)} %broadcast_in_dim.9.weight_ref), custom_call_target="tpu_custom_call" | custom-call | tf_op jit(solution)/shard_map/pallas_call | solution.py:332
  85.4 0.6 collective-permute-start
  86.0 1.8 %collective-permute-start.1 = (f32[16,16,128]{2,1,0:T(8,128)S(1)}, f32[16,16,128]{2,1,0:T(8,128)S(1)}, u32[]{:S(2)}, u32[]{:S(2)}) collective-permute-start(f32[16,16,128]{2,1,0:T(8,128)S(1)} %shard_map.88), channel_id=1, source_target_pairs={{0,64},{32,96},{64,0},{96,32},{1,65},{33,97},{65,1},{97,33},{2,66}... | collective-permute-start | bytes 393224 | tf_op jit(solution)/shard_map/ppermute | solution.py:279
  87.7 2.0 %collective-permute-start.2 = (f32[16,16,128]{2,1,0:T(8,128)S(1)}, f32[16,16,128]{2,1,0:T(8,128)S(1)}, u32[]{:S(2)}, u32[]{:S(2)}) collective-permute-start(f32[16,16,128]{2,1,0:T(8,128)S(1)} %shard_map.88), channel_id=1, source_target_pairs={{0,96},{32,0},{64,32},{96,64},{1,97},{33,1},{65,33},{97,65},{2,98}... | collective-permute-start | bytes 393224 | tf_op jit(solution)/shard_map/ppermute | solution.py:279
  89.7 0.1 slice_convert_fusion
  89.8 0.1 copy.22
  89.9 2.2 %collective-permute-done = f32[16,16,128]{2,1,0:T(8,128)S(1)} collective-permute-done((f32[16,16,128]{2,1,0:T(8,128)S(1)}, f32[16,16,128]{2,1,0:T(8,128)S(1)}, u32[]{:S(2)}, u32[]{:S(2)}) %collective-permute-start) | collective-permute-done | bytes 131104 | tf_op jit(solution)/shard_map/ppermute | solution.py:279
  92.1 1.9 %collective-permute-done.1 = f32[16,16,128]{2,1,0:T(8,128)S(1)} collective-permute-done((f32[16,16,128]{2,1,0:T(8,128)S(1)}, f32[16,16,128]{2,1,0:T(8,128)S(1)}, u32[]{:S(2)}, u32[]{:S(2)}) %collective-permute-start.1) | collective-permute-done | bytes 131104 | tf_op jit(solution)/shard_map/ppermute | solution.py:279
  94.0 0.7 collective-permute-done.2
  94.7 1.2 %collective-permute-start.3 = (f32[16,16,128]{2,1,0:T(8,128)S(1)}, f32[16,16,128]{2,1,0:T(8,128)S(1)}, u32[]{:S(2)}, u32[]{:S(2)}) collective-permute-start(f32[16,16,128]{2,1,0:T(8,128)S(1)} %add_add_fusion), channel_id=1, source_target_pairs={{0,8},{8,16},{16,24},{24,0},{1,9},{9,17},{17,25},{25,1},{2,10},{10... | collective-permute-start | bytes 393224 | tf_op jit(solution)/shard_map/ppermute | solution.py:279
  96.0 1.3 %collective-permute-start.4 = (f32[16,16,128]{2,1,0:T(8,128)S(1)}, f32[16,16,128]{2,1,0:T(8,128)S(1)}, u32[]{:S(2)}, u32[]{:S(2)}) collective-permute-start(f32[16,16,128]{2,1,0:T(8,128)S(1)} %add_add_fusion), channel_id=1, source_target_pairs={{0,16},{8,24},{16,0},{24,8},{1,17},{9,25},{17,1},{25,9},{2,18},{10... | collective-permute-start | bytes 393224 | tf_op jit(solution)/shard_map/ppermute | solution.py:279
  97.2 1.2 %collective-permute-start.5 = (f32[16,16,128]{2,1,0:T(8,128)S(1)}, f32[16,16,128]{2,1,0:T(8,128)S(1)}, u32[]{:S(2)}, u32[]{:S(2)}) collective-permute-start(f32[16,16,128]{2,1,0:T(8,128)S(1)} %add_add_fusion), channel_id=1, source_target_pairs={{0,24},{8,0},{16,8},{24,16},{1,25},{9,1},{17,9},{25,17},{2,26},{10... | collective-permute-start | bytes 393224 | tf_op jit(solution)/shard_map/ppermute | solution.py:279
  98.5 0.1 slice_bitcast_fusion
  98.6 0.1 broadcast_in_dim.10.weight_ref
  98.6 2.4 %shard_map.89 = f32[16,16,128]{2,1,0:T(8,128)S(1)} custom-call(s32[4,32]{1,0:T(4,128)S(1)} %bitcast.35, s32[4,256]{1,0:T(4,128)S(1)} %convert_element_type.53.tiles_ref, f32[4,16,128]{2,1,0:T(8,128)S(1)} %broadcast_in_dim.10.weight_ref), custom_call_target="tpu_custom_call" | custom-call | tf_op jit(solution)/shard_map/pallas_call | solution.py:325
  101.1 1.6 %collective-permute-done.4 = f32[16,16,128]{2,1,0:T(8,128)S(1)} collective-permute-done((f32[16,16,128]{2,1,0:T(8,128)S(1)}, f32[16,16,128]{2,1,0:T(8,128)S(1)}, u32[]{:S(2)}, u32[]{:S(2)}) %collective-permute-start.4) | collective-permute-done | bytes 131104 | tf_op jit(solution)/shard_map/ppermute | solution.py:279
  102.7 0.2 collective-permute-done.5
  102.9 5.9 %collective-permute-start.6 = (f32[16,1,128]{2,1,0:T(1,128)S(1)}, f32[16,1,128]{2,1,0:T(1,128)S(1)}, u32[]{:S(2)}, u32[]{:S(2)}) collective-permute-start(f32[16,1,128]{2,1,0:T(1,128)S(1)} %constant_dynamic-slice_fusion), channel_id=1, source_target_pairs={{0,0},{1,16},{2,32},{3,48},{4,64},{5,80},{6,96},{7,112},{8,1},{9,1... | collective-permute-start | bytes 24584 | tf_op jit(solution)/shard_map/ppermute | solution.py:350
  108.8 11.4 %shard_map.90 = f32[1,16,32768]{2,1,0:T(8,128)} custom-call(s32[1,32]{1,0:T(1,128)S(1)} %copy-done.3, s32[256]{0:T(256)S(1)} %bitcast.34, bf16[32,16,1024]{2,1,0:T(8,128)(2,1)S(1)} %all-to-all-done.1.data_ref, f32[16,16,128]{2,1,0:T(8,128)S(1)} %add_divide_fusion.sky_ref, bf16[16,8,129]{2,1,0:T(8,128)(2,1)S(1)} %bitcast.32), custom_call_target="tpu_custom_call" | custom-call | tf_op jit(solution)/shard_map/pallas_call | solution.py:351
  120.2 0.0 collective-permute-done.6
  120.2 0.6 copy.24
  (26 shorter events, 0.3 us)
Async XLA Ops:
  0.6 1.2 %copy-start = (bf16[1,16,32768]{2,1,0:T(8,128)(2,1)S(1)}, bf16[1,16,32768]{2,1,0:T(8,128)(2,1)}, u32[]{:S(2)}) copy-start(bf16[1,16,32768]{2,1,0:T(8,128)(2,1)} %x_ref.1) | copy-start | bytes 3145732
  1.9 0.8 copy-start.1
  2.7 17.9 %copy-start.4 = (f32[2,512]{1,0:T(2,128)S(1)}, f32[2,512]{1,0:T(2,128)}, u32[]{:S(2)}) copy-start(f32[2,512]{1,0:T(2,128)} %param.12) | copy-start | bytes 12292
  2.7 17.9 %copy-start.5 = (s32[512]{0:T(512)S(1)}, s32[512]{0:T(512)}, u32[]{:S(2)}) copy-start(s32[512]{0:T(512)} %param.13) | copy-start | bytes 6148
  12.0 25.8 %all-to-all-start = ((bf16[32,16,1024]{2,1,0:T(8,128)(2,1)}), bf16[32,16,1024]{2,1,0:T(8,128)(2,1)S(1)}, u32[]{:S(2)}, u32[]{:S(2)}) async-start(bf16[32,16,1024]{2,1,0:T(8,128)(2,1)} %shard_map.86), calls=%async_computation | async-start | bytes 2097152 | tf_op jit(solution)/shard_map/all_to_all | solution.py:316
  31.0 12.5 %copy-start.3 = (s32[1,32]{1,0:T(1,128)S(1)}, s32[1,32]{1,0:T(1,128)}, u32[]{:S(2)}) copy-start(s32[1,32]{1,0:T(1,128)} %bounds_ref.3) | copy-start | bytes 388
  31.1 13.8 %copy-start.6 = (s32[1,8]{1,0:T(1,128)S(1)}, s32[1,8]{1,0:T(1,128)}, u32[]{:S(2)}) copy-start(s32[1,8]{1,0:T(1,128)} %param.10) | copy-start | bytes 100
  39.5 44.0 %all-to-all-start.1 = ((bf16[32,16,1024]{2,1,0:T(8,128)(2,1)}), bf16[32,16,1024]{2,1,0:T(8,128)(2,1)S(1)}, u32[]{:S(2)}, u32[]{:S(2)}) async-start(bf16[32,16,1024]{2,1,0:T(8,128)(2,1)} %shard_map.87), calls=%async_computation.1 | async-start | bytes 2097152 | tf_op jit(solution)/shard_map/all_to_all | solution.py:323
  43.5 65.2 %copy-start.2 = (bf16[1,16,8,129]{3,2,1,0:T(8,128)(2,1)S(1)}, bf16[1,16,8,129]{3,2,1,0:T(8,128)(2,1)}, u32[]{:S(2)}) copy-start(bf16[1,16,8,129]{3,2,1,0:T(8,128)(2,1)} %param.8) | copy-start | bytes 99076
  85.4 6.7 %collective-permute-start = (f32[16,16,128]{2,1,0:T(8,128)S(1)}, f32[16,16,128]{2,1,0:T(8,128)S(1)}, u32[]{:S(2)}, u32[]{:S(2)}) collective-permute-start(f32[16,16,128]{2,1,0:T(8,128)S(1)} %shard_map.88), channel_id=1, source_target_pairs={{0,32},{32,64},{64,96},{96,0},{1,33},{33,65},{65,97},{97,1},{2,34}... | collective-permute-start | bytes 393224 | tf_op jit(solution)/shard_map/ppermute | solution.py:279
  86.0 8.0 %collective-permute-start.1 = (f32[16,16,128]{2,1,0:T(8,128)S(1)}, f32[16,16,128]{2,1,0:T(8,128)S(1)}, u32[]{:S(2)}, u32[]{:S(2)}) collective-permute-start(f32[16,16,128]{2,1,0:T(8,128)S(1)} %shard_map.88), channel_id=1, source_target_pairs={{0,64},{32,96},{64,0},{96,32},{1,65},{33,97},{65,1},{97,33},{2,66}... | collective-permute-start | bytes 393224 | tf_op jit(solution)/shard_map/ppermute | solution.py:279
  87.7 6.9 %collective-permute-start.2 = (f32[16,16,128]{2,1,0:T(8,128)S(1)}, f32[16,16,128]{2,1,0:T(8,128)S(1)}, u32[]{:S(2)}, u32[]{:S(2)}) collective-permute-start(f32[16,16,128]{2,1,0:T(8,128)S(1)} %shard_map.88), channel_id=1, source_target_pairs={{0,96},{32,0},{64,32},{96,64},{1,97},{33,1},{65,33},{97,65},{2,98}... | collective-permute-start | bytes 393224 | tf_op jit(solution)/shard_map/ppermute | solution.py:279
  94.7 6.4 %collective-permute-start.3 = (f32[16,16,128]{2,1,0:T(8,128)S(1)}, f32[16,16,128]{2,1,0:T(8,128)S(1)}, u32[]{:S(2)}, u32[]{:S(2)}) collective-permute-start(f32[16,16,128]{2,1,0:T(8,128)S(1)} %add_add_fusion), channel_id=1, source_target_pairs={{0,8},{8,16},{16,24},{24,0},{1,9},{9,17},{17,25},{25,1},{2,10},{10... | collective-permute-start | bytes 393224 | tf_op jit(solution)/shard_map/ppermute | solution.py:279
  96.0 6.7 %collective-permute-start.4 = (f32[16,16,128]{2,1,0:T(8,128)S(1)}, f32[16,16,128]{2,1,0:T(8,128)S(1)}, u32[]{:S(2)}, u32[]{:S(2)}) collective-permute-start(f32[16,16,128]{2,1,0:T(8,128)S(1)} %add_add_fusion), channel_id=1, source_target_pairs={{0,16},{8,24},{16,0},{24,8},{1,17},{9,25},{17,1},{25,9},{2,18},{10... | collective-permute-start | bytes 393224 | tf_op jit(solution)/shard_map/ppermute | solution.py:279
  97.2 5.6 %collective-permute-start.5 = (f32[16,16,128]{2,1,0:T(8,128)S(1)}, f32[16,16,128]{2,1,0:T(8,128)S(1)}, u32[]{:S(2)}, u32[]{:S(2)}) collective-permute-start(f32[16,16,128]{2,1,0:T(8,128)S(1)} %add_add_fusion), channel_id=1, source_target_pairs={{0,24},{8,0},{16,8},{24,16},{1,25},{9,1},{17,9},{25,17},{2,26},{10... | collective-permute-start | bytes 393224 | tf_op jit(solution)/shard_map/ppermute | solution.py:279
  102.9 17.3 %collective-permute-start.6 = (f32[16,1,128]{2,1,0:T(1,128)S(1)}, f32[16,1,128]{2,1,0:T(1,128)S(1)}, u32[]{:S(2)}, u32[]{:S(2)}) collective-permute-start(f32[16,1,128]{2,1,0:T(1,128)S(1)} %constant_dynamic-slice_fusion), channel_id=1, source_target_pairs={{0,0},{1,16},{2,32},{3,48},{4,64},{5,80},{6,96},{7,112},{8,1},{9,1... | collective-permute-start | bytes 24584 | tf_op jit(solution)/shard_map/ppermute | solution.py:350

commit v2 on v1

v2 whole, which is shorter than its diff:
```python
import functools

import jax
import jax.numpy as jnp
from jax import lax
from jax.experimental import pallas as pl
from jax.experimental.pallas import tpu as pltpu
from jax.sharding import Mesh
from jax.sharding import PartitionSpec as P

TAPS = 129
BANDS = 8
TILE = 128
WAFERS = 8
POLY = 6
NINT = 16
OBS = 4
DET = 512
SAMP = 32768
TILES = 16

QUADS = 4
GROUPS = 8
ROWS = 16
BLOCKS = SAMP // TILE
SLABS = QUADS * GROUPS
SLAB_BLOCKS = BLOCKS // SLABS
BAND_BLOCKS = BLOCKS // BANDS
HALF = TILE // 2
GROUP_AXES = ("obs", "q")
SLAB_AXES = ("q", "g")
ALL_AXES = ("obs", "q", "g")

prior_weight = 1.0
MIB = 1024 * 1024
BAND_SLABS = SLABS // BANDS
SLAB_LEN = SLAB_BLOCKS * TILE
SHARE = TILE // SLABS
SUM_ROWS = TILES * SHARE


def vmem():
    return pl.BlockSpec(memory_space=pltpu.VMEM)


def smem():
    return pl.BlockSpec(memory_space=pltpu.SMEM)


def hbm():
    return pl.BlockSpec(memory_space=pltpu.HBM)


def call(kernel, out_shape, in_specs, out_specs, scratch=(), limit=32, micros=2):
    return pl.pallas_call(
        kernel,
        out_shape=out_shape,
        in_specs=in_specs,
        out_specs=out_specs,
        scratch_shapes=list(scratch),
        compiler_params=pltpu.CompilerParams(vmem_limit_bytes=limit * MIB),
        cost_estimate=pl.CostEstimate(
            flops=0, bytes_accessed=micros * 3_000_000, transcendentals=0
        ),
    )


def lane_ids(shape):
    return lax.broadcasted_iota(jnp.int32, shape, len(shape) - 1)


def row_ids(shape):
    return lax.broadcasted_iota(jnp.int32, shape, len(shape) - 2)


def circulant(row):
    return pltpu.roll(jnp.broadcast_to(row, (TILE, TILE)), 0, 1, stride=1, stride_axis=0)


def start(block, size):
    return pl.multiple_of(block * size, size)


def forward_kernel(
    x_ref, taps_ref, meta_ref, y_ref, x_buf, taps_buf, shifted, summed, y_buf, first, last, sems
):
    taps_copy = pltpu.make_async_copy(taps_ref, taps_buf, sems.at[0, BANDS])
    taps_copy.start()

    def x_copy(band):
        part = pl.ds(start(band, BAND_BLOCKS * TILE), BAND_BLOCKS * TILE)
        return pltpu.make_async_copy(x_ref.at[0, :, part], x_buf.at[:, part], sems.at[0, band])

    def y_copy(band):
        part = pl.ds(band * BAND_SLABS, BAND_SLABS)
        return pltpu.make_async_copy(y_buf.at[part], y_ref.at[part], sems.at[1, band])

    for band in range(BANDS):
        x_copy(band).start()
    low = lane_ids((ROWS, TILE)) < HALF
    rows, lanes = row_ids((TILE, TILE)), lane_ids((TILE, TILE))
    in_first = lanes <= rows
    on_diag = lanes == rows
    reverse = (rows == ((TILE - lanes) & (TILE - 1))).astype(jnp.float32).astype(jnp.bfloat16)
    taps_copy.wait()
    taps = taps_buf[...].astype(jnp.float32)
    front = taps[:, :, :TILE].reshape(ROWS * BANDS, TILE).astype(jnp.bfloat16)
    first[...] = jnp.dot(front, reverse, preferred_element_type=jnp.float32)
    last[...] = jnp.broadcast_to(taps[:, :, TILE:], (ROWS, BANDS, TILE)).reshape(
        ROWS * BANDS, TILE
    )

    def rolled(block):
        part = x_buf[:, pl.ds(start(block, TILE), TILE)]
        return pltpu.roll(part.astype(jnp.float32), HALF, 1)

    x_copy(0).wait()
    opening = rolled(0)
    shifted[:ROWS, :] = jnp.where(low, 0.0, opening)

    def one_band(band, before):
        @pl.when(band < BANDS - 1)
        def _():
            x_copy(band + 1).wait()

        for inner in range(1, BAND_BLOCKS + 1):
            block = band * BAND_BLOCKS + inner
            if inner == BAND_BLOCKS:
                here = jnp.where(
                    band < BANDS - 1, rolled(jnp.minimum(block, BLOCKS - 1)), 0.0
                )
            else:
                here = rolled(block)
            shifted[pl.ds(start(block, ROWS), ROWS), :] = jnp.where(low, before, here)
            before = here
        for det in range(ROWS):
            pair = det * BANDS + band
            turned = circulant(first[pl.ds(pair, 1), :])
            end = jnp.broadcast_to(last[pl.ds(pair, 1), :], (TILE, TILE))
            upper = jnp.where(in_first, turned, 0.0)
            lower = jnp.where(in_first, jnp.where(on_diag, end, 0.0), turned)
            kernel = jnp.concatenate([upper, lower], axis=0).astype(jnp.bfloat16)
            base = band * BAND_BLOCKS * ROWS + det
            one = shifted[pl.ds(base, BAND_BLOCKS, stride=ROWS), :]
            two = shifted[pl.ds(base + ROWS, BAND_BLOCKS, stride=ROWS), :]
            window = jnp.concatenate([one, two], axis=1).astype(jnp.bfloat16)
            summed[pl.ds(base, BAND_BLOCKS, stride=ROWS), :] = jnp.dot(
                window, kernel, preferred_element_type=jnp.float32
            )
        for part in range(BAND_SLABS):
            slab = band * BAND_SLABS + part
            for inner in range(SLAB_BLOCKS):
                block = slab * SLAB_BLOCKS + inner
                y_buf[slab, :, inner * TILE : (inner + 1) * TILE] = summed[
                    pl.ds(start(block, ROWS), ROWS), :
                ].astype(jnp.bfloat16)
            y_buf[slab, :, SLAB_LEN:] = meta_ref[...]
        y_copy(band).start()
        return before

    lax.fori_loop(0, BANDS, one_band, opening)
    for band in range(BANDS):
        y_copy(band).wait()


def count_flags(bounds_ref, blocks, offset):
    sample = (row_ids((blocks, TILE)) + offset) * TILE + lane_ids((blocks, TILE))
    passed = jnp.zeros((blocks, TILE), jnp.int32)
    for bound in range(2 * NINT):
        passed = passed + (bounds_ref[0, bound] <= sample).astype(jnp.int32)
    return (passed & 1).astype(jnp.float32)


def clean_kernel(
    bounds_ref, data_ref, basis_ref, basis_t_ref, inverse_ref, weight_ref, out_ref, sums_ref, tiles_ref
):
    data = data_ref[:, :, :SLAB_LEN].reshape(DET, SLAB_LEN)
    tiles_ref[...] = data_ref[:, :, SLAB_LEN:].astype(jnp.float32)[:, 0, :].astype(jnp.int32)
    raw = jnp.dot(basis_ref[...], data, preferred_element_type=jnp.float32)
    coef = jnp.dot(
        inverse_ref[...],
        raw,
        precision=lax.Precision.HIGHEST,
        preferred_element_type=jnp.float32,
    )
    high = coef.astype(jnp.bfloat16)
    rest = (coef - high.astype(jnp.float32)).astype(jnp.bfloat16)
    both = jnp.concatenate([high, rest], axis=0)
    fitted = jnp.dot(basis_t_ref[...], both, preferred_element_type=jnp.float32)
    cleaned = (data.astype(jnp.float32) - fitted).astype(jnp.bfloat16)
    out_ref[...] = cleaned.reshape(out_ref.shape)
    flags = count_flags(bounds_ref, SLAB_BLOCKS, 0)
    for block in range(SLAB_BLOCKS):
        part = cleaned[:, block * TILE : (block + 1) * TILE].astype(jnp.float32)
        weighted = (part * weight_ref[...]).reshape(DET // TILE, TILE, TILE)
        total = jnp.sum(weighted, axis=0) * flags[block : block + 1, :]
        for quad in range(QUADS):
            for group in range(GROUPS):
                row = group * ROWS + quad * SHARE
                sums_ref[quad * GROUPS + group, block * SHARE : (block + 1) * SHARE, :] = total[
                    row : row + SHARE, :
                ]


def scan_kernel(bounds_ref, tiles_ref, weight_ref, flags_ref, scan_ref, acc):
    for band in range(BANDS):
        flags_ref[band * BAND_BLOCKS : (band + 1) * BAND_BLOCKS, :] = count_flags(
            bounds_ref, BAND_BLOCKS, band * BAND_BLOCKS
        )
    acc[...] = jnp.zeros_like(acc)

    def add_slab(slab, carry):
        for inner in range(SLAB_BLOCKS):
            tile = tiles_ref[slab, inner]
            row = flags_ref[pl.ds(slab * SLAB_BLOCKS + inner, 1), :]
            acc[tile] = acc[tile] + jnp.broadcast_to(row, (8, TILE))
        return carry

    lax.fori_loop(0, SLABS, add_slab, 0)
    for tile in range(TILES):
        scan_ref[tile : tile + 1, :] = acc[tile, :1, :]
    scan_ref[TILES:, :] = weight_ref[...]


def bin_kernel(tiles_ref, sums_ref, scan_ref, out_ref, acc):
    acc[...] = jnp.zeros_like(acc)
    upper = row_ids((2 * SHARE, TILE)) < SHARE

    def add_slab(slab, carry):
        for pair in range(SLAB_BLOCKS // 2):
            part = sums_ref[slab, pair * 2 * SHARE : (pair + 1) * 2 * SHARE, :]
            even = tiles_ref[slab, 2 * pair]
            acc[even] = acc[even] + jnp.where(upper, part, 0.0)
            odd = tiles_ref[slab, 2 * pair + 1]
            acc[odd] = acc[odd] + jnp.where(upper, 0.0, part)
        return carry

    lax.fori_loop(0, SLABS, add_slab, 0)
    for tile in range(TILES):
        both = acc[tile]
        out_ref[tile * SHARE : (tile + 1) * SHARE, :] = both[:SHARE, :] + both[SHARE:, :]
    out_ref[SUM_ROWS:, :] = scan_ref[...]


def sky_kernel(a_ref, b_ref, c_ref, d_ref, sky_ref, sky_b_ref):
    refs = (a_ref, b_ref, c_ref, d_ref)
    upper = row_ids((2 * SHARE, TILE)) < SHARE
    weights = [ref[SUM_ROWS + TILES :, :] for ref in refs]
    for pair in range(TILES // 2):
        rows = slice(pair * 2 * SHARE, (pair + 1) * 2 * SHARE)
        total = jnp.zeros((2 * SHARE, TILE), jnp.float32)
        hits = jnp.zeros((2 * SHARE, TILE), jnp.float32)
        for ref, weight in zip(refs, weights):
            total = total + ref[rows, :]
            even = ref[SUM_ROWS + 2 * pair : SUM_ROWS + 2 * pair + 1, :]
            odd = ref[SUM_ROWS + 2 * pair + 1 : SUM_ROWS + 2 * pair + 2, :]
            hits = hits + weight * jnp.where(upper, even, odd)
        sky_ref[rows, :] = total / (hits + prior_weight)
    sky_b_ref[...] = sky_ref[...].astype(jnp.bfloat16)


def adjoint_kernel(
    tiles_ref, flags_ref, data_ref, sky_ref, taps_ref, out_ref, sky, resid, same, after, out_buf, first, last, sems
):
    def out_copy(band):
        part = pl.ds(start(band, BAND_BLOCKS * TILE), BAND_BLOCKS * TILE)
        return pltpu.make_async_copy(out_buf.at[:, part], out_ref.at[0, :, part], sems.at[band])

    sky[...] = sky_ref[...].astype(jnp.float32)
    taps = taps_ref[...].astype(jnp.float32)
    first[...] = taps[:, :, :TILE].reshape(ROWS * BANDS, TILE)
    last[...] = jnp.broadcast_to(taps[:, :, TILE:], (ROWS, BANDS, TILE)).reshape(
        ROWS * BANDS, TILE
    )
    rows, lanes = row_ids((TILE, TILE)), lane_ids((TILE, TILE))
    in_first = lanes >= rows
    on_diag = lanes == rows
    low = lane_ids((ROWS, TILE)) < HALF
    after[:ROWS, :] = jnp.zeros((ROWS, TILE), jnp.float32)

    def write_block(block, before, here):
        out_buf[:, pl.ds(start(block, TILE), TILE)] = jnp.where(low, before, here)

    def one_band(band, before):
        for part in range(BAND_SLABS):
            slab = band * BAND_SLABS + part
            for inner in range(SLAB_BLOCKS):
                block = slab * SLAB_BLOCKS + inner
                value = data_ref[slab, :, inner * TILE : (inner + 1) * TILE].astype(jnp.float32)
                value = flags_ref[pl.ds(block, 1), :] * (value - sky[tiles_ref[slab, inner]])
                resid[pl.ds(start(block, ROWS), ROWS), :] = value
        for det in range(ROWS):
            pair = det * BANDS + band
            turned = circulant(first[pl.ds(pair, 1), :])
            end = jnp.broadcast_to(last[pl.ds(pair, 1), :], (TILE, TILE))
            upper = jnp.where(in_first, turned, 0.0)
            lower = jnp.where(in_first, jnp.where(on_diag, end, 0.0), turned)
            kernel = jnp.concatenate([upper, lower], axis=1).astype(jnp.bfloat16)
            base = band * BAND_BLOCKS * ROWS + det
            part = resid[pl.ds(base, BAND_BLOCKS, stride=ROWS), :].astype(jnp.bfloat16)
            spread = jnp.dot(part, kernel, preferred_element_type=jnp.float32)
            same[pl.ds(base, BAND_BLOCKS, stride=ROWS), :] = spread[:, :TILE]
            after[pl.ds(base + ROWS, BAND_BLOCKS, stride=ROWS), :] = spread[:, TILE:]
        for inner in range(BAND_BLOCKS):
            block = band * BAND_BLOCKS + inner
            place = pl.ds(start(block, ROWS), ROWS)
            here = pltpu.roll(same[place, :] + after[place, :], HALF, 1)
            if inner == 0:

                @pl.when(band > 0)
                def _():
                    write_block(block - 1, before, here)
                    out_copy(band - 1).start()

            else:
                write_block(block - 1, before, here)
            before = here
        return before

    before = lax.fori_loop(0, BANDS, one_band, jnp.zeros((ROWS, TILE), jnp.float32))
    write_block(BLOCKS - 1, before, pltpu.roll(after[BLOCKS * ROWS :, :], HALF, 1))
    out_copy(BANDS - 1).start()
    for band in range(BANDS):
        out_copy(band).wait()


def make_basis(positions, wafer_group):
    x_pos = positions[0]
    y_pos = positions[1]
    monomials = jnp.stack(
        [jnp.ones_like(x_pos), x_pos, y_pos, x_pos * x_pos, x_pos * y_pos, y_pos * y_pos]
    )
    member = (wafer_group[None, :] == jnp.arange(WAFERS, dtype=jnp.int32)[:, None]).astype(
        jnp.float32
    )
    basis_b = (member[:, None, :] * monomials[None]).reshape(WAFERS * POLY, -1).astype(jnp.bfloat16)
    basis_f = basis_b.astype(jnp.float32)
    gram_matrix = jnp.dot(basis_f, basis_f.T, precision=lax.Precision.HIGHEST)
    factor = jnp.linalg.cholesky(gram_matrix)
    lower_inv = lax.linalg.triangular_solve(
        factor, jnp.eye(WAFERS * POLY, dtype=jnp.float32), left_side=True, lower=True
    )
    inverse = jnp.dot(lower_inv.T, lower_inv, precision=lax.Precision.HIGHEST)
    return (basis_b, inverse)


def exchange(value, axis):
    size = lax.axis_size(axis)
    return [
        lax.ppermute(value, axis, [(src, (src + step) % size) for src in range(size)])
        for step in range(1, size)
    ]


def local(timestreams, filter_taps, scan_bounds, tile_index, det_weights, positions, wafer_group):
    f32, bf16 = jnp.float32, jnp.bfloat16
    shape = jax.ShapeDtypeStruct
    buffer = pltpu.VMEM
    quad = lax.axis_index("q")
    group = lax.axis_index("g")
    slab = lax.axis_index(SLAB_AXES)
    taps = filter_taps.reshape(ROWS, BANDS, TAPS)
    meta = jnp.pad(tile_index[0].astype(bf16), (0, TILE - SLAB_BLOCKS))
    filtered = call(
        forward_kernel,
        shape((SLABS, ROWS, SLAB_LEN + TILE), bf16),
        [hbm(), hbm(), vmem()],
        hbm(),
        [
            buffer((ROWS, SAMP), bf16),
            buffer((ROWS, BANDS, TAPS), bf16),
            buffer(((BLOCKS + 1) * ROWS, TILE), f32),
            buffer((BLOCKS * ROWS, TILE), f32),
            buffer((SLABS, ROWS, SLAB_LEN + TILE), bf16),
            buffer((ROWS * BANDS, TILE), f32),
            buffer((ROWS * BANDS, TILE), f32),
            pltpu.SemaphoreType.DMA((2, BANDS + 1)),
        ],
        limit=60,
        micros=7,
    )(timestreams, taps, jnp.broadcast_to(meta[None], (ROWS, TILE)))
    gathered = lax.all_to_all(filtered, SLAB_AXES, split_axis=0, concat_axis=0, tiled=True)

    basis, inverse = make_basis(positions, wafer_group)
    basis_t = jnp.concatenate([basis, basis], axis=0).T
    weights = det_weights[0].astype(f32)
    lane_weights = jnp.broadcast_to(weights[:, None], (DET, TILE))
    row_weights = jnp.sum(weights.reshape(DET // TILE, TILE), axis=0)
    own_rows = lax.dynamic_slice_in_dim(row_weights, group * ROWS + quad * SHARE, SHARE)
    own_rows = jnp.broadcast_to(jnp.tile(own_rows, 2)[:, None], (2 * SHARE, TILE))
    cleaned, sums, tiles = call(
        clean_kernel,
        (
            shape((SLABS, ROWS, SLAB_LEN), bf16),
            shape((SLABS, SLAB_BLOCKS * SHARE, TILE), f32),
            shape((SLABS, TILE), jnp.int32),
        ),
        [smem()] + [vmem()] * 5,
        (vmem(), vmem(), vmem()),
    )(scan_bounds - slab * SLAB_LEN, gathered, basis, basis_t, inverse, lane_weights)
    sums = lax.all_to_all(sums, SLAB_AXES, split_axis=0, concat_axis=0, tiled=True)
    flags, scans = call(
        scan_kernel,
        (shape((BLOCKS, TILE), f32), shape((TILES + 2 * SHARE, TILE), f32)),
        [smem(), smem(), vmem()],
        (vmem(), vmem()),
        [buffer((TILES, 8, TILE), f32)],
    )(scan_bounds, tiles, own_rows)
    cleaned, sums = lax.optimization_barrier((cleaned, sums))
    returned = lax.all_to_all(cleaned, SLAB_AXES, split_axis=0, concat_axis=0, tiled=True)

    part = call(
        bin_kernel,
        shape((SUM_ROWS + TILES + 2 * SHARE, TILE), f32),
        [smem(), vmem(), vmem()],
        vmem(),
        [buffer((TILES, 2 * SHARE, TILE), f32)],
    )(tiles, sums, scans)
    sky, sky_b = call(
        sky_kernel,
        (shape((SUM_ROWS, TILE), f32), shape((SUM_ROWS, TILE), bf16)),
        [vmem()] * OBS,
        (vmem(), vmem()),
        micros=1,
    )(part, *exchange(part, "obs"))
    held = jnp.stack([sky_b] + exchange(sky_b, "q")).reshape(QUADS, TILES, SHARE, TILE)
    held = [
        lax.dynamic_index_in_dim(held, lax.rem(quad - src + QUADS, QUADS), 0, keepdims=False)
        for src in range(QUADS)
    ]
    sky_rows = jnp.stack(held, axis=1).reshape(TILES, ROWS, TILE)
    sky_row = lax.dynamic_slice_in_dim(
        sky.reshape(TILES, SHARE, TILE), lax.axis_index("obs"), 1, 1
    )
    moves = [
        ((o * QUADS + q) * GROUPS + g, g * ROWS + q * SHARE + o)
        for o in range(OBS)
        for q in range(QUADS)
        for g in range(GROUPS)
    ]
    sky_own = lax.ppermute(sky_row, ALL_AXES, moves)
    out = call(
        adjoint_kernel,
        shape((1, ROWS, SAMP), f32),
        [smem(), vmem(), vmem(), vmem(), vmem()],
        hbm(),
        [
            buffer((TILES, ROWS, TILE), f32),
            buffer((BLOCKS * ROWS, TILE), f32),
            buffer((BLOCKS * ROWS, TILE), f32),
            buffer(((BLOCKS + 1) * ROWS, TILE), f32),
            buffer((ROWS, SAMP), f32),
            buffer((ROWS * BANDS, TILE), f32),
            buffer((ROWS * BANDS, TILE), f32),
            pltpu.SemaphoreType.DMA((BANDS,)),
        ],
        micros=9,
    )(tiles, flags, returned, sky_rows, taps)
    return (out, sky_own)


def solution(mesh):
    split = Mesh(mesh.devices.reshape(OBS, QUADS, GROUPS), ALL_AXES)
    placed = (
        P("obs", SLAB_AXES, None),
        P("obs", SLAB_AXES, None, None),
        P("obs", None),
        P("obs", SLAB_AXES),
        P("obs", None),
        P(),
        P(),
    )
    return jax.shard_map(
        local,
        mesh=split,
        in_specs=placed,
        out_specs=(P("obs", SLAB_AXES, None), P(None, ALL_AXES, None)),
        check_vma=False,
    )
```

time: 123 us -> 95.5 us (0.78)
  the two profiles are of different devices: /device:TPU:1 before, /device:TPU:14 now
where the time goes in v2:
time: 95.5 us; the launch traced here: 95 us
  starting transfers between devices  27.6 us (29%)
  Pallas kernels  20.2 us (21%)
  waiting for transfers between devices  18.5 us (19%)
  blocking collectives  15 us (16%)
  other arithmetic  10.3 us (11%)
  local copies, waits for them, and re-layouts  1.89 us (2%)
  between operations  0.97 us (1%)
    all_to_all x1, blocking collectives, local(): lax.all_to_all(sums, SLAB_AXES, split_axis=0, concat_axis=0, tiled=True)  15 us
    ppermute x6, starting transfers between devices, exchange(): lax.ppermute(value, axis, [(src, (src + step) % size) for src in range(si...  10.3 us
    ppermute x1, waiting for transfers between devices, local(): sky_own = lax.ppermute(sky_row, ALL_AXES, moves)  8.85 us
    all_to_all x1, starting transfers between devices, local(): lax.all_to_all(filtered, SLAB_AXES, split_axis=0, concat_axis=0, tiled=True)  7.6 us
    pallas_call x1, Pallas kernels, local(): call(adjoint_kernel, shape((1, ROWS, SAMP), f32), [smem(), vmem(), vmem()...  7.26 us
    all_to_all x1, starting transfers between devices, local(): lax.all_to_all(cleaned, SLAB_AXES, split_axis=0, concat_axis=0, tiled=True)  7.02 us
    pallas_call x1, Pallas kernels, local(): call(forward_kernel, shape((SLABS, ROWS, SLAB_LEN + TILE), bf16), [hbm(),...  6.71 us
    all_to_all x1, waiting for transfers between devices, local(): lax.all_to_all(filtered, SLAB_AXES, split_axis=0, concat_axis=0, tiled=True)  5.16 us
  transfers between devices with their start and end apart: 9, of which 5 were waited for; matrix products, arithmetic and copies ran while one was open for 11% of the time, Pallas kernels for 4%

profile of v2, /device:TPU:14, one launch (start us, length us, event | category | flops | bytes accessed | tf_op | source)
XLA Modules:
  0.0 95.0 jit_solution(10443288001696354781)
XLA Ops:
  0.6 0.7 convert_bitcast_fusion
  1.3 0.6 broadcast_in_dim.10.meta_ref
  1.9 6.7 %shard_map.86 = bf16[32,16,1152]{2,1,0:T(8,128)(2,1)} custom-call(bf16[1,16,32768]{2,1,0:T(8,128)(2,1)} %x_ref.1, bf16[16,8,129]{2,1,0:T(8,128)(2,1)} %bitcast.34, bf16[16,128]{1,0:T(8,128)(2,1)} %broadcast_in_dim.10.meta_ref), custom_call_target="tpu_custom_call" | custom-call | bytes 21000000 | tf_op jit(solution)/shard_map/pallas_call | solution.py:364
  8.6 0.0 copy-start.2
  8.6 0.0 copy-start.3
  8.6 0.0 copy-start.4
  8.6 0.0 copy-start.1
  8.7 7.6 %all-to-all-start = ((bf16[32,16,1152]{2,1,0:T(8,128)(2,1)}), bf16[32,16,1152]{2,1,0:T(8,128)(2,1)S(1)}, u32[]{:S(2)}, u32[]{:S(2)}) async-start(bf16[32,16,1152]{2,1,0:T(8,128)(2,1)} %shard_map.86), calls=%async_computation | async-start | bytes 2359296 | tf_op jit(solution)/shard_map/all_to_all | solution.py:382
  16.4 0.1 fusion.5
  16.5 0.1 copy.14
  16.6 4.4 %cholesky.17 = f32[48,48]{1,0:T(8,128)S(1)} custom-call(f32[48,48]{1,0:T(8,128)S(1)} %fusion.3), custom_call_target="Cholesky" | custom-call | tf_op jit(solution)/shard_map/jit(cholesky)/cholesky | solution.py:339
  21.1 0.1 copy.12
  21.2 0.6 compare_reduce_fusion
  21.8 0.7 fusion
  22.5 3.7 %custom-call.6 = f32[1,48,48]{1,2,0:T(8,128)S(1)} custom-call(f32[1,48,48]{2,1,0:T(8,128)S(1)} %fusion), custom_call_target="InvertDiagBlocksLowerTriangular" | custom-call | tf_op jit(solution)/shard_map/triangular_solve | solution.py:340
  26.2 0.1 maximum_bitcast_fusion.basis_t_ref
  26.3 0.2 fusion.1
  26.5 0.2 fusion.6.inverse_ref
  26.8 5.2 %all-to-all-done.data_ref = bf16[32,16,1152]{2,1,0:T(8,128)(2,1)S(1)} async-done(((bf16[32,16,1152]{2,1,0:T(8,128)(2,1)}), bf16[32,16,1152]{2,1,0:T(8,128)(2,1)S(1)}, u32[]{:S(2)}, u32[]{:S(2)}) %all-to-all-start) | async-done | bytes 1179680 | tf_op jit(solution)/shard_map/all_to_all | solution.py:382
  31.9 0.1 broadcast_in_dim.11.weight_ref
  32.1 2.6 %shard_map.87 = (bf16[32,16,1024]{2,1,0:T(8,128)(2,1)}, f32[32,32,128]{2,1,0:T(8,128)S(1)}, s32[32,128]{1,0:T(8,128)S(1)}) custom-call(s32[1,32]{1,0:T(1,128)S(1)} %broadcast_subtract_fusion.bounds_ref, bf16[32,16,1152]{2,1,0:T(8,128)(2,1)S(1)} %all-to-all-done.data_ref, bf16[48,512]{1,0:T(8,128)(2,1)S(1)} %convert_element_type.46.basis_ref, ...), custom_call_target="tpu_custom_call" | custom-call | bytes 6000000 | tf_op jit(solution)/shard_map/pallas_call | solution.py:391
  34.6 15.0 %all_to_all.15.sums_ref = f32[32,32,128]{2,1,0:T(8,128)S(1)} all-to-all(f32[32,32,128]{2,1,0:T(8,128)S(1)} %get-tuple-element.14), channel_id=1, replica_groups=mesh['obs'=4,'q'=4,'g'=8] {'q','g'}, dimensions={0} | all-to-all | bytes 1048576 | tf_op jit(solution)/shard_map/all_to_all | solution.py:401
  49.7 7.0 %all-to-all-start.2 = ((bf16[32,16,1024]{2,1,0:T(8,128)(2,1)}), bf16[32,16,1024]{2,1,0:T(8,128)(2,1)S(1)}, u32[]{:S(2)}, u32[]{:S(2)}) async-start(bf16[32,16,1024]{2,1,0:T(8,128)(2,1)} %get-tuple-element.15), calls=%async_computation.2 | async-start | bytes 2097152 | tf_op jit(solution)/shard_map/all_to_all | solution.py:410
  56.7 0.0 copy-start
  56.8 0.1 dynamic_slice.19
  56.8 0.1 broadcast_in_dim.12
  56.9 0.1 broadcast_in_dim.13.weight_ref
  57.0 2.0 %shard_map.88 = (f32[256,128]{1,0:T(8,128)S(1)}, f32[24,128]{1,0:T(8,128)S(1)}) custom-call(s32[1,32]{1,0:T(1,128)S(1)} %copy-done.1, s32[32,128]{1,0:T(8,128)S(1)} %get-tuple-element.11.tiles_ref, f32[8,128]{1,0:T(8,128)S(1)} %broadcast_in_dim.13.weight_ref), custom_call_target="tpu_custom_call" | custom-call | bytes 6000000 | tf_op jit(solution)/shard_map/pallas_call | solution.py:402
  59.0 1.6 %shard_map.89.a_ref = f32[88,128]{1,0:T(8,128)S(1)} custom-call(s32[32,128]{1,0:T(8,128)S(1)} %get-tuple-element.11.tiles_ref, f32[32,32,128]{2,1,0:T(8,128)S(1)} %all_to_all.15.sums_ref, f32[24,128]{1,0:T(8,128)S(1)} %get-tuple-element.17.scan_ref), custom_call_target="tpu_custom_call" | custom-call | bytes 6000000 | tf_op jit(solution)/shard_map/pallas_call | solution.py:412
  60.6 4.1 %collective-permute-start.2 = (f32[88,128]{1,0:T(8,128)S(1)}, f32[88,128]{1,0:T(8,128)S(1)}, u32[]{:S(2)}, u32[]{:S(2)}) collective-permute-start(f32[88,128]{1,0:T(8,128)S(1)} %shard_map.89.a_ref), channel_id=1, source_target_pairs={{0,96},{32,0},{64,32},{96,64},{1,97},{33,1},{65,33},{97,65},{2,98}... | collective-permute-start | bytes 135176 | tf_op jit(solution)/shard_map/ppermute | solution.py:350
  64.7 0.0 collective-permute-start.1
  64.7 1.3 %collective-permute-start = (f32[88,128]{1,0:T(8,128)S(1)}, f32[88,128]{1,0:T(8,128)S(1)}, u32[]{:S(2)}, u32[]{:S(2)}) collective-permute-start(f32[88,128]{1,0:T(8,128)S(1)} %shard_map.89.a_ref), channel_id=1, source_target_pairs={{0,32},{32,64},{64,96},{96,0},{1,33},{33,65},{65,97},{97,1},{2,34}... | collective-permute-start | bytes 135176 | tf_op jit(solution)/shard_map/ppermute | solution.py:350
  66.0 0.4 collective-permute-done.2.d_ref
  66.5 3.9 %collective-permute-done.1.c_ref = f32[88,128]{1,0:T(8,128)S(1)} collective-permute-done((f32[88,128]{1,0:T(8,128)S(1)}, f32[88,128]{1,0:T(8,128)S(1)}, u32[]{:S(2)}, u32[]{:S(2)}) %collective-permute-start.1) | collective-permute-done | bytes 45088 | tf_op jit(solution)/shard_map/ppermute | solution.py:350
  70.3 0.1 collective-permute-done.b_ref
  70.5 0.6 collective-permute-start.5
  71.1 2.5 %collective-permute-start.4 = (bf16[64,128]{1,0:T(8,128)(2,1)S(1)}, bf16[64,128]{1,0:T(8,128)(2,1)S(1)}, u32[]{:S(2)}, u32[]{:S(2)}) collective-permute-start(bf16[64,128]{1,0:T(8,128)(2,1)S(1)} %get-tuple-element.18), channel_id=1, source_target_pairs={{0,16},{8,24},{16,0},{24,8},{1,17},{9,25},{17,1},{25,9},{2,18},{10... | collective-permute-start | bytes 49160 | tf_op jit(solution)/shard_map/ppermute | solution.py:350
  73.6 1.8 %collective-permute-start.3 = (bf16[64,128]{1,0:T(8,128)(2,1)S(1)}, bf16[64,128]{1,0:T(8,128)(2,1)S(1)}, u32[]{:S(2)}, u32[]{:S(2)}) collective-permute-start(bf16[64,128]{1,0:T(8,128)(2,1)S(1)} %get-tuple-element.18), channel_id=1, source_target_pairs={{0,8},{8,16},{16,24},{24,0},{1,9},{9,17},{17,25},{25,1},{2,10},{10... | collective-permute-start | bytes 49160 | tf_op jit(solution)/shard_map/ppermute | solution.py:350
  75.4 2.7 %collective-permute-start.6 = (f32[16,1,128]{2,1,0:T(1,128)S(1)}, f32[16,1,128]{2,1,0:T(1,128)S(1)}, u32[]{:S(2)}, u32[]{:S(2)}) collective-permute-start(f32[16,1,128]{2,1,0:T(1,128)S(1)} %constant_dynamic-slice_fusion), channel_id=1, source_target_pairs={{0,0},{1,16},{2,32},{3,48},{4,64},{5,80},{6,96},{7,112},{8,4},{9,2... | collective-permute-start | bytes 24584 | tf_op jit(solution)/shard_map/ppermute | solution.py:441
  78.1 8.9 %collective-permute-done.6 = f32[16,1,128]{2,1,0:T(1,128)S(1)} collective-permute-done((f32[16,1,128]{2,1,0:T(1,128)S(1)}, f32[16,1,128]{2,1,0:T(1,128)S(1)}, u32[]{:S(2)}, u32[]{:S(2)}) %collective-permute-start.6) | collective-permute-done | bytes 8224 | tf_op jit(solution)/shard_map/ppermute | solution.py:441
  87.0 0.0 collective-permute-done.5
  87.0 0.0 collective-permute-done.4
  87.0 0.0 collective-permute-done.3
  87.0 0.1 pad_maximum_fusion
  87.1 0.1 pad_maximum_fusion.1
  87.2 0.0 all-to-all-done.2.data_ref
  87.2 7.3 %shard_map.91 = f32[1,16,32768]{2,1,0:T(8,128)} custom-call(s32[32,128]{1,0:T(8,128)S(1)} %get-tuple-element.11.tiles_ref, f32[256,128]{1,0:T(8,128)S(1)} %get-tuple-element.12.flags_ref, bf16[32,16,1024]{2,1,0:T(8,128)(2,1)S(1)} %all-to-all-done.2.data_ref, bf16[16,16,128]{2,1,0:T(8,128)(2,1)S(1)} %bitcast.36, bf16[16,8,129]{2,1,0:T(8,128)(2,1)S(1)} %bitcast.35), custom_call_target="tpu_custom_call" | custom-call | bytes 27000000 | tf_op jit(solution)/shard_map/pallas_call | solution.py:442
  94.4 0.6 copy.16
  (21 shorter events, 0.3 us)
Async XLA Ops:
  8.6 7.7 %copy-start.2 = (f32[2,512]{1,0:T(2,128)S(1)}, f32[2,512]{1,0:T(2,128)}, u32[]{:S(2)}) copy-start(f32[2,512]{1,0:T(2,128)} %param.12) | copy-start | bytes 12292
  8.6 7.7 %copy-start.3 = (s32[512]{0:T(512)S(1)}, s32[512]{0:T(512)}, u32[]{:S(2)}) copy-start(s32[512]{0:T(512)} %param.13) | copy-start | bytes 6148
  8.6 12.6 %copy-start.4 = (bf16[1,512]{1,0:T(2,128)(2,1)S(1)}, bf16[1,512]{1,0:T(2,128)(2,1)}, u32[]{:S(2)}) copy-start(bf16[1,512]{1,0:T(2,128)(2,1)} %param.11) | copy-start | bytes 3076
  8.6 17.7 %copy-start.1 = (s32[1,32]{1,0:T(1,128)S(1)}, s32[1,32]{1,0:T(1,128)}, u32[]{:S(2)}) copy-start(s32[1,32]{1,0:T(1,128)} %bounds_ref.1) | copy-start | bytes 388
  8.7 23.3 %all-to-all-start = ((bf16[32,16,1152]{2,1,0:T(8,128)(2,1)}), bf16[32,16,1152]{2,1,0:T(8,128)(2,1)S(1)}, u32[]{:S(2)}, u32[]{:S(2)}) async-start(bf16[32,16,1152]{2,1,0:T(8,128)(2,1)} %shard_map.86), calls=%async_computation | async-start | bytes 2359296 | tf_op jit(solution)/shard_map/all_to_all | solution.py:382
  49.7 37.5 %all-to-all-start.2 = ((bf16[32,16,1024]{2,1,0:T(8,128)(2,1)}), bf16[32,16,1024]{2,1,0:T(8,128)(2,1)S(1)}, u32[]{:S(2)}, u32[]{:S(2)}) async-start(bf16[32,16,1024]{2,1,0:T(8,128)(2,1)} %get-tuple-element.15), calls=%async_computation.2 | async-start | bytes 2097152 | tf_op jit(solution)/shard_map/all_to_all | solution.py:410
  56.7 30.5 %copy-start = (bf16[1,16,8,129]{3,2,1,0:T(8,128)(2,1)S(1)}, bf16[1,16,8,129]{3,2,1,0:T(8,128)(2,1)}, u32[]{:S(2)}) copy-start(bf16[1,16,8,129]{3,2,1,0:T(8,128)(2,1)} %param.8) | copy-start | bytes 99076
  60.6 5.8 %collective-permute-start.2 = (f32[88,128]{1,0:T(8,128)S(1)}, f32[88,128]{1,0:T(8,128)S(1)}, u32[]{:S(2)}, u32[]{:S(2)}) collective-permute-start(f32[88,128]{1,0:T(8,128)S(1)} %shard_map.89.a_ref), channel_id=1, source_target_pairs={{0,96},{32,0},{64,32},{96,64},{1,97},{33,1},{65,33},{97,65},{2,98}... | collective-permute-start | bytes 135176 | tf_op jit(solution)/shard_map/ppermute | solution.py:350
  64.7 5.6 %collective-permute-start.1 = (f32[88,128]{1,0:T(8,128)S(1)}, f32[88,128]{1,0:T(8,128)S(1)}, u32[]{:S(2)}, u32[]{:S(2)}) collective-permute-start(f32[88,128]{1,0:T(8,128)S(1)} %shard_map.89.a_ref), channel_id=1, source_target_pairs={{0,64},{32,96},{64,0},{96,32},{1,65},{33,97},{65,1},{97,33},{2,66}... | collective-permute-start | bytes 135176 | tf_op jit(solution)/shard_map/ppermute | solution.py:350
  64.7 5.7 %collective-permute-start = (f32[88,128]{1,0:T(8,128)S(1)}, f32[88,128]{1,0:T(8,128)S(1)}, u32[]{:S(2)}, u32[]{:S(2)}) collective-permute-start(f32[88,128]{1,0:T(8,128)S(1)} %shard_map.89.a_ref), channel_id=1, source_target_pairs={{0,32},{32,64},{64,96},{96,0},{1,33},{33,65},{65,97},{97,1},{2,34}... | collective-permute-start | bytes 135176 | tf_op jit(solution)/shard_map/ppermute | solution.py:350
  70.5 16.5 %collective-permute-start.5 = (bf16[64,128]{1,0:T(8,128)(2,1)S(1)}, bf16[64,128]{1,0:T(8,128)(2,1)S(1)}, u32[]{:S(2)}, u32[]{:S(2)}) collective-permute-start(bf16[64,128]{1,0:T(8,128)(2,1)S(1)} %get-tuple-element.18), channel_id=1, source_target_pairs={{0,24},{8,0},{16,8},{24,16},{1,25},{9,1},{17,9},{25,17},{2,26},{10... | collective-permute-start | bytes 49160 | tf_op jit(solution)/shard_map/ppermute | solution.py:350
  71.1 15.9 %collective-permute-start.4 = (bf16[64,128]{1,0:T(8,128)(2,1)S(1)}, bf16[64,128]{1,0:T(8,128)(2,1)S(1)}, u32[]{:S(2)}, u32[]{:S(2)}) collective-permute-start(bf16[64,128]{1,0:T(8,128)(2,1)S(1)} %get-tuple-element.18), channel_id=1, source_target_pairs={{0,16},{8,24},{16,0},{24,8},{1,17},{9,25},{17,1},{25,9},{2,18},{10... | collective-permute-start | bytes 49160 | tf_op jit(solution)/shard_map/ppermute | solution.py:350
  73.6 13.4 %collective-permute-start.3 = (bf16[64,128]{1,0:T(8,128)(2,1)S(1)}, bf16[64,128]{1,0:T(8,128)(2,1)S(1)}, u32[]{:S(2)}, u32[]{:S(2)}) collective-permute-start(bf16[64,128]{1,0:T(8,128)(2,1)S(1)} %get-tuple-element.18), channel_id=1, source_target_pairs={{0,8},{8,16},{16,24},{24,0},{1,9},{9,17},{17,25},{25,1},{2,10},{10... | collective-permute-start | bytes 49160 | tf_op jit(solution)/shard_map/ppermute | solution.py:350
  75.4 11.6 %collective-permute-start.6 = (f32[16,1,128]{2,1,0:T(1,128)S(1)}, f32[16,1,128]{2,1,0:T(1,128)S(1)}, u32[]{:S(2)}, u32[]{:S(2)}) collective-permute-start(f32[16,1,128]{2,1,0:T(1,128)S(1)} %constant_dynamic-slice_fusion), channel_id=1, source_target_pairs={{0,0},{1,16},{2,32},{3,48},{4,64},{5,80},{6,96},{7,112},{8,4},{9,2... | collective-permute-start | bytes 24584 | tf_op jit(solution)/shard_map/ppermute | solution.py:441

commit v3 on v2

--- a/solution.py
+++ b/solution.py
@@ -82,10 +82,12 @@
 
 
 def forward_kernel(
-    x_ref, taps_ref, meta_ref, y_ref, x_buf, taps_buf, shifted, summed, y_buf, first, last, sems
+    x_ref, taps_ref, tiles_ref, y_ref, x_buf, taps_buf, shifted, summed, y_buf, first, last, tiles, sems
 ):
     taps_copy = pltpu.make_async_copy(taps_ref, taps_buf, sems.at[0, BANDS])
     taps_copy.start()
+    tiles_copy = pltpu.make_async_copy(tiles_ref, tiles, sems.at[1, BANDS])
+    tiles_copy.start()
 
     def x_copy(band):
         part = pl.ds(start(band, BAND_BLOCKS * TILE), BAND_BLOCKS * TILE)
@@ -114,6 +116,12 @@
         part = x_buf[:, pl.ds(start(block, TILE), TILE)]
         return pltpu.roll(part.astype(jnp.float32), HALF, 1)
 
+    tiles_copy.wait()
+    lane = lane_ids((ROWS, TILE))
+    meta = jnp.zeros((ROWS, TILE), jnp.int32)
+    for block in range(SLAB_BLOCKS):
+        meta = jnp.where(lane == block, tiles[0, block], meta)
+    meta = meta.astype(jnp.float32).astype(jnp.bfloat16)
     x_copy(0).wait()
     opening = rolled(0)
     shifted[:ROWS, :] = jnp.where(low, 0.0, opening)
@@ -154,7 +162,7 @@
                 y_buf[slab, :, inner * TILE : (inner + 1) * TILE] = summed[
                     pl.ds(start(block, ROWS), ROWS), :
                 ].astype(jnp.bfloat16)
-            y_buf[slab, :, SLAB_LEN:] = meta_ref[...]
+            y_buf[slab, :, SLAB_LEN:] = meta
         y_copy(band).start()
         return before
 
@@ -172,7 +180,7 @@
 
 
 def clean_kernel(
-    bounds_ref, data_ref, basis_ref, basis_t_ref, inverse_ref, weight_ref, out_ref, sums_ref, tiles_ref
+    bounds_ref, data_ref, basis_ref, basis_t_ref, inverse_ref, weight_ref, out_ref, sums_ref, tiles_ref, sums
 ):
     data = data_ref[:, :, :SLAB_LEN].reshape(DET, SLAB_LEN)
     tiles_ref[...] = data_ref[:, :, SLAB_LEN:].astype(jnp.float32)[:, 0, :].astype(jnp.int32)
@@ -197,9 +205,10 @@
         for quad in range(QUADS):
             for group in range(GROUPS):
                 row = group * ROWS + quad * SHARE
-                sums_ref[quad * GROUPS + group, block * SHARE : (block + 1) * SHARE, :] = total[
+                sums[quad * GROUPS + group, block * SHARE : (block + 1) * SHARE, :] = total[
                     row : row + SHARE, :
                 ]
+    sums_ref[...] = sums[...].astype(jnp.bfloat16)
 
 
 def scan_kernel(bounds_ref, tiles_ref, weight_ref, flags_ref, scan_ref, acc):
@@ -227,8 +236,9 @@
     upper = row_ids((2 * SHARE, TILE)) < SHARE
 
     def add_slab(slab, carry):
+        received = sums_ref[slab].astype(jnp.float32)
         for pair in range(SLAB_BLOCKS // 2):
-            part = sums_ref[slab, pair * 2 * SHARE : (pair + 1) * 2 * SHARE, :]
+            part = received[pair * 2 * SHARE : (pair + 1) * 2 * SHARE, :]
             even = tiles_ref[slab, 2 * pair]
             acc[even] = acc[even] + jnp.where(upper, part, 0.0)
             odd = tiles_ref[slab, 2 * pair + 1]
@@ -360,11 +370,10 @@
     group = lax.axis_index("g")
     slab = lax.axis_index(SLAB_AXES)
     taps = filter_taps.reshape(ROWS, BANDS, TAPS)
-    meta = jnp.pad(tile_index[0].astype(bf16), (0, TILE - SLAB_BLOCKS))
     filtered = call(
         forward_kernel,
         shape((SLABS, ROWS, SLAB_LEN + TILE), bf16),
-        [hbm(), hbm(), vmem()],
+        [hbm(), hbm(), hbm()],
         hbm(),
         [
             buffer((ROWS, SAMP), bf16),
@@ -374,11 +383,12 @@
             buffer((SLABS, ROWS, SLAB_LEN + TILE), bf16),
             buffer((ROWS * BANDS, TILE), f32),
             buffer((ROWS * BANDS, TILE), f32),
+            pltpu.SMEM((1, SLAB_BLOCKS), jnp.int32),
             pltpu.SemaphoreType.DMA((2, BANDS + 1)),
         ],
         limit=60,
         micros=7,
-    )(timestreams, taps, jnp.broadcast_to(meta[None], (ROWS, TILE)))
+    )(timestreams, taps, tile_index)
     gathered = lax.all_to_all(filtered, SLAB_AXES, split_axis=0, concat_axis=0, tiled=True)
 
     basis, inverse = make_basis(positions, wafer_group)
@@ -392,11 +402,12 @@
         clean_kernel,
         (
             shape((SLABS, ROWS, SLAB_LEN), bf16),
-            shape((SLABS, SLAB_BLOCKS * SHARE, TILE), f32),
+            shape((SLABS, SLAB_BLOCKS * SHARE, TILE), bf16),
             shape((SLABS, TILE), jnp.int32),
         ),
         [smem()] + [vmem()] * 5,
         (vmem(), vmem(), vmem()),
+        [buffer((SLABS, SLAB_BLOCKS * SHARE, TILE), f32)],
     )(scan_bounds - slab * SLAB_LEN, gathered, basis, basis_t, inverse, lane_weights)
     sums = lax.all_to_all(sums, SLAB_AXES, split_axis=0, concat_axis=0, tiled=True)
     flags, scans = call(
@@ -406,7 +417,7 @@
         (vmem(), vmem()),
         [buffer((TILES, 8, TILE), f32)],
     )(scan_bounds, tiles, own_rows)
-    cleaned, sums = lax.optimization_barrier((cleaned, sums))
+    cleaned, sums, flags, scans = lax.optimization_barrier((cleaned, sums, flags, scans))
     returned = lax.all_to_all(cleaned, SLAB_AXES, split_axis=0, concat_axis=0, tiled=True)
 
     part = call(
@@ -438,6 +449,7 @@
         for q in range(QUADS)
         for g in range(GROUPS)
     ]
+    sky_row, returned = lax.optimization_barrier((sky_row, returned))
     sky_own = lax.ppermute(sky_row, ALL_AXES, moves)
     out = call(
         adjoint_kernel,

time: 95.5 us -> 86.8 us (0.909)
  the two profiles are of different devices: /device:TPU:14 before, /device:TPU:1 now
where the time goes in v3:
time: 86.8 us; the launch traced here: 85.9 us
  starting transfers between devices  32.4 us (37%)
  waiting for transfers between devices  21.3 us (25%)
  Pallas kernels  19.7 us (23%)
  other arithmetic  9.68 us (11%)
  local copies, waits for them, and re-layouts  1.29 us (1%)
  between operations  0.94 us (1%)
    all_to_all x1, starting transfers between devices, local(): lax.all_to_all(filtered, SLAB_AXES, split_axis=0, concat_axis=0, tiled=True)  8.73 us
    ppermute x6, starting transfers between devices, exchange(): lax.ppermute(value, axis, [(src, (src + step) % size) for src in range(si...  8.46 us
    ppermute x6, waiting for transfers between devices, exchange(): lax.ppermute(value, axis, [(src, (src + step) % size) for src in range(si...  7.42 us
    pallas_call x1, Pallas kernels, local(): call(adjoint_kernel, shape((1, ROWS, SAMP), f32), [smem(), vmem(), vmem()...  7.27 us
    all_to_all x1, waiting for transfers between devices, local(): lax.all_to_all(filtered, SLAB_AXES, split_axis=0, concat_axis=0, tiled=True)  7.18 us
    all_to_all x1, waiting for transfers between devices, local(): lax.all_to_all(sums, SLAB_AXES, split_axis=0, concat_axis=0, tiled=True)  6.71 us
    ppermute x1, starting transfers between devices, local(): sky_own = lax.ppermute(sky_row, ALL_AXES, moves)  6.21 us
    pallas_call x1, Pallas kernels, local(): call(forward_kernel, shape((SLABS, ROWS, SLAB_LEN + TILE), bf16), [hbm(),...  6.07 us
  transfers between devices with their start and end apart: 10, of which 8 were waited for; matrix products, arithmetic and copies ran while one was open for 13% of the time, Pallas kernels for 13%

profile of v3, /device:TPU:1, one launch (start us, length us, event | category | flops | bytes accessed | tf_op | source)
XLA Modules:
  0.0 85.9 jit_solution(13630177397155753437)
XLA Ops:
  0.6 6.1 %shard_map.86 = bf16[32,16,1152]{2,1,0:T(8,128)(2,1)} custom-call(bf16[1,16,32768]{2,1,0:T(8,128)(2,1)} %x_ref.1, bf16[16,8,129]{2,1,0:T(8,128)(2,1)} %bitcast.32, s32[1,8]{1,0:T(1,128)} %tiles_ref.1), custom_call_target="tpu_custom_call" | custom-call | bytes 21000000 | tf_op jit(solution)/shard_map/pallas_call | solution.py:373
  6.7 0.0 copy-start.2
  6.7 0.0 copy-start.3
  6.7 0.0 copy-start.4
  6.7 0.0 copy-start.1
  6.8 8.7 %all-to-all-start = ((bf16[32,16,1152]{2,1,0:T(8,128)(2,1)}), bf16[32,16,1152]{2,1,0:T(8,128)(2,1)S(1)}, u32[]{:S(2)}, u32[]{:S(2)}) async-start(bf16[32,16,1152]{2,1,0:T(8,128)(2,1)} %shard_map.86), calls=%async_computation | async-start | bytes 2359296 | tf_op jit(solution)/shard_map/all_to_all | solution.py:392
  15.5 0.0 copy-done.3
  15.6 0.1 fusion.5
  15.8 0.1 copy.14
  15.9 4.4 %cholesky.17 = f32[48,48]{1,0:T(8,128)S(1)} custom-call(f32[48,48]{1,0:T(8,128)S(1)} %fusion.3), custom_call_target="Cholesky" | custom-call | tf_op jit(solution)/shard_map/jit(cholesky)/cholesky | solution.py:349
  20.3 0.1 copy.12
  20.4 0.6 compare_reduce_fusion
  21.1 0.7 fusion
  21.7 3.7 %custom-call.6 = f32[1,48,48]{1,2,0:T(8,128)S(1)} custom-call(f32[1,48,48]{2,1,0:T(8,128)S(1)} %fusion), custom_call_target="InvertDiagBlocksLowerTriangular" | custom-call | tf_op jit(solution)/shard_map/triangular_solve | solution.py:350
  25.4 0.1 maximum_bitcast_fusion.basis_t_ref
  25.5 0.0 copy-done.1
  25.6 0.2 fusion.1
  25.8 0.2 fusion.6.inverse_ref
  26.0 7.2 %all-to-all-done.data_ref = bf16[32,16,1152]{2,1,0:T(8,128)(2,1)S(1)} async-done(((bf16[32,16,1152]{2,1,0:T(8,128)(2,1)}), bf16[32,16,1152]{2,1,0:T(8,128)(2,1)S(1)}, u32[]{:S(2)}, u32[]{:S(2)}) %all-to-all-start) | async-done | bytes 1179680 | tf_op jit(solution)/shard_map/all_to_all | solution.py:392
  33.2 0.1 broadcast_in_dim.8.weight_ref
  33.3 2.7 %shard_map.87 = (bf16[32,16,1024]{2,1,0:T(8,128)(2,1)}, bf16[32,32,128]{2,1,0:T(8,128)(2,1)}, s32[32,128]{1,0:T(8,128)S(1)}) custom-call(s32[1,32]{1,0:T(1,128)S(1)} %broadcast_subtract_fusion.bounds_ref, bf16[32,16,1152]{2,1,0:T(8,128)(2,1)S(1)} %all-to-all-done.data_ref, bf16[48,512]{1,0:T(8,128)(2,1)S(1)} %convert_element_type.36.basis_ref, ...), custom_call_target="tpu_custom_call" | custom-call | bytes 6000000 | tf_op jit(solution)/shard_map/pallas_call | solution.py:401
  36.0 5.1 %all-to-all-start.1 = ((bf16[32,32,128]{2,1,0:T(8,128)(2,1)}), bf16[32,32,128]{2,1,0:T(8,128)(2,1)S(1)}, u32[]{:S(2)}, u32[]{:S(2)}) async-start(bf16[32,32,128]{2,1,0:T(8,128)(2,1)} %get-tuple-element.17), calls=%async_computation.1 | async-start | bytes 524288 | tf_op jit(solution)/shard_map/all_to_all | solution.py:412
  41.1 0.1 dynamic_slice.19
  41.2 0.1 broadcast_in_dim.9
  41.3 0.1 broadcast_in_dim.10.weight_ref
  41.4 2.0 %shard_map.88 = (f32[256,128]{1,0:T(8,128)S(1)}, f32[24,128]{1,0:T(8,128)S(1)}) custom-call(s32[1,32]{1,0:T(1,128)S(1)} %copy-done.1, s32[32,128]{1,0:T(8,128)S(1)} %get-tuple-element.15.tiles_ref, f32[8,128]{1,0:T(8,128)S(1)} %broadcast_in_dim.10.weight_ref), custom_call_target="tpu_custom_call" | custom-call | bytes 6000000 | tf_op jit(solution)/shard_map/pallas_call | solution.py:413
  43.4 6.7 %all-to-all-done.1.sums_ref = bf16[32,32,128]{2,1,0:T(8,128)(2,1)S(1)} async-done(((bf16[32,32,128]{2,1,0:T(8,128)(2,1)}), bf16[32,32,128]{2,1,0:T(8,128)(2,1)S(1)}, u32[]{:S(2)}, u32[]{:S(2)}) %all-to-all-start.1) | async-done | bytes 262176 | tf_op jit(solution)/shard_map/all_to_all | solution.py:412
  50.1 4.0 %all-to-all-start.2 = ((bf16[32,16,1024]{2,1,0:T(8,128)(2,1)}), bf16[32,16,1024]{2,1,0:T(8,128)(2,1)S(1)}, u32[]{:S(2)}, u32[]{:S(2)}) async-start(bf16[32,16,1024]{2,1,0:T(8,128)(2,1)} %get-tuple-element.24), calls=%async_computation.2 | async-start | bytes 2097152 | tf_op jit(solution)/shard_map/all_to_all | solution.py:421
  54.1 1.6 %shard_map.89.a_ref = f32[88,128]{1,0:T(8,128)S(1)} custom-call(s32[32,128]{1,0:T(8,128)S(1)} %get-tuple-element.15.tiles_ref, bf16[32,32,128]{2,1,0:T(8,128)(2,1)S(1)} %all-to-all-done.1.sums_ref, f32[24,128]{1,0:T(8,128)S(1)} %get-tuple-element.22.scan_ref), custom_call_target="tpu_custom_call" | custom-call | bytes 6000000 | tf_op jit(solution)/shard_map/pallas_call | solution.py:423
  55.7 3.8 %collective-permute-start.2 = (f32[88,128]{1,0:T(8,128)S(1)}, f32[88,128]{1,0:T(8,128)S(1)}, u32[]{:S(2)}, u32[]{:S(2)}) collective-permute-start(f32[88,128]{1,0:T(8,128)S(1)} %shard_map.89.a_ref), channel_id=1, source_target_pairs={{0,96},{32,0},{64,32},{96,64},{1,97},{33,1},{65,33},{97,65},{2,98}... | collective-permute-start | bytes 135176 | tf_op jit(solution)/shard_map/ppermute | solution.py:360
  59.5 0.0 collective-permute-start.1
  59.5 0.7 collective-permute-start
  60.2 0.4 collective-permute-done.2.d_ref
  60.7 3.6 %collective-permute-done.1.c_ref = f32[88,128]{1,0:T(8,128)S(1)} collective-permute-done((f32[88,128]{1,0:T(8,128)S(1)}, f32[88,128]{1,0:T(8,128)S(1)}, u32[]{:S(2)}, u32[]{:S(2)}) %collective-permute-start.1) | collective-permute-done | bytes 45088 | tf_op jit(solution)/shard_map/ppermute | solution.py:360
  64.2 0.2 collective-permute-done.b_ref
  64.4 2.8 %collective-permute-start.5 = (bf16[64,128]{1,0:T(8,128)(2,1)S(1)}, bf16[64,128]{1,0:T(8,128)(2,1)S(1)}, u32[]{:S(2)}, u32[]{:S(2)}) collective-permute-start(bf16[64,128]{1,0:T(8,128)(2,1)S(1)} %get-tuple-element.26), channel_id=1, source_target_pairs={{0,24},{8,0},{16,8},{24,16},{1,25},{9,1},{17,9},{25,17},{2,26},{10... | collective-permute-start | bytes 49160 | tf_op jit(solution)/shard_map/ppermute | solution.py:360
  67.3 0.5 collective-permute-start.4
  67.7 0.6 collective-permute-start.3
  68.4 0.5 collective-permute-done.5
  68.8 2.6 %collective-permute-done.4 = bf16[64,128]{1,0:T(8,128)(2,1)S(1)} collective-permute-done((bf16[64,128]{1,0:T(8,128)(2,1)S(1)}, bf16[64,128]{1,0:T(8,128)(2,1)S(1)}, u32[]{:S(2)}, u32[]{:S(2)}) %collective-permute-start.4) | collective-permute-done | bytes 16416 | tf_op jit(solution)/shard_map/ppermute | solution.py:360
  71.4 0.2 collective-permute-done.3
  71.6 0.1 pad_maximum_fusion
  71.7 0.0 all-to-all-done.2.data_ref
  71.7 6.2 %collective-permute-start.6 = (f32[16,1,128]{2,1,0:T(1,128)S(1)}, f32[16,1,128]{2,1,0:T(1,128)S(1)}, u32[]{:S(2)}, u32[]{:S(2)}) collective-permute-start(f32[16,1,128]{2,1,0:T(1,128)S(1)} %constant_dynamic-slice_fusion), channel_id=1, source_target_pairs={{0,0},{1,16},{2,32},{3,48},{4,64},{5,80},{6,96},{7,112},{8,4},{9,2... | collective-permute-start | bytes 24584 | tf_op jit(solution)/shard_map/ppermute | solution.py:453
  77.9 0.1 pad_maximum_fusion.1
  78.0 7.3 %shard_map.91 = f32[1,16,32768]{2,1,0:T(8,128)} custom-call(s32[32,128]{1,0:T(8,128)S(1)} %get-tuple-element.15.tiles_ref, f32[256,128]{1,0:T(8,128)S(1)} %get-tuple-element.20.flags_ref, bf16[32,16,1024]{2,1,0:T(8,128)(2,1)S(1)} %all-to-all-done.2.data_ref, bf16[16,16,128]{2,1,0:T(8,128)(2,1)S(1)} %bitcast.34, bf16[16,8,129]{2,1,0:T(8,128)(2,1)S(1)} %bitcast.33), custom_call_target="tpu_custom_call" | custom-call | bytes 27000000 | tf_op jit(solution)/shard_map/pallas_call | solution.py:454
  85.3 0.0 collective-permute-done.6
  85.3 0.6 copy.16
  (19 shorter events, 0.3 us)
Async XLA Ops:
  6.7 8.8 %copy-start.2 = (f32[2,512]{1,0:T(2,128)S(1)}, f32[2,512]{1,0:T(2,128)}, u32[]{:S(2)}) copy-start(f32[2,512]{1,0:T(2,128)} %param.12) | copy-start | bytes 12292
  6.7 8.8 %copy-start.3 = (s32[512]{0:T(512)S(1)}, s32[512]{0:T(512)}, u32[]{:S(2)}) copy-start(s32[512]{0:T(512)} %param.13) | copy-start | bytes 6148
  6.7 13.7 %copy-start.4 = (bf16[1,512]{1,0:T(2,128)(2,1)S(1)}, bf16[1,512]{1,0:T(2,128)(2,1)}, u32[]{:S(2)}) copy-start(bf16[1,512]{1,0:T(2,128)(2,1)} %param.11) | copy-start | bytes 3076
  6.7 18.8 %copy-start.1 = (s32[1,32]{1,0:T(1,128)S(1)}, s32[1,32]{1,0:T(1,128)}, u32[]{:S(2)}) copy-start(s32[1,32]{1,0:T(1,128)} %bounds_ref.1) | copy-start | bytes 388
  6.8 26.4 %all-to-all-start = ((bf16[32,16,1152]{2,1,0:T(8,128)(2,1)}), bf16[32,16,1152]{2,1,0:T(8,128)(2,1)S(1)}, u32[]{:S(2)}, u32[]{:S(2)}) async-start(bf16[32,16,1152]{2,1,0:T(8,128)(2,1)} %shard_map.86), calls=%async_computation | async-start | bytes 2359296 | tf_op jit(solution)/shard_map/all_to_all | solution.py:392
  36.0 14.1 %all-to-all-start.1 = ((bf16[32,32,128]{2,1,0:T(8,128)(2,1)}), bf16[32,32,128]{2,1,0:T(8,128)(2,1)S(1)}, u32[]{:S(2)}, u32[]{:S(2)}) async-start(bf16[32,32,128]{2,1,0:T(8,128)(2,1)} %get-tuple-element.17), calls=%async_computation.1 | async-start | bytes 524288 | tf_op jit(solution)/shard_map/all_to_all | solution.py:412
  50.1 27.9 %copy-start = (bf16[1,16,8,129]{3,2,1,0:T(8,128)(2,1)S(1)}, bf16[1,16,8,129]{3,2,1,0:T(8,128)(2,1)}, u32[]{:S(2)}) copy-start(bf16[1,16,8,129]{3,2,1,0:T(8,128)(2,1)} %param.8) | copy-start | bytes 99076
  50.1 21.6 %all-to-all-start.2 = ((bf16[32,16,1024]{2,1,0:T(8,128)(2,1)}), bf16[32,16,1024]{2,1,0:T(8,128)(2,1)S(1)}, u32[]{:S(2)}, u32[]{:S(2)}) async-start(bf16[32,16,1024]{2,1,0:T(8,128)(2,1)} %get-tuple-element.24), calls=%async_computation.2 | async-start | bytes 2097152 | tf_op jit(solution)/shard_map/all_to_all | solution.py:421
  55.7 5.0 %collective-permute-start.2 = (f32[88,128]{1,0:T(8,128)S(1)}, f32[88,128]{1,0:T(8,128)S(1)}, u32[]{:S(2)}, u32[]{:S(2)}) collective-permute-start(f32[88,128]{1,0:T(8,128)S(1)} %shard_map.89.a_ref), channel_id=1, source_target_pairs={{0,96},{32,0},{64,32},{96,64},{1,97},{33,1},{65,33},{97,65},{2,98}... | collective-permute-start | bytes 135176 | tf_op jit(solution)/shard_map/ppermute | solution.py:360
  59.5 4.7 %collective-permute-start.1 = (f32[88,128]{1,0:T(8,128)S(1)}, f32[88,128]{1,0:T(8,128)S(1)}, u32[]{:S(2)}, u32[]{:S(2)}) collective-permute-start(f32[88,128]{1,0:T(8,128)S(1)} %shard_map.89.a_ref), channel_id=1, source_target_pairs={{0,64},{32,96},{64,0},{96,32},{1,65},{33,97},{65,1},{97,33},{2,66}... | collective-permute-start | bytes 135176 | tf_op jit(solution)/shard_map/ppermute | solution.py:360
  59.5 4.9 %collective-permute-start = (f32[88,128]{1,0:T(8,128)S(1)}, f32[88,128]{1,0:T(8,128)S(1)}, u32[]{:S(2)}, u32[]{:S(2)}) collective-permute-start(f32[88,128]{1,0:T(8,128)S(1)} %shard_map.89.a_ref), channel_id=1, source_target_pairs={{0,32},{32,64},{64,96},{96,0},{1,33},{33,65},{65,97},{97,1},{2,34}... | collective-permute-start | bytes 135176 | tf_op jit(solution)/shard_map/ppermute | solution.py:360
  64.4 4.4 %collective-permute-start.5 = (bf16[64,128]{1,0:T(8,128)(2,1)S(1)}, bf16[64,128]{1,0:T(8,128)(2,1)S(1)}, u32[]{:S(2)}, u32[]{:S(2)}) collective-permute-start(bf16[64,128]{1,0:T(8,128)(2,1)S(1)} %get-tuple-element.26), channel_id=1, source_target_pairs={{0,24},{8,0},{16,8},{24,16},{1,25},{9,1},{17,9},{25,17},{2,26},{10... | collective-permute-start | bytes 49160 | tf_op jit(solution)/shard_map/ppermute | solution.py:360
  67.3 4.2 %collective-permute-start.4 = (bf16[64,128]{1,0:T(8,128)(2,1)S(1)}, bf16[64,128]{1,0:T(8,128)(2,1)S(1)}, u32[]{:S(2)}, u32[]{:S(2)}) collective-permute-start(bf16[64,128]{1,0:T(8,128)(2,1)S(1)} %get-tuple-element.26), channel_id=1, source_target_pairs={{0,16},{8,24},{16,0},{24,8},{1,17},{9,25},{17,1},{25,9},{2,18},{10... | collective-permute-start | bytes 49160 | tf_op jit(solution)/shard_map/ppermute | solution.py:360
  67.7 3.9 %collective-permute-start.3 = (bf16[64,128]{1,0:T(8,128)(2,1)S(1)}, bf16[64,128]{1,0:T(8,128)(2,1)S(1)}, u32[]{:S(2)}, u32[]{:S(2)}) collective-permute-start(bf16[64,128]{1,0:T(8,128)(2,1)S(1)} %get-tuple-element.26), channel_id=1, source_target_pairs={{0,8},{8,16},{16,24},{24,0},{1,9},{9,17},{17,25},{25,1},{2,10},{10... | collective-permute-start | bytes 49160 | tf_op jit(solution)/shard_map/ppermute | solution.py:360
  71.7 13.6 %collective-permute-start.6 = (f32[16,1,128]{2,1,0:T(1,128)S(1)}, f32[16,1,128]{2,1,0:T(1,128)S(1)}, u32[]{:S(2)}, u32[]{:S(2)}) collective-permute-start(f32[16,1,128]{2,1,0:T(1,128)S(1)} %constant_dynamic-slice_fusion), channel_id=1, source_target_pairs={{0,0},{1,16},{2,32},{3,48},{4,64},{5,80},{6,96},{7,112},{8,4},{9,2... | collective-permute-start | bytes 24584 | tf_op jit(solution)/shard_map/ppermute | solution.py:453

commit v4 on v3

--- a/solution.py
+++ b/solution.py
@@ -63,6 +63,24 @@
             flops=0, bytes_accessed=micros * 3_000_000, transcendentals=0
         ),
     )
+
+
+def share_of(quad, group):
+    turn = (quad - 2 * (group & 1)) & 3
+    near = turn >> 1
+    return ((turn + 1) & 2) | (((group >> 2) ^ 1) ^ near), near
+
+
+def quad_of(share, group):
+    near = (share & 1) ^ ((group >> 2) ^ 1)
+    return (2 * near + (near ^ (share >> 1)) + 2 * (group & 1)) & 3
+
+
+def sent_row(obs, quad, group):
+    step = (obs - (group >> 1)) & 3
+    near = share_of(quad, group)[1]
+    code = near * ((2 - step) & 3) + (1 - near) * (step ^ (step >> 1))
+    return code ^ (2 * ((group >> 1) & 1))
 
 
 def lane_ids(shape):
@@ -204,7 +222,7 @@
         total = jnp.sum(weighted, axis=0) * flags[block : block + 1, :]
         for quad in range(QUADS):
             for group in range(GROUPS):
-                row = group * ROWS + quad * SHARE
+                row = group * ROWS + share_of(quad, group)[0] * SHARE
                 sums[quad * GROUPS + group, block * SHARE : (block + 1) * SHARE, :] = total[
                     row : row + SHARE, :
                 ]
@@ -231,23 +249,25 @@
     scan_ref[TILES:, :] = weight_ref[...]
 
 
-def bin_kernel(tiles_ref, sums_ref, scan_ref, out_ref, acc):
-    acc[...] = jnp.zeros_like(acc)
+def bin_kernel(tiles_ref, sums_ref, scan_ref, out_ref, *accs):
+    for acc in accs:
+        acc[...] = jnp.zeros_like(acc)
     upper = row_ids((2 * SHARE, TILE)) < SHARE
 
-    def add_slab(slab, carry):
-        received = sums_ref[slab].astype(jnp.float32)
-        for pair in range(SLAB_BLOCKS // 2):
-            part = received[pair * 2 * SHARE : (pair + 1) * 2 * SHARE, :]
-            even = tiles_ref[slab, 2 * pair]
-            acc[even] = acc[even] + jnp.where(upper, part, 0.0)
-            odd = tiles_ref[slab, 2 * pair + 1]
-            acc[odd] = acc[odd] + jnp.where(upper, 0.0, part)
+    def add_slabs(step, carry):
+        for inner in range(SLAB_BLOCKS):
+            pair = slice(inner // 2 * 2 * SHARE, (inner // 2 + 1) * 2 * SHARE)
+            for which, acc in enumerate(accs):
+                slab = step * len(accs) + which
+                part = sums_ref[slab].astype(jnp.float32)[pair, :]
+                part = jnp.where(upper, 0.0, part) if inner % 2 else jnp.where(upper, part, 0.0)
+                tile = tiles_ref[slab, inner]
+                acc[tile] = acc[tile] + part
         return carry
 
-    lax.fori_loop(0, SLABS, add_slab, 0)
+    lax.fori_loop(0, SLABS // len(accs), add_slabs, 0)
     for tile in range(TILES):
-        both = acc[tile]
+        both = sum(acc[tile] for acc in accs)
         out_ref[tile * SHARE : (tile + 1) * SHARE, :] = both[:SHARE, :] + both[SHARE:, :]
     out_ref[SUM_ROWS:, :] = scan_ref[...]
 
@@ -270,10 +290,28 @@
 
 
 def adjoint_kernel(
-    tiles_ref, flags_ref, data_ref, sky_ref, taps_ref, out_ref, sky, resid, same, after, out_buf, first, last, sems
+    tiles_ref,
+    flags_ref,
+    data_ref,
+    sky_ref,
+    taps_ref,
+    out_ref,
+    sky,
+    resid_a,
+    resid_b,
+    same_a,
+    same_b,
+    after_a,
+    after_b,
+    out_buf,
+    first,
+    last,
+    sems,
 ):
+    resid, same, after = (resid_a, resid_b), (same_a, same_b), (after_a, after_b)
+
     def out_copy(band):
-        part = pl.ds(start(band, BAND_BLOCKS * TILE), BAND_BLOCKS * TILE)
+        part = pl.ds(band * BAND_BLOCKS * TILE, BAND_BLOCKS * TILE)
         return pltpu.make_async_copy(out_buf.at[:, part], out_ref.at[0, :, part], sems.at[band])
 
     sky[...] = sky_ref[...].astype(jnp.float32)
@@ -286,49 +324,58 @@
     in_first = lanes >= rows
     on_diag = lanes == rows
     low = lane_ids((ROWS, TILE)) < HALF
-    after[:ROWS, :] = jnp.zeros((ROWS, TILE), jnp.float32)
+    zero = jnp.zeros((ROWS, TILE), jnp.float32)
+
+    def make_residual(band, index):
+        block = band * BAND_BLOCKS + index
+        slab, inner = block // SLAB_BLOCKS, block % SLAB_BLOCKS
+        value = data_ref[slab, :, inner * TILE : (inner + 1) * TILE].astype(jnp.float32)
+        value = flags_ref[block : block + 1, :] * (value - sky[tiles_ref[slab, inner]])
+        resid[band % 2][index * ROWS : (index + 1) * ROWS, :] = value
 
     def write_block(block, before, here):
-        out_buf[:, pl.ds(start(block, TILE), TILE)] = jnp.where(low, before, here)
-
-    def one_band(band, before):
-        for part in range(BAND_SLABS):
-            slab = band * BAND_SLABS + part
-            for inner in range(SLAB_BLOCKS):
-                block = slab * SLAB_BLOCKS + inner
-                value = data_ref[slab, :, inner * TILE : (inner + 1) * TILE].astype(jnp.float32)
-                value = flags_ref[pl.ds(block, 1), :] * (value - sky[tiles_ref[slab, inner]])
-                resid[pl.ds(start(block, ROWS), ROWS), :] = value
+        if block >= 0:
+            out_buf[:, block * TILE : (block + 1) * TILE] = jnp.where(low, before, here)
+
+    def join(band, index, before, spill):
+        place = slice(index * ROWS, (index + 1) * ROWS)
+        if index > 0:
+            spill = after[band % 2][(index - 1) * ROWS : index * ROWS, :]
+        here = pltpu.roll(same[band % 2][place, :] + spill, HALF, 1)
+        write_block(band * BAND_BLOCKS + index - 1, before, here)
+        return here
+
+    for index in range(BAND_BLOCKS):
+        make_residual(0, index)
+    before, spill, next_spill = zero, zero, zero
+    for band in range(BANDS + 1):
+        if band >= 2:
+            spill = next_spill
+        if 1 <= band < BANDS:
+            next_spill = after[(band - 1) % 2][(BAND_BLOCKS - 1) * ROWS :, :]
         for det in range(ROWS):
-            pair = det * BANDS + band
-            turned = circulant(first[pl.ds(pair, 1), :])
-            end = jnp.broadcast_to(last[pl.ds(pair, 1), :], (TILE, TILE))
-            upper = jnp.where(in_first, turned, 0.0)
-            lower = jnp.where(in_first, jnp.where(on_diag, end, 0.0), turned)
-            kernel = jnp.concatenate([upper, lower], axis=1).astype(jnp.bfloat16)
-            base = band * BAND_BLOCKS * ROWS + det
-            part = resid[pl.ds(base, BAND_BLOCKS, stride=ROWS), :].astype(jnp.bfloat16)
-            spread = jnp.dot(part, kernel, preferred_element_type=jnp.float32)
-            same[pl.ds(base, BAND_BLOCKS, stride=ROWS), :] = spread[:, :TILE]
-            after[pl.ds(base + ROWS, BAND_BLOCKS, stride=ROWS), :] = spread[:, TILE:]
-        for inner in range(BAND_BLOCKS):
-            block = band * BAND_BLOCKS + inner
-            place = pl.ds(start(block, ROWS), ROWS)
-            here = pltpu.roll(same[place, :] + after[place, :], HALF, 1)
-            if inner == 0:
-
-                @pl.when(band > 0)
-                def _():
-                    write_block(block - 1, before, here)
-                    out_copy(band - 1).start()
-
-            else:
-                write_block(block - 1, before, here)
-            before = here
-        return before
-
-    before = lax.fori_loop(0, BANDS, one_band, jnp.zeros((ROWS, TILE), jnp.float32))
-    write_block(BLOCKS - 1, before, pltpu.roll(after[BLOCKS * ROWS :, :], HALF, 1))
+            if band < BANDS:
+                pair = det * BANDS + band
+                turned = circulant(first[pair : pair + 1, :])
+                end = jnp.broadcast_to(last[pair : pair + 1, :], (TILE, TILE))
+                upper = jnp.where(in_first, turned, 0.0)
+                lower = jnp.where(in_first, jnp.where(on_diag, end, 0.0), turned)
+                kernel = jnp.concatenate([upper, lower], axis=1).astype(jnp.bfloat16)
+                part = resid[band % 2][pl.ds(det, BAND_BLOCKS, stride=ROWS), :]
+                spread = jnp.dot(
+                    part.astype(jnp.bfloat16), kernel, preferred_element_type=jnp.float32
+                )
+                same[band % 2][pl.ds(det, BAND_BLOCKS, stride=ROWS), :] = spread[:, :TILE]
+                after[band % 2][pl.ds(det, BAND_BLOCKS, stride=ROWS), :] = spread[:, TILE:]
+            for index in (2 * det, 2 * det + 1):
+                if band + 1 < BANDS:
+                    make_residual(band + 1, index)
+                if band > 0:
+                    before = join(band - 1, index, before, spill)
+        if band >= 2:
+            out_copy(band - 2).start()
+    final = after[(BANDS - 1) % 2][(BAND_BLOCKS - 1) * ROWS :, :]
+    write_block(BLOCKS - 1, before, pltpu.roll(final, HALF, 1))
     out_copy(BANDS - 1).start()
     for band in range(BANDS):
         out_copy(band).wait()
@@ -396,7 +443,7 @@
     weights = det_weights[0].astype(f32)
     lane_weights = jnp.broadcast_to(weights[:, None], (DET, TILE))
     row_weights = jnp.sum(weights.reshape(DET // TILE, TILE), axis=0)
-    own_rows = lax.dynamic_slice_in_dim(row_weights, group * ROWS + quad * SHARE, SHARE)
+    own_rows = lax.dynamic_slice_in_dim(row_weights, group * ROWS + share_of(quad, group)[0] * SHARE, SHARE)
     own_rows = jnp.broadcast_to(jnp.tile(own_rows, 2)[:, None], (2 * SHARE, TILE))
     cleaned, sums, tiles = call(
         clean_kernel,
@@ -425,7 +472,7 @@
         shape((SUM_ROWS + TILES + 2 * SHARE, TILE), f32),
         [smem(), vmem(), vmem()],
         vmem(),
-        [buffer((TILES, 2 * SHARE, TILE), f32)],
+        [buffer((TILES, 2 * SHARE, TILE), f32)] * 4,
     )(tiles, sums, scans)
     sky, sky_b = call(
         sky_kernel,
@@ -436,15 +483,15 @@
     )(part, *exchange(part, "obs"))
     held = jnp.stack([sky_b] + exchange(sky_b, "q")).reshape(QUADS, TILES, SHARE, TILE)
     held = [
-        lax.dynamic_index_in_dim(held, lax.rem(quad - src + QUADS, QUADS), 0, keepdims=False)
-        for src in range(QUADS)
+        lax.dynamic_index_in_dim(held, (quad - quad_of(share, group)) & 3, 0, keepdims=False)
+        for share in range(QUADS)
     ]
     sky_rows = jnp.stack(held, axis=1).reshape(TILES, ROWS, TILE)
     sky_row = lax.dynamic_slice_in_dim(
-        sky.reshape(TILES, SHARE, TILE), lax.axis_index("obs"), 1, 1
+        sky.reshape(TILES, SHARE, TILE), sent_row(lax.axis_index("obs"), quad, group), 1, 1
     )
     moves = [
-        ((o * QUADS + q) * GROUPS + g, g * ROWS + q * SHARE + o)
+        ((o * QUADS + q) * GROUPS + g, g * ROWS + share_of(q, g)[0] * SHARE + sent_row(o, q, g))
         for o in range(OBS)
         for q in range(QUADS)
         for g in range(GROUPS)
@@ -458,9 +505,7 @@
         hbm(),
         [
             buffer((TILES, ROWS, TILE), f32),
-            buffer((BLOCKS * ROWS, TILE), f32),
-            buffer((BLOCKS * ROWS, TILE), f32),
-            buffer(((BLOCKS + 1) * ROWS, TILE), f32),
+            *[buffer((BAND_BLOCKS * ROWS, TILE), f32)] * 6,
             buffer((ROWS, SAMP), f32),
             buffer((ROWS * BANDS, TILE), f32),
             buffer((ROWS * BANDS, TILE), f32),

time: 86.8 us -> 83.4 us (0.961)
  starting transfers between devices: 32.4 us -> 30.1 us
  Pallas kernels: 19.7 us -> 18.2 us
    ppermute x1, starting transfers between devices: 6.21 us -> 3.88 us  [local(): sky_own = lax.ppermute(sky_row, ALL_AXES, moves)]
    pallas_call x1, Pallas kernels: 7.27 us -> 6.16 us  [local(): call(adjoint_kernel, shape((1, ROWS, SAMP), f32), [smem(), vmem(), vmem()...]
  transfers between devices with their start and end apart: 10 -> 10, of which waited for: 8 -> 7; matrix products, arithmetic and copies ran while one was open for 13% -> 13% of each run, Pallas kernels for 13% -> 11%
where the time goes in v4:
time: 83.4 us; the launch traced here: 82.2 us
  starting transfers between devices  30.1 us (36%)
  waiting for transfers between devices  21.5 us (26%)
  Pallas kernels  18.2 us (22%)
  other arithmetic  9.68 us (12%)
  local copies, waits for them, and re-layouts  1.29 us (2%)
  between operations  0.95 us (1%)
    all_to_all x1, starting transfers between devices, local(): lax.all_to_all(filtered, SLAB_AXES, split_axis=0, concat_axis=0, tiled=True)  8.73 us
    ppermute x6, starting transfers between devices, exchange(): lax.ppermute(value, axis, [(src, (src + step) % size) for src in range(si...  8.45 us
    ppermute x6, waiting for transfers between devices, exchange(): lax.ppermute(value, axis, [(src, (src + step) % size) for src in range(si...  7.62 us
    all_to_all x1, waiting for transfers between devices, local(): lax.all_to_all(filtered, SLAB_AXES, split_axis=0, concat_axis=0, tiled=True)  7.17 us
    all_to_all x1, waiting for transfers between devices, local(): lax.all_to_all(sums, SLAB_AXES, split_axis=0, concat_axis=0, tiled=True)  6.7 us
    pallas_call x1, Pallas kernels, local(): call(adjoint_kernel, shape((1, ROWS, SAMP), f32), [smem(), vmem(), vmem()...  6.16 us
    pallas_call x1, Pallas kernels, local(): call(forward_kernel, shape((SLABS, ROWS, SLAB_LEN + TILE), bf16), [hbm(),...  6.07 us
    all_to_all x1, starting transfers between devices, local(): lax.all_to_all(sums, SLAB_AXES, split_axis=0, concat_axis=0, tiled=True)  5.08 us
  transfers between devices with their start and end apart: 10, of which 7 were waited for; matrix products, arithmetic and copies ran while one was open for 13% of the time, Pallas kernels for 11%

profile of v4, /device:TPU:1, one launch (start us, length us, event | category | flops | bytes accessed | tf_op | source)
XLA Modules:
  0.0 82.2 jit_solution(6111175081952768075)
XLA Ops:
  0.6 6.1 %shard_map.86 = bf16[32,16,1152]{2,1,0:T(8,128)(2,1)} custom-call(bf16[1,16,32768]{2,1,0:T(8,128)(2,1)} %x_ref.1, bf16[16,8,129]{2,1,0:T(8,128)(2,1)} %bitcast.32, s32[1,8]{1,0:T(1,128)} %tiles_ref.1), custom_call_target="tpu_custom_call" | custom-call | bytes 21000000 | tf_op jit(solution)/shard_map/pallas_call | solution.py:420
  6.7 0.0 copy-start.2
  6.7 0.0 copy-start.3
  6.7 0.0 copy-start.4
  6.7 0.0 copy-start.1
  6.8 8.7 %all-to-all-start = ((bf16[32,16,1152]{2,1,0:T(8,128)(2,1)}), bf16[32,16,1152]{2,1,0:T(8,128)(2,1)S(1)}, u32[]{:S(2)}, u32[]{:S(2)}) async-start(bf16[32,16,1152]{2,1,0:T(8,128)(2,1)} %shard_map.86), calls=%async_computation | async-start | bytes 2359296 | tf_op jit(solution)/shard_map/all_to_all | solution.py:439
  15.5 0.0 copy-done.2
  15.5 0.0 copy-done.3
  15.6 0.1 fusion.5
  15.8 0.1 copy.14
  15.9 4.4 %cholesky.17 = f32[48,48]{1,0:T(8,128)S(1)} custom-call(f32[48,48]{1,0:T(8,128)S(1)} %fusion.3), custom_call_target="Cholesky" | custom-call | tf_op jit(solution)/shard_map/jit(cholesky)/cholesky | solution.py:396
  20.3 0.1 copy.12
  20.4 0.6 compare_reduce_fusion
  21.1 0.7 fusion
  21.7 3.7 %custom-call.6 = f32[1,48,48]{1,2,0:T(8,128)S(1)} custom-call(f32[1,48,48]{2,1,0:T(8,128)S(1)} %fusion), custom_call_target="InvertDiagBlocksLowerTriangular" | custom-call | tf_op jit(solution)/shard_map/triangular_solve | solution.py:397
  25.4 0.1 maximum_bitcast_fusion.basis_t_ref
  25.6 0.2 fusion.1
  25.8 0.2 fusion.6.inverse_ref
  26.0 7.2 %all-to-all-done.data_ref = bf16[32,16,1152]{2,1,0:T(8,128)(2,1)S(1)} async-done(((bf16[32,16,1152]{2,1,0:T(8,128)(2,1)}), bf16[32,16,1152]{2,1,0:T(8,128)(2,1)S(1)}, u32[]{:S(2)}, u32[]{:S(2)}) %all-to-all-start) | async-done | bytes 1179680 | tf_op jit(solution)/shard_map/all_to_all | solution.py:439
  33.2 0.1 broadcast_in_dim.8.weight_ref
  33.3 2.7 %shard_map.87 = (bf16[32,16,1024]{2,1,0:T(8,128)(2,1)}, bf16[32,32,128]{2,1,0:T(8,128)(2,1)}, s32[32,128]{1,0:T(8,128)S(1)}) custom-call(s32[1,32]{1,0:T(1,128)S(1)} %broadcast_subtract_fusion.bounds_ref, bf16[32,16,1152]{2,1,0:T(8,128)(2,1)S(1)} %all-to-all-done.data_ref, bf16[48,512]{1,0:T(8,128)(2,1)S(1)} %convert_element_type.36.basis_ref, ...), custom_call_target="tpu_custom_call" | custom-call | bytes 6000000 | tf_op jit(solution)/shard_map/pallas_call | solution.py:448
  36.0 5.1 %all-to-all-start.1 = ((bf16[32,32,128]{2,1,0:T(8,128)(2,1)}), bf16[32,32,128]{2,1,0:T(8,128)(2,1)S(1)}, u32[]{:S(2)}, u32[]{:S(2)}) async-start(bf16[32,32,128]{2,1,0:T(8,128)(2,1)} %get-tuple-element.17), calls=%async_computation.1 | async-start | bytes 524288 | tf_op jit(solution)/shard_map/all_to_all | solution.py:459
  41.1 0.1 dynamic_slice.19
  41.2 0.1 broadcast_in_dim.9
  41.3 0.1 broadcast_in_dim.10.weight_ref
  41.4 2.0 %shard_map.88 = (f32[256,128]{1,0:T(8,128)S(1)}, f32[24,128]{1,0:T(8,128)S(1)}) custom-call(s32[1,32]{1,0:T(1,128)S(1)} %copy-done.1, s32[32,128]{1,0:T(8,128)S(1)} %get-tuple-element.15.tiles_ref, f32[8,128]{1,0:T(8,128)S(1)} %broadcast_in_dim.10.weight_ref), custom_call_target="tpu_custom_call" | custom-call | bytes 6000000 | tf_op jit(solution)/shard_map/pallas_call | solution.py:460
  43.4 6.7 %all-to-all-done.1.sums_ref = bf16[32,32,128]{2,1,0:T(8,128)(2,1)S(1)} async-done(((bf16[32,32,128]{2,1,0:T(8,128)(2,1)}), bf16[32,32,128]{2,1,0:T(8,128)(2,1)S(1)}, u32[]{:S(2)}, u32[]{:S(2)}) %all-to-all-start.1) | async-done | bytes 262176 | tf_op jit(solution)/shard_map/all_to_all | solution.py:459
  50.1 4.0 %all-to-all-start.2 = ((bf16[32,16,1024]{2,1,0:T(8,128)(2,1)}), bf16[32,16,1024]{2,1,0:T(8,128)(2,1)S(1)}, u32[]{:S(2)}, u32[]{:S(2)}) async-start(bf16[32,16,1024]{2,1,0:T(8,128)(2,1)} %get-tuple-element.24), calls=%async_computation.2 | async-start | bytes 2097152 | tf_op jit(solution)/shard_map/all_to_all | solution.py:468
  54.1 1.2 %shard_map.89.a_ref = f32[88,128]{1,0:T(8,128)S(1)} custom-call(s32[32,128]{1,0:T(8,128)S(1)} %get-tuple-element.15.tiles_ref, bf16[32,32,128]{2,1,0:T(8,128)(2,1)S(1)} %all-to-all-done.1.sums_ref, f32[24,128]{1,0:T(8,128)S(1)} %get-tuple-element.22.scan_ref), custom_call_target="tpu_custom_call" | custom-call | bytes 6000000 | tf_op jit(solution)/shard_map/pallas_call | solution.py:470
  55.3 3.8 %collective-permute-start.2 = (f32[88,128]{1,0:T(8,128)S(1)}, f32[88,128]{1,0:T(8,128)S(1)}, u32[]{:S(2)}, u32[]{:S(2)}) collective-permute-start(f32[88,128]{1,0:T(8,128)S(1)} %shard_map.89.a_ref), channel_id=1, source_target_pairs={{0,96},{32,0},{64,32},{96,64},{1,97},{33,1},{65,33},{97,65},{2,98}... | collective-permute-start | bytes 135176 | tf_op jit(solution)/shard_map/ppermute | solution.py:407
  59.1 0.0 collective-permute-start.1
  59.1 0.7 collective-permute-start
  59.8 0.4 collective-permute-done.2.d_ref
  60.3 3.6 %collective-permute-done.1.c_ref = f32[88,128]{1,0:T(8,128)S(1)} collective-permute-done((f32[88,128]{1,0:T(8,128)S(1)}, f32[88,128]{1,0:T(8,128)S(1)}, u32[]{:S(2)}, u32[]{:S(2)}) %collective-permute-start.1) | collective-permute-done | bytes 45088 | tf_op jit(solution)/shard_map/ppermute | solution.py:407
  63.8 0.2 collective-permute-done.b_ref
  64.0 2.8 %collective-permute-start.5 = (bf16[64,128]{1,0:T(8,128)(2,1)S(1)}, bf16[64,128]{1,0:T(8,128)(2,1)S(1)}, u32[]{:S(2)}, u32[]{:S(2)}) collective-permute-start(bf16[64,128]{1,0:T(8,128)(2,1)S(1)} %get-tuple-element.26), channel_id=1, source_target_pairs={{0,24},{8,0},{16,8},{24,16},{1,25},{9,1},{17,9},{25,17},{2,26},{10... | collective-permute-start | bytes 49160 | tf_op jit(solution)/shard_map/ppermute | solution.py:407
  66.9 0.5 collective-permute-start.4
  67.3 0.6 collective-permute-start.3
  68.0 1.1 %collective-permute-done.5 = bf16[64,128]{1,0:T(8,128)(2,1)S(1)} collective-permute-done((bf16[64,128]{1,0:T(8,128)(2,1)S(1)}, bf16[64,128]{1,0:T(8,128)(2,1)S(1)}, u32[]{:S(2)}, u32[]{:S(2)}) %collective-permute-start.5) | collective-permute-done | bytes 16416 | tf_op jit(solution)/shard_map/ppermute | solution.py:407
  69.1 2.3 %collective-permute-done.4 = bf16[64,128]{1,0:T(8,128)(2,1)S(1)} collective-permute-done((bf16[64,128]{1,0:T(8,128)(2,1)S(1)}, bf16[64,128]{1,0:T(8,128)(2,1)S(1)}, u32[]{:S(2)}, u32[]{:S(2)}) %collective-permute-start.4) | collective-permute-done | bytes 16416 | tf_op jit(solution)/shard_map/ppermute | solution.py:407
  71.4 0.0 collective-permute-done.3
  71.4 0.1 pad_maximum_fusion
  71.5 0.0 all-to-all-done.2.data_ref
  71.5 3.9 %collective-permute-start.6 = (f32[16,1,128]{2,1,0:T(1,128)S(1)}, f32[16,1,128]{2,1,0:T(1,128)S(1)}, u32[]{:S(2)}, u32[]{:S(2)}) collective-permute-start(f32[16,1,128]{2,1,0:T(1,128)S(1)} %constant_dynamic-slice_fusion), channel_id=1, source_target_pairs={{0,4},{1,26},{2,36},{3,57},{4,67},{5,92},{6,99},{7,127},{8,12},{9,... | collective-permute-start | bytes 24584 | tf_op jit(solution)/shard_map/ppermute | solution.py:500
  75.4 0.1 pad_maximum_fusion.1
  75.5 6.2 %shard_map.91 = f32[1,16,32768]{2,1,0:T(8,128)} custom-call(s32[32,128]{1,0:T(8,128)S(1)} %get-tuple-element.15.tiles_ref, f32[256,128]{1,0:T(8,128)S(1)} %get-tuple-element.20.flags_ref, bf16[32,16,1024]{2,1,0:T(8,128)(2,1)S(1)} %all-to-all-done.2.data_ref, bf16[16,16,128]{2,1,0:T(8,128)(2,1)S(1)} %bitcast.34, bf16[16,8,129]{2,1,0:T(8,128)(2,1)S(1)} %bitcast.33), custom_call_target="tpu_custom_call" | custom-call | bytes 27000000 | tf_op jit(solution)/shard_map/pallas_call | solution.py:501
  81.6 0.0 collective-permute-done.6
  81.6 0.6 copy.16
  (19 shorter events, 0.3 us)
Async XLA Ops:
  6.7 8.8 %copy-start.2 = (f32[2,512]{1,0:T(2,128)S(1)}, f32[2,512]{1,0:T(2,128)}, u32[]{:S(2)}) copy-start(f32[2,512]{1,0:T(2,128)} %param.12) | copy-start | bytes 12292
  6.7 8.8 %copy-start.3 = (s32[512]{0:T(512)S(1)}, s32[512]{0:T(512)}, u32[]{:S(2)}) copy-start(s32[512]{0:T(512)} %param.13) | copy-start | bytes 6148
  6.7 13.7 %copy-start.4 = (bf16[1,512]{1,0:T(2,128)(2,1)S(1)}, bf16[1,512]{1,0:T(2,128)(2,1)}, u32[]{:S(2)}) copy-start(bf16[1,512]{1,0:T(2,128)(2,1)} %param.11) | copy-start | bytes 3076
  6.7 18.8 %copy-start.1 = (s32[1,32]{1,0:T(1,128)S(1)}, s32[1,32]{1,0:T(1,128)}, u32[]{:S(2)}) copy-start(s32[1,32]{1,0:T(1,128)} %bounds_ref.1) | copy-start | bytes 388
  6.8 26.4 %all-to-all-start = ((bf16[32,16,1152]{2,1,0:T(8,128)(2,1)}), bf16[32,16,1152]{2,1,0:T(8,128)(2,1)S(1)}, u32[]{:S(2)}, u32[]{:S(2)}) async-start(bf16[32,16,1152]{2,1,0:T(8,128)(2,1)} %shard_map.86), calls=%async_computation | async-start | bytes 2359296 | tf_op jit(solution)/shard_map/all_to_all | solution.py:439
  36.0 14.1 %all-to-all-start.1 = ((bf16[32,32,128]{2,1,0:T(8,128)(2,1)}), bf16[32,32,128]{2,1,0:T(8,128)(2,1)S(1)}, u32[]{:S(2)}, u32[]{:S(2)}) async-start(bf16[32,32,128]{2,1,0:T(8,128)(2,1)} %get-tuple-element.17), calls=%async_computation.1 | async-start | bytes 524288 | tf_op jit(solution)/shard_map/all_to_all | solution.py:459
  50.1 25.3 %copy-start = (bf16[1,16,8,129]{3,2,1,0:T(8,128)(2,1)S(1)}, bf16[1,16,8,129]{3,2,1,0:T(8,128)(2,1)}, u32[]{:S(2)}) copy-start(bf16[1,16,8,129]{3,2,1,0:T(8,128)(2,1)} %param.8) | copy-start | bytes 99076
  50.1 21.4 %all-to-all-start.2 = ((bf16[32,16,1024]{2,1,0:T(8,128)(2,1)}), bf16[32,16,1024]{2,1,0:T(8,128)(2,1)S(1)}, u32[]{:S(2)}, u32[]{:S(2)}) async-start(bf16[32,16,1024]{2,1,0:T(8,128)(2,1)} %get-tuple-element.24), calls=%async_computation.2 | async-start | bytes 2097152 | tf_op jit(solution)/shard_map/all_to_all | solution.py:468
  55.3 5.0 %collective-permute-start.2 = (f32[88,128]{1,0:T(8,128)S(1)}, f32[88,128]{1,0:T(8,128)S(1)}, u32[]{:S(2)}, u32[]{:S(2)}) collective-permute-start(f32[88,128]{1,0:T(8,128)S(1)} %shard_map.89.a_ref), channel_id=1, source_target_pairs={{0,96},{32,0},{64,32},{96,64},{1,97},{33,1},{65,33},{97,65},{2,98}... | collective-permute-start | bytes 135176 | tf_op jit(solution)/shard_map/ppermute | solution.py:407
  59.1 4.7 %collective-permute-start.1 = (f32[88,128]{1,0:T(8,128)S(1)}, f32[88,128]{1,0:T(8,128)S(1)}, u32[]{:S(2)}, u32[]{:S(2)}) collective-permute-start(f32[88,128]{1,0:T(8,128)S(1)} %shard_map.89.a_ref), channel_id=1, source_target_pairs={{0,64},{32,96},{64,0},{96,32},{1,65},{33,97},{65,1},{97,33},{2,66}... | collective-permute-start | bytes 135176 | tf_op jit(solution)/shard_map/ppermute | solution.py:407
  59.1 4.9 %collective-permute-start = (f32[88,128]{1,0:T(8,128)S(1)}, f32[88,128]{1,0:T(8,128)S(1)}, u32[]{:S(2)}, u32[]{:S(2)}) collective-permute-start(f32[88,128]{1,0:T(8,128)S(1)} %shard_map.89.a_ref), channel_id=1, source_target_pairs={{0,32},{32,64},{64,96},{96,0},{1,33},{33,65},{65,97},{97,1},{2,34}... | collective-permute-start | bytes 135176 | tf_op jit(solution)/shard_map/ppermute | solution.py:407
  64.0 5.0 %collective-permute-start.5 = (bf16[64,128]{1,0:T(8,128)(2,1)S(1)}, bf16[64,128]{1,0:T(8,128)(2,1)S(1)}, u32[]{:S(2)}, u32[]{:S(2)}) collective-permute-start(bf16[64,128]{1,0:T(8,128)(2,1)S(1)} %get-tuple-element.26), channel_id=1, source_target_pairs={{0,24},{8,0},{16,8},{24,16},{1,25},{9,1},{17,9},{25,17},{2,26},{10... | collective-permute-start | bytes 49160 | tf_op jit(solution)/shard_map/ppermute | solution.py:407
  66.9 4.5 %collective-permute-start.4 = (bf16[64,128]{1,0:T(8,128)(2,1)S(1)}, bf16[64,128]{1,0:T(8,128)(2,1)S(1)}, u32[]{:S(2)}, u32[]{:S(2)}) collective-permute-start(bf16[64,128]{1,0:T(8,128)(2,1)S(1)} %get-tuple-element.26), channel_id=1, source_target_pairs={{0,16},{8,24},{16,0},{24,8},{1,17},{9,25},{17,1},{25,9},{2,18},{10... | collective-permute-start | bytes 49160 | tf_op jit(solution)/shard_map/ppermute | solution.py:407
  67.3 4.1 %collective-permute-start.3 = (bf16[64,128]{1,0:T(8,128)(2,1)S(1)}, bf16[64,128]{1,0:T(8,128)(2,1)S(1)}, u32[]{:S(2)}, u32[]{:S(2)}) collective-permute-start(bf16[64,128]{1,0:T(8,128)(2,1)S(1)} %get-tuple-element.26), channel_id=1, source_target_pairs={{0,8},{8,16},{16,24},{24,0},{1,9},{9,17},{17,25},{25,1},{2,10},{10... | collective-permute-start | bytes 49160 | tf_op jit(solution)/shard_map/ppermute | solution.py:407
  71.5 10.1 %collective-permute-start.6 = (f32[16,1,128]{2,1,0:T(1,128)S(1)}, f32[16,1,128]{2,1,0:T(1,128)S(1)}, u32[]{:S(2)}, u32[]{:S(2)}) collective-permute-start(f32[16,1,128]{2,1,0:T(1,128)S(1)} %constant_dynamic-slice_fusion), channel_id=1, source_target_pairs={{0,4},{1,26},{2,36},{3,57},{4,67},{5,92},{6,99},{7,127},{8,12},{9,... | collective-permute-start | bytes 24584 | tf_op jit(solution)/shard_map/ppermute | solution.py:500

commit v5 on v4

--- a/solution.py
+++ b/solution.py
@@ -100,22 +100,38 @@
 
 
 def forward_kernel(
-    x_ref, taps_ref, tiles_ref, y_ref, x_buf, taps_buf, shifted, summed, y_buf, first, last, tiles, sems
+    x_ref,
+    taps_ref,
+    tiles_ref,
+    y_ref,
+    x_buf,
+    taps_buf,
+    shifted_a,
+    shifted_b,
+    summed_a,
+    summed_b,
+    y_buf,
+    first,
+    last,
+    tiles,
+    sems,
 ):
-    taps_copy = pltpu.make_async_copy(taps_ref, taps_buf, sems.at[0, BANDS])
-    taps_copy.start()
-    tiles_copy = pltpu.make_async_copy(tiles_ref, tiles, sems.at[1, BANDS])
-    tiles_copy.start()
+    shifted, summed = (shifted_a, shifted_b), (summed_a, summed_b)
 
     def x_copy(band):
-        part = pl.ds(start(band, BAND_BLOCKS * TILE), BAND_BLOCKS * TILE)
+        part = pl.ds(band * BAND_BLOCKS * TILE, BAND_BLOCKS * TILE)
         return pltpu.make_async_copy(x_ref.at[0, :, part], x_buf.at[:, part], sems.at[0, band])
 
     def y_copy(band):
         part = pl.ds(band * BAND_SLABS, BAND_SLABS)
         return pltpu.make_async_copy(y_buf.at[part], y_ref.at[part], sems.at[1, band])
 
-    for band in range(BANDS):
+    taps_copy = pltpu.make_async_copy(taps_ref, taps_buf, sems.at[0, BANDS])
+    tiles_copy = pltpu.make_async_copy(tiles_ref, tiles, sems.at[1, BANDS])
+    taps_copy.start()
+    x_copy(0).start()
+    tiles_copy.start()
+    for band in range(1, BANDS):
         x_copy(band).start()
     low = lane_ids((ROWS, TILE)) < HALF
     rows, lanes = row_ids((TILE, TILE)), lane_ids((TILE, TILE))
@@ -129,62 +145,63 @@
     last[...] = jnp.broadcast_to(taps[:, :, TILE:], (ROWS, BANDS, TILE)).reshape(
         ROWS * BANDS, TILE
     )
-
-    def rolled(block):
-        part = x_buf[:, pl.ds(start(block, TILE), TILE)]
-        return pltpu.roll(part.astype(jnp.float32), HALF, 1)
-
     tiles_copy.wait()
     lane = lane_ids((ROWS, TILE))
     meta = jnp.zeros((ROWS, TILE), jnp.int32)
     for block in range(SLAB_BLOCKS):
         meta = jnp.where(lane == block, tiles[0, block], meta)
     meta = meta.astype(jnp.float32).astype(jnp.bfloat16)
+
+    def rolled(block):
+        if not 0 <= block < BLOCKS:
+            return jnp.zeros((ROWS, TILE), jnp.float32)
+        part = x_buf[:, block * TILE : (block + 1) * TILE]
+        return pltpu.roll(part.astype(jnp.float32), HALF, 1)
+
+    def shift(band, index, before):
+        here = rolled(band * BAND_BLOCKS + index)
+        place = slice(index * ROWS, (index + 1) * ROWS)
+        shifted[band % 2][place, :] = jnp.where(low, before, here)
+        return here
+
+    def write(band, index):
+        slab, inner = band * BAND_SLABS + index // SLAB_BLOCKS, index % SLAB_BLOCKS
+        part = summed[band % 2][index * ROWS : (index + 1) * ROWS, :]
+        y_buf[slab, :, inner * TILE : (inner + 1) * TILE] = part.astype(jnp.bfloat16)
+        if inner == 0:
+            y_buf[slab, :, SLAB_LEN:] = meta
+
     x_copy(0).wait()
-    opening = rolled(0)
-    shifted[:ROWS, :] = jnp.where(low, 0.0, opening)
-
-    def one_band(band, before):
-        @pl.when(band < BANDS - 1)
-        def _():
+    before = rolled(-1)
+    for index in range(BAND_BLOCKS):
+        before = shift(0, index, before)
+    for band in range(BANDS):
+        if band + 1 < BANDS:
             x_copy(band + 1).wait()
-
-        for inner in range(1, BAND_BLOCKS + 1):
-            block = band * BAND_BLOCKS + inner
-            if inner == BAND_BLOCKS:
-                here = jnp.where(
-                    band < BANDS - 1, rolled(jnp.minimum(block, BLOCKS - 1)), 0.0
-                )
-            else:
-                here = rolled(block)
-            shifted[pl.ds(start(block, ROWS), ROWS), :] = jnp.where(low, before, here)
-            before = here
+        shift(band, BAND_BLOCKS, before)
         for det in range(ROWS):
             pair = det * BANDS + band
-            turned = circulant(first[pl.ds(pair, 1), :])
-            end = jnp.broadcast_to(last[pl.ds(pair, 1), :], (TILE, TILE))
+            turned = circulant(first[pair : pair + 1, :])
+            end = jnp.broadcast_to(last[pair : pair + 1, :], (TILE, TILE))
             upper = jnp.where(in_first, turned, 0.0)
             lower = jnp.where(in_first, jnp.where(on_diag, end, 0.0), turned)
             kernel = jnp.concatenate([upper, lower], axis=0).astype(jnp.bfloat16)
-            base = band * BAND_BLOCKS * ROWS + det
-            one = shifted[pl.ds(base, BAND_BLOCKS, stride=ROWS), :]
-            two = shifted[pl.ds(base + ROWS, BAND_BLOCKS, stride=ROWS), :]
+            one = shifted[band % 2][pl.ds(det, BAND_BLOCKS, stride=ROWS), :]
+            two = shifted[band % 2][pl.ds(det + ROWS, BAND_BLOCKS, stride=ROWS), :]
             window = jnp.concatenate([one, two], axis=1).astype(jnp.bfloat16)
-            summed[pl.ds(base, BAND_BLOCKS, stride=ROWS), :] = jnp.dot(
+            summed[band % 2][pl.ds(det, BAND_BLOCKS, stride=ROWS), :] = jnp.dot(
                 window, kernel, preferred_element_type=jnp.float32
             )
-        for part in range(BAND_SLABS):
-            slab = band * BAND_SLABS + part
-            for inner in range(SLAB_BLOCKS):
-                block = slab * SLAB_BLOCKS + inner
-                y_buf[slab, :, inner * TILE : (inner + 1) * TILE] = summed[
-                    pl.ds(start(block, ROWS), ROWS), :
-                ].astype(jnp.bfloat16)
-            y_buf[slab, :, SLAB_LEN:] = meta
-        y_copy(band).start()
-        return before
-
-    lax.fori_loop(0, BANDS, one_band, opening)
+            for index in (2 * det, 2 * det + 1):
+                if band + 1 < BANDS:
+                    before = shift(band + 1, index, before)
+                if band > 0:
+                    write(band - 1, index)
+        if band > 0:
+            y_copy(band - 1).start()
+    for index in range(BAND_BLOCKS):
+        write(BANDS - 1, index)
+    y_copy(BANDS - 1).start()
     for band in range(BANDS):
         y_copy(band).wait()
 
@@ -197,8 +214,13 @@
     return (passed & 1).astype(jnp.float32)
 
 
-def clean_kernel(
-    bounds_ref, data_ref, basis_ref, basis_t_ref, inverse_ref, weight_ref, out_ref, sums_ref, tiles_ref, sums
+def fit(data, basis_t, both):
+    fitted = jnp.dot(basis_t, both, preferred_element_type=jnp.float32)
+    return (data.astype(jnp.float32) - fitted).astype(jnp.bfloat16)
+
+
+def sums_kernel(
+    bounds_ref, data_ref, basis_ref, basis_t_ref, inverse_ref, weight_ref, both_ref, sums_ref, tiles_ref, sums
 ):
     data = data_ref[:, :, :SLAB_LEN].reshape(DET, SLAB_LEN)
     tiles_ref[...] = data_ref[:, :, SLAB_LEN:].astype(jnp.float32)[:, 0, :].astype(jnp.int32)
@@ -212,9 +234,8 @@
     high = coef.astype(jnp.bfloat16)
     rest = (coef - high.astype(jnp.float32)).astype(jnp.bfloat16)
     both = jnp.concatenate([high, rest], axis=0)
-    fitted = jnp.dot(basis_t_ref[...], both, preferred_element_type=jnp.float32)
-    cleaned = (data.astype(jnp.float32) - fitted).astype(jnp.bfloat16)
-    out_ref[...] = cleaned.reshape(out_ref.shape)
+    both_ref[...] = both
+    cleaned = fit(data, basis_t_ref[...], both)
     flags = count_flags(bounds_ref, SLAB_BLOCKS, 0)
     for block in range(SLAB_BLOCKS):
         part = cleaned[:, block * TILE : (block + 1) * TILE].astype(jnp.float32)
@@ -227,6 +248,11 @@
                     row : row + SHARE, :
                 ]
     sums_ref[...] = sums[...].astype(jnp.bfloat16)
+
+
+def clean_kernel(data_ref, basis_t_ref, both_ref, out_ref):
+    data = data_ref[:, :, :SLAB_LEN].reshape(DET, SLAB_LEN)
+    out_ref[...] = fit(data, basis_t_ref[...], both_ref[...]).reshape(out_ref.shape)
 
 
 def scan_kernel(bounds_ref, tiles_ref, weight_ref, flags_ref, scan_ref, acc):
@@ -425,8 +451,8 @@
         [
             buffer((ROWS, SAMP), bf16),
             buffer((ROWS, BANDS, TAPS), bf16),
-            buffer(((BLOCKS + 1) * ROWS, TILE), f32),
-            buffer((BLOCKS * ROWS, TILE), f32),
+            *[buffer(((BAND_BLOCKS + 1) * ROWS, TILE), f32)] * 2,
+            *[buffer((BAND_BLOCKS * ROWS, TILE), f32)] * 2,
             buffer((SLABS, ROWS, SLAB_LEN + TILE), bf16),
             buffer((ROWS * BANDS, TILE), f32),
             buffer((ROWS * BANDS, TILE), f32),
@@ -445,10 +471,10 @@
     row_weights = jnp.sum(weights.reshape(DET // TILE, TILE), axis=0)
     own_rows = lax.dynamic_slice_in_dim(row_weights, group * ROWS + share_of(quad, group)[0] * SHARE, SHARE)
     own_rows = jnp.broadcast_to(jnp.tile(own_rows, 2)[:, None], (2 * SHARE, TILE))
-    cleaned, sums, tiles = call(
-        clean_kernel,
+    both, sums, tiles = call(
+        sums_kernel,
         (
-            shape((SLABS, ROWS, SLAB_LEN), bf16),
+            shape((2 * WAFERS * POLY, SLAB_LEN), bf16),
             shape((SLABS, SLAB_BLOCKS * SHARE, TILE), bf16),
             shape((SLABS, TILE), jnp.int32),
         ),
@@ -456,6 +482,9 @@
         (vmem(), vmem(), vmem()),
         [buffer((SLABS, SLAB_BLOCKS * SHARE, TILE), f32)],
     )(scan_bounds - slab * SLAB_LEN, gathered, basis, basis_t, inverse, lane_weights)
+    cleaned = call(
+        clean_kernel, shape((SLABS, ROWS, SLAB_LEN), bf16), [vmem()] * 3, vmem()
+    )(gathered, basis_t, both)
     sums = lax.all_to_all(sums, SLAB_AXES, split_axis=0, concat_axis=0, tiled=True)
     flags, scans = call(
         scan_kernel,

time: 83.4 us -> 82.9 us (level)
  waiting for transfers between devices: 21.5 us -> 20.1 us
    all_to_all x1, waiting for transfers between devices: 6.7 us -> 5.31 us  [local(): lax.all_to_all(sums, SLAB_AXES, split_axis=0, concat_axis=0, tiled=True)]
    pallas_call x1 -> x2, Pallas kernels: 2.7 us -> 3.72 us  [the longest x1 2.34 us: local(): call(sums_kernel, (shape((2 * WAFERS * POLY, SLAB_LEN), bf16), shape((SLA...]
  transfers between devices with their start and end apart: 10 -> 10, of which waited for: 7 -> 7; matrix products, arithmetic and copies ran while one was open for 13% -> 13% of each run, Pallas kernels for 11% -> 13%
where the time goes in v5:
time: 82.9 us; the launch traced here: 81.7 us
  starting transfers between devices  30.3 us (37%)
  waiting for transfers between devices  20.1 us (24%)
  Pallas kernels  18.9 us (23%)
  other arithmetic  9.68 us (12%)
  local copies, waits for them, and re-layouts  1.29 us (2%)
  between operations  0.95 us (1%)
    all_to_all x1, starting transfers between devices, local(): lax.all_to_all(filtered, SLAB_AXES, split_axis=0, concat_axis=0, tiled=True)  8.73 us
    ppermute x6, starting transfers between devices, exchange(): lax.ppermute(value, axis, [(src, (src + step) % size) for src in range(si...  8.44 us
    ppermute x6, waiting for transfers between devices, exchange(): lax.ppermute(value, axis, [(src, (src + step) % size) for src in range(si...  7.63 us
    all_to_all x1, waiting for transfers between devices, local(): lax.all_to_all(filtered, SLAB_AXES, split_axis=0, concat_axis=0, tiled=True)  7.17 us
    pallas_call x1, Pallas kernels, local(): call(adjoint_kernel, shape((1, ROWS, SAMP), f32), [smem(), vmem(), vmem()...  6.17 us
    pallas_call x1, Pallas kernels, local(): call(forward_kernel, shape((SLABS, ROWS, SLAB_LEN + TILE), bf16), [hbm(),...  5.75 us
    all_to_all x1, waiting for transfers between devices, local(): lax.all_to_all(sums, SLAB_AXES, split_axis=0, concat_axis=0, tiled=True)  5.31 us
    all_to_all x1, starting transfers between devices, local(): lax.all_to_all(sums, SLAB_AXES, split_axis=0, concat_axis=0, tiled=True)  5.09 us
  transfers between devices with their start and end apart: 10, of which 7 were waited for; matrix products, arithmetic and copies ran while one was open for 13% of the time, Pallas kernels for 13%

profile of v5, /device:TPU:1, one launch (start us, length us, event | category | flops | bytes accessed | tf_op | source)
XLA Modules:
  0.0 81.7 jit_solution(4590719110171205420)
XLA Ops:
  0.6 5.8 %shard_map.86 = bf16[32,16,1152]{2,1,0:T(8,128)(2,1)} custom-call(bf16[1,16,32768]{2,1,0:T(8,128)(2,1)} %x_ref.1, bf16[16,8,129]{2,1,0:T(8,128)(2,1)} %bitcast.32, s32[1,8]{1,0:T(1,128)} %tiles_ref.1), custom_call_target="tpu_custom_call" | custom-call | bytes 21000000 | tf_op jit(solution)/shard_map/pallas_call | solution.py:446
  6.4 0.0 copy-start.2
  6.4 0.0 copy-start.3
  6.4 0.0 copy-start.4
  6.4 0.0 copy-start.1
  6.4 8.7 %all-to-all-start = ((bf16[32,16,1152]{2,1,0:T(8,128)(2,1)}), bf16[32,16,1152]{2,1,0:T(8,128)(2,1)S(1)}, u32[]{:S(2)}, u32[]{:S(2)}) async-start(bf16[32,16,1152]{2,1,0:T(8,128)(2,1)} %shard_map.86), calls=%async_computation | async-start | bytes 2359296 | tf_op jit(solution)/shard_map/all_to_all | solution.py:465
  15.3 0.1 fusion.5
  15.4 0.1 copy.14
  15.5 4.4 %cholesky.17 = f32[48,48]{1,0:T(8,128)S(1)} custom-call(f32[48,48]{1,0:T(8,128)S(1)} %fusion.3), custom_call_target="Cholesky" | custom-call | tf_op jit(solution)/shard_map/jit(cholesky)/cholesky | solution.py:422
  20.0 0.1 copy.12
  20.1 0.6 compare_reduce_fusion
  20.8 0.7 fusion
  21.4 3.7 %custom-call.6 = f32[1,48,48]{1,2,0:T(8,128)S(1)} custom-call(f32[1,48,48]{2,1,0:T(8,128)S(1)} %fusion), custom_call_target="InvertDiagBlocksLowerTriangular" | custom-call | tf_op jit(solution)/shard_map/triangular_solve | solution.py:423
  25.1 0.1 maximum_bitcast_fusion.basis_t_ref
  25.2 0.2 fusion.1
  25.5 0.2 fusion.6.inverse_ref
  25.7 7.2 %all-to-all-done.data_ref = bf16[32,16,1152]{2,1,0:T(8,128)(2,1)S(1)} async-done(((bf16[32,16,1152]{2,1,0:T(8,128)(2,1)}), bf16[32,16,1152]{2,1,0:T(8,128)(2,1)S(1)}, u32[]{:S(2)}, u32[]{:S(2)}) %all-to-all-start) | async-done | bytes 1179680 | tf_op jit(solution)/shard_map/all_to_all | solution.py:465
  32.9 0.1 broadcast_in_dim.8.weight_ref
  33.0 2.3 %shard_map.87 = (bf16[96,1024]{1,0:T(8,128)(2,1)S(1)}, bf16[32,32,128]{2,1,0:T(8,128)(2,1)}, s32[32,128]{1,0:T(8,128)S(1)}) custom-call(s32[1,32]{1,0:T(1,128)S(1)} %broadcast_subtract_fusion.bounds_ref, bf16[32,16,1152]{2,1,0:T(8,128)(2,1)S(1)} %all-to-all-done.data_ref, bf16[48,512]{1,0:T(8,128)(2,1)S(1)} %convert_element_type.36.basis_ref, ...), custom_call_target="tpu_custom_call" | custom-call | bytes 6000000 | tf_op jit(solution)/shard_map/pallas_call | solution.py:474
  35.3 5.1 %all-to-all-start.1 = ((bf16[32,32,128]{2,1,0:T(8,128)(2,1)}), bf16[32,32,128]{2,1,0:T(8,128)(2,1)S(1)}, u32[]{:S(2)}, u32[]{:S(2)}) async-start(bf16[32,32,128]{2,1,0:T(8,128)(2,1)} %get-tuple-element.17), calls=%async_computation.1 | async-start | bytes 524288 | tf_op jit(solution)/shard_map/all_to_all | solution.py:488
  40.5 0.1 dynamic_slice.19
  40.5 0.1 broadcast_in_dim.9
  40.6 0.1 broadcast_in_dim.10.weight_ref
  40.7 2.0 %shard_map.89 = (f32[256,128]{1,0:T(8,128)S(1)}, f32[24,128]{1,0:T(8,128)S(1)}) custom-call(s32[1,32]{1,0:T(1,128)S(1)} %copy-done.1, s32[32,128]{1,0:T(8,128)S(1)} %get-tuple-element.15.tiles_ref, f32[8,128]{1,0:T(8,128)S(1)} %broadcast_in_dim.10.weight_ref), custom_call_target="tpu_custom_call" | custom-call | bytes 6000000 | tf_op jit(solution)/shard_map/pallas_call | solution.py:489
  42.7 1.4 %shard_map.88 = bf16[32,16,1024]{2,1,0:T(8,128)(2,1)} custom-call(bf16[32,16,1152]{2,1,0:T(8,128)(2,1)S(1)} %all-to-all-done.data_ref, bf16[512,96]{1,0:T(8,128)(2,1)S(1)} %maximum_bitcast_fusion.basis_t_ref, bf16[96,1024]{1,0:T(8,128)(2,1)S(1)} %get-tuple-element.16.both_ref), custom_call_target="tpu_custom_call" | custom-call | bytes 6000000 | tf_op jit(solution)/shard_map/pallas_call | solution.py:485
  44.1 5.3 %all-to-all-done.1.sums_ref = bf16[32,32,128]{2,1,0:T(8,128)(2,1)S(1)} async-done(((bf16[32,32,128]{2,1,0:T(8,128)(2,1)}), bf16[32,32,128]{2,1,0:T(8,128)(2,1)S(1)}, u32[]{:S(2)}, u32[]{:S(2)}) %all-to-all-start.1) | async-done | bytes 262176 | tf_op jit(solution)/shard_map/all_to_all | solution.py:488
  49.4 4.0 %all-to-all-start.2 = ((bf16[32,16,1024]{2,1,0:T(8,128)(2,1)}), bf16[32,16,1024]{2,1,0:T(8,128)(2,1)S(1)}, u32[]{:S(2)}, u32[]{:S(2)}) async-start(bf16[32,16,1024]{2,1,0:T(8,128)(2,1)} %shard_map.88), calls=%async_computation.2 | async-start | bytes 2097152 | tf_op jit(solution)/shard_map/all_to_all | solution.py:497
  53.4 1.2 %shard_map.90.a_ref = f32[88,128]{1,0:T(8,128)S(1)} custom-call(s32[32,128]{1,0:T(8,128)S(1)} %get-tuple-element.15.tiles_ref, bf16[32,32,128]{2,1,0:T(8,128)(2,1)S(1)} %all-to-all-done.1.sums_ref, f32[24,128]{1,0:T(8,128)S(1)} %get-tuple-element.22.scan_ref), custom_call_target="tpu_custom_call" | custom-call | bytes 6000000 | tf_op jit(solution)/shard_map/pallas_call | solution.py:499
  54.6 3.8 %collective-permute-start.2 = (f32[88,128]{1,0:T(8,128)S(1)}, f32[88,128]{1,0:T(8,128)S(1)}, u32[]{:S(2)}, u32[]{:S(2)}) collective-permute-start(f32[88,128]{1,0:T(8,128)S(1)} %shard_map.90.a_ref), channel_id=1, source_target_pairs={{0,96},{32,0},{64,32},{96,64},{1,97},{33,1},{65,33},{97,65},{2,98}... | collective-permute-start | bytes 135176 | tf_op jit(solution)/shard_map/ppermute | solution.py:433
  58.4 0.0 collective-permute-start.1
  58.4 0.7 collective-permute-start
  59.1 0.4 collective-permute-done.2.d_ref
  59.6 3.6 %collective-permute-done.1.c_ref = f32[88,128]{1,0:T(8,128)S(1)} collective-permute-done((f32[88,128]{1,0:T(8,128)S(1)}, f32[88,128]{1,0:T(8,128)S(1)}, u32[]{:S(2)}, u32[]{:S(2)}) %collective-permute-start.1) | collective-permute-done | bytes 45088 | tf_op jit(solution)/shard_map/ppermute | solution.py:433
  63.1 0.2 collective-permute-done.b_ref
  63.3 2.8 %collective-permute-start.5 = (bf16[64,128]{1,0:T(8,128)(2,1)S(1)}, bf16[64,128]{1,0:T(8,128)(2,1)S(1)}, u32[]{:S(2)}, u32[]{:S(2)}) collective-permute-start(bf16[64,128]{1,0:T(8,128)(2,1)S(1)} %get-tuple-element.26), channel_id=1, source_target_pairs={{0,24},{8,0},{16,8},{24,16},{1,25},{9,1},{17,9},{25,17},{2,26},{10... | collective-permute-start | bytes 49160 | tf_op jit(solution)/shard_map/ppermute | solution.py:433
  66.2 0.5 collective-permute-start.4
  66.6 0.6 collective-permute-start.3
  67.3 1.1 %collective-permute-done.5 = bf16[64,128]{1,0:T(8,128)(2,1)S(1)} collective-permute-done((bf16[64,128]{1,0:T(8,128)(2,1)S(1)}, bf16[64,128]{1,0:T(8,128)(2,1)S(1)}, u32[]{:S(2)}, u32[]{:S(2)}) %collective-permute-start.5) | collective-permute-done | bytes 16416 | tf_op jit(solution)/shard_map/ppermute | solution.py:433
  68.4 2.3 %collective-permute-done.4 = bf16[64,128]{1,0:T(8,128)(2,1)S(1)} collective-permute-done((bf16[64,128]{1,0:T(8,128)(2,1)S(1)}, bf16[64,128]{1,0:T(8,128)(2,1)S(1)}, u32[]{:S(2)}, u32[]{:S(2)}) %collective-permute-start.4) | collective-permute-done | bytes 16416 | tf_op jit(solution)/shard_map/ppermute | solution.py:433
  70.7 0.0 collective-permute-done.3
  70.7 0.1 pad_maximum_fusion
  70.8 0.0 all-to-all-done.2.data_ref
  70.8 4.0 %collective-permute-start.6 = (f32[16,1,128]{2,1,0:T(1,128)S(1)}, f32[16,1,128]{2,1,0:T(1,128)S(1)}, u32[]{:S(2)}, u32[]{:S(2)}) collective-permute-start(f32[16,1,128]{2,1,0:T(1,128)S(1)} %constant_dynamic-slice_fusion), channel_id=1, source_target_pairs={{0,4},{1,26},{2,36},{3,57},{4,67},{5,92},{6,99},{7,127},{8,12},{9,... | collective-permute-start | bytes 24584 | tf_op jit(solution)/shard_map/ppermute | solution.py:529
  74.9 0.1 pad_maximum_fusion.1
  74.9 0.0 copy-done
  74.9 6.2 %shard_map.92 = f32[1,16,32768]{2,1,0:T(8,128)} custom-call(s32[32,128]{1,0:T(8,128)S(1)} %get-tuple-element.15.tiles_ref, f32[256,128]{1,0:T(8,128)S(1)} %get-tuple-element.20.flags_ref, bf16[32,16,1024]{2,1,0:T(8,128)(2,1)S(1)} %all-to-all-done.2.data_ref, bf16[16,16,128]{2,1,0:T(8,128)(2,1)S(1)} %bitcast.34, bf16[16,8,129]{2,1,0:T(8,128)(2,1)S(1)} %bitcast.33), custom_call_target="tpu_custom_call" | custom-call | bytes 27000000 | tf_op jit(solution)/shard_map/pallas_call | solution.py:530
  81.1 0.0 collective-permute-done.6
  81.1 0.6 copy.16
  (20 shorter events, 0.3 us)
Async XLA Ops:
  6.4 8.8 %copy-start.2 = (f32[2,512]{1,0:T(2,128)S(1)}, f32[2,512]{1,0:T(2,128)}, u32[]{:S(2)}) copy-start(f32[2,512]{1,0:T(2,128)} %param.12) | copy-start | bytes 12292
  6.4 8.8 %copy-start.3 = (s32[512]{0:T(512)S(1)}, s32[512]{0:T(512)}, u32[]{:S(2)}) copy-start(s32[512]{0:T(512)} %param.13) | copy-start | bytes 6148
  6.4 13.7 %copy-start.4 = (bf16[1,512]{1,0:T(2,128)(2,1)S(1)}, bf16[1,512]{1,0:T(2,128)(2,1)}, u32[]{:S(2)}) copy-start(bf16[1,512]{1,0:T(2,128)(2,1)} %param.11) | copy-start | bytes 3076
  6.4 18.8 %copy-start.1 = (s32[1,32]{1,0:T(1,128)S(1)}, s32[1,32]{1,0:T(1,128)}, u32[]{:S(2)}) copy-start(s32[1,32]{1,0:T(1,128)} %bounds_ref.1) | copy-start | bytes 388
  6.4 26.4 %all-to-all-start = ((bf16[32,16,1152]{2,1,0:T(8,128)(2,1)}), bf16[32,16,1152]{2,1,0:T(8,128)(2,1)S(1)}, u32[]{:S(2)}, u32[]{:S(2)}) async-start(bf16[32,16,1152]{2,1,0:T(8,128)(2,1)} %shard_map.86), calls=%async_computation | async-start | bytes 2359296 | tf_op jit(solution)/shard_map/all_to_all | solution.py:465
  35.3 14.1 %all-to-all-start.1 = ((bf16[32,32,128]{2,1,0:T(8,128)(2,1)}), bf16[32,32,128]{2,1,0:T(8,128)(2,1)S(1)}, u32[]{:S(2)}, u32[]{:S(2)}) async-start(bf16[32,32,128]{2,1,0:T(8,128)(2,1)} %get-tuple-element.17), calls=%async_computation.1 | async-start | bytes 524288 | tf_op jit(solution)/shard_map/all_to_all | solution.py:488
  49.4 25.5 %copy-start = (bf16[1,16,8,129]{3,2,1,0:T(8,128)(2,1)S(1)}, bf16[1,16,8,129]{3,2,1,0:T(8,128)(2,1)}, u32[]{:S(2)}) copy-start(bf16[1,16,8,129]{3,2,1,0:T(8,128)(2,1)} %param.8) | copy-start | bytes 99076
  49.4 21.4 %all-to-all-start.2 = ((bf16[32,16,1024]{2,1,0:T(8,128)(2,1)}), bf16[32,16,1024]{2,1,0:T(8,128)(2,1)S(1)}, u32[]{:S(2)}, u32[]{:S(2)}) async-start(bf16[32,16,1024]{2,1,0:T(8,128)(2,1)} %shard_map.88), calls=%async_computation.2 | async-start | bytes 2097152 | tf_op jit(solution)/shard_map/all_to_all | solution.py:497
  54.6 5.0 %collective-permute-start.2 = (f32[88,128]{1,0:T(8,128)S(1)}, f32[88,128]{1,0:T(8,128)S(1)}, u32[]{:S(2)}, u32[]{:S(2)}) collective-permute-start(f32[88,128]{1,0:T(8,128)S(1)} %shard_map.90.a_ref), channel_id=1, source_target_pairs={{0,96},{32,0},{64,32},{96,64},{1,97},{33,1},{65,33},{97,65},{2,98}... | collective-permute-start | bytes 135176 | tf_op jit(solution)/shard_map/ppermute | solution.py:433
  58.4 4.7 %collective-permute-start.1 = (f32[88,128]{1,0:T(8,128)S(1)}, f32[88,128]{1,0:T(8,128)S(1)}, u32[]{:S(2)}, u32[]{:S(2)}) collective-permute-start(f32[88,128]{1,0:T(8,128)S(1)} %shard_map.90.a_ref), channel_id=1, source_target_pairs={{0,64},{32,96},{64,0},{96,32},{1,65},{33,97},{65,1},{97,33},{2,66}... | collective-permute-start | bytes 135176 | tf_op jit(solution)/shard_map/ppermute | solution.py:433
  58.4 4.9 %collective-permute-start = (f32[88,128]{1,0:T(8,128)S(1)}, f32[88,128]{1,0:T(8,128)S(1)}, u32[]{:S(2)}, u32[]{:S(2)}) collective-permute-start(f32[88,128]{1,0:T(8,128)S(1)} %shard_map.90.a_ref), channel_id=1, source_target_pairs={{0,32},{32,64},{64,96},{96,0},{1,33},{33,65},{65,97},{97,1},{2,34}... | collective-permute-start | bytes 135176 | tf_op jit(solution)/shard_map/ppermute | solution.py:433
  63.3 5.1 %collective-permute-start.5 = (bf16[64,128]{1,0:T(8,128)(2,1)S(1)}, bf16[64,128]{1,0:T(8,128)(2,1)S(1)}, u32[]{:S(2)}, u32[]{:S(2)}) collective-permute-start(bf16[64,128]{1,0:T(8,128)(2,1)S(1)} %get-tuple-element.26), channel_id=1, source_target_pairs={{0,24},{8,0},{16,8},{24,16},{1,25},{9,1},{17,9},{25,17},{2,26},{10... | collective-permute-start | bytes 49160 | tf_op jit(solution)/shard_map/ppermute | solution.py:433
  66.2 4.5 %collective-permute-start.4 = (bf16[64,128]{1,0:T(8,128)(2,1)S(1)}, bf16[64,128]{1,0:T(8,128)(2,1)S(1)}, u32[]{:S(2)}, u32[]{:S(2)}) collective-permute-start(bf16[64,128]{1,0:T(8,128)(2,1)S(1)} %get-tuple-element.26), channel_id=1, source_target_pairs={{0,16},{8,24},{16,0},{24,8},{1,17},{9,25},{17,1},{25,9},{2,18},{10... | collective-permute-start | bytes 49160 | tf_op jit(solution)/shard_map/ppermute | solution.py:433
  66.6 4.1 %collective-permute-start.3 = (bf16[64,128]{1,0:T(8,128)(2,1)S(1)}, bf16[64,128]{1,0:T(8,128)(2,1)S(1)}, u32[]{:S(2)}, u32[]{:S(2)}) collective-permute-start(bf16[64,128]{1,0:T(8,128)(2,1)S(1)} %get-tuple-element.26), channel_id=1, source_target_pairs={{0,8},{8,16},{16,24},{24,0},{1,9},{9,17},{17,25},{25,1},{2,10},{10... | collective-permute-start | bytes 49160 | tf_op jit(solution)/shard_map/ppermute | solution.py:433
  70.8 10.3 %collective-permute-start.6 = (f32[16,1,128]{2,1,0:T(1,128)S(1)}, f32[16,1,128]{2,1,0:T(1,128)S(1)}, u32[]{:S(2)}, u32[]{:S(2)}) collective-permute-start(f32[16,1,128]{2,1,0:T(1,128)S(1)} %constant_dynamic-slice_fusion), channel_id=1, source_target_pairs={{0,4},{1,26},{2,36},{3,57},{4,67},{5,92},{6,99},{7,127},{8,12},{9,... | collective-permute-start | bytes 24584 | tf_op jit(solution)/shard_map/ppermute | solution.py:529

commit v6 on v5

--- a/solution.py
+++ b/solution.py
@@ -235,10 +235,13 @@
     rest = (coef - high.astype(jnp.float32)).astype(jnp.bfloat16)
     both = jnp.concatenate([high, rest], axis=0)
     both_ref[...] = both
-    cleaned = fit(data, basis_t_ref[...], both)
     flags = count_flags(bounds_ref, SLAB_BLOCKS, 0)
     for block in range(SLAB_BLOCKS):
-        part = cleaned[:, block * TILE : (block + 1) * TILE].astype(jnp.float32)
+        if block % 2 == 0:
+            pair = slice(block * TILE, (block + 2) * TILE)
+            cleaned = fit(data[:, pair], basis_t_ref[...], both[:, pair])
+        inner = block % 2
+        part = cleaned[:, inner * TILE : (inner + 1) * TILE].astype(jnp.float32)
         weighted = (part * weight_ref[...]).reshape(DET // TILE, TILE, TILE)
         total = jnp.sum(weighted, axis=0) * flags[block : block + 1, :]
         for quad in range(QUADS):
@@ -398,8 +401,8 @@
                     make_residual(band + 1, index)
                 if band > 0:
                     before = join(band - 1, index, before, spill)
-        if band >= 2:
-            out_copy(band - 2).start()
+            if det == 0 and band >= 2:
+                out_copy(band - 2).start()
     final = after[(BANDS - 1) % 2][(BAND_BLOCKS - 1) * ROWS :, :]
     write_block(BLOCKS - 1, before, pltpu.roll(final, HALF, 1))
     out_copy(BANDS - 1).start()

time: 82.9 us -> 82.9 us (level)
  no operation moved by 1% of the time
where the time goes in v6:
time: 82.9 us; the launch traced here: 81.7 us
  starting transfers between devices  30.2 us (36%)
  waiting for transfers between devices  20.1 us (24%)
  Pallas kernels  18.9 us (23%)
  other arithmetic  9.68 us (12%)
  local copies, waits for them, and re-layouts  1.29 us (2%)
  between operations  0.94 us (1%)
    all_to_all x1, starting transfers between devices, local(): lax.all_to_all(filtered, SLAB_AXES, split_axis=0, concat_axis=0, tiled=True)  8.73 us
    ppermute x6, starting transfers between devices, exchange(): lax.ppermute(value, axis, [(src, (src + step) % size) for src in range(si...  8.44 us
    ppermute x6, waiting for transfers between devices, exchange(): lax.ppermute(value, axis, [(src, (src + step) % size) for src in range(si...  7.63 us
    all_to_all x1, waiting for transfers between devices, local(): lax.all_to_all(filtered, SLAB_AXES, split_axis=0, concat_axis=0, tiled=True)  7.17 us
    pallas_call x1, Pallas kernels, local(): call(adjoint_kernel, shape((1, ROWS, SAMP), f32), [smem(), vmem(), vmem()...  6.12 us
    pallas_call x1, Pallas kernels, local(): call(forward_kernel, shape((SLABS, ROWS, SLAB_LEN + TILE), bf16), [hbm(),...  5.75 us
    all_to_all x1, waiting for transfers between devices, local(): lax.all_to_all(sums, SLAB_AXES, split_axis=0, concat_axis=0, tiled=True)  5.3 us
    all_to_all x1, starting transfers between devices, local(): lax.all_to_all(sums, SLAB_AXES, split_axis=0, concat_axis=0, tiled=True)  5.08 us
  transfers between devices with their start and end apart: 10, of which 7 were waited for; matrix products, arithmetic and copies ran while one was open for 13% of the time, Pallas kernels for 13%

profile of v6, /device:TPU:1, one launch (start us, length us, event | category | flops | bytes accessed | tf_op | source)
XLA Modules:
  0.0 81.7 jit_solution(2744331642356322792)
XLA Ops:
  0.6 5.8 %shard_map.86 = bf16[32,16,1152]{2,1,0:T(8,128)(2,1)} custom-call(bf16[1,16,32768]{2,1,0:T(8,128)(2,1)} %x_ref.1, bf16[16,8,129]{2,1,0:T(8,128)(2,1)} %bitcast.32, s32[1,8]{1,0:T(1,128)} %tiles_ref.1), custom_call_target="tpu_custom_call" | custom-call | bytes 21000000 | tf_op jit(solution)/shard_map/pallas_call | solution.py:449
  6.4 0.0 copy-start.2
  6.4 0.0 copy-start.3
  6.4 0.0 copy-start.4
  6.4 0.0 copy-start.1
  6.4 8.7 %all-to-all-start = ((bf16[32,16,1152]{2,1,0:T(8,128)(2,1)}), bf16[32,16,1152]{2,1,0:T(8,128)(2,1)S(1)}, u32[]{:S(2)}, u32[]{:S(2)}) async-start(bf16[32,16,1152]{2,1,0:T(8,128)(2,1)} %shard_map.86), calls=%async_computation | async-start | bytes 2359296 | tf_op jit(solution)/shard_map/all_to_all | solution.py:468
  15.2 0.0 copy-done.2
  15.3 0.1 fusion.5
  15.4 0.1 copy.14
  15.5 4.4 %cholesky.17 = f32[48,48]{1,0:T(8,128)S(1)} custom-call(f32[48,48]{1,0:T(8,128)S(1)} %fusion.3), custom_call_target="Cholesky" | custom-call | tf_op jit(solution)/shard_map/jit(cholesky)/cholesky | solution.py:425
  20.0 0.1 copy.12
  20.1 0.6 compare_reduce_fusion
  20.8 0.7 fusion
  21.4 3.7 %custom-call.6 = f32[1,48,48]{1,2,0:T(8,128)S(1)} custom-call(f32[1,48,48]{2,1,0:T(8,128)S(1)} %fusion), custom_call_target="InvertDiagBlocksLowerTriangular" | custom-call | tf_op jit(solution)/shard_map/triangular_solve | solution.py:426
  25.1 0.1 maximum_bitcast_fusion.basis_t_ref
  25.2 0.2 fusion.1
  25.5 0.2 fusion.6.inverse_ref
  25.7 7.2 %all-to-all-done.data_ref = bf16[32,16,1152]{2,1,0:T(8,128)(2,1)S(1)} async-done(((bf16[32,16,1152]{2,1,0:T(8,128)(2,1)}), bf16[32,16,1152]{2,1,0:T(8,128)(2,1)S(1)}, u32[]{:S(2)}, u32[]{:S(2)}) %all-to-all-start) | async-done | bytes 1179680 | tf_op jit(solution)/shard_map/all_to_all | solution.py:468
  32.9 0.1 broadcast_in_dim.8.weight_ref
  33.0 2.3 %shard_map.87 = (bf16[96,1024]{1,0:T(8,128)(2,1)S(1)}, bf16[32,32,128]{2,1,0:T(8,128)(2,1)}, s32[32,128]{1,0:T(8,128)S(1)}) custom-call(s32[1,32]{1,0:T(1,128)S(1)} %broadcast_subtract_fusion.bounds_ref, bf16[32,16,1152]{2,1,0:T(8,128)(2,1)S(1)} %all-to-all-done.data_ref, bf16[48,512]{1,0:T(8,128)(2,1)S(1)} %convert_element_type.36.basis_ref, ...), custom_call_target="tpu_custom_call" | custom-call | bytes 6000000 | tf_op jit(solution)/shard_map/pallas_call | solution.py:477
  35.3 5.1 %all-to-all-start.1 = ((bf16[32,32,128]{2,1,0:T(8,128)(2,1)}), bf16[32,32,128]{2,1,0:T(8,128)(2,1)S(1)}, u32[]{:S(2)}, u32[]{:S(2)}) async-start(bf16[32,32,128]{2,1,0:T(8,128)(2,1)} %get-tuple-element.17), calls=%async_computation.1 | async-start | bytes 524288 | tf_op jit(solution)/shard_map/all_to_all | solution.py:491
  40.5 0.1 dynamic_slice.19
  40.5 0.1 broadcast_in_dim.9
  40.6 0.1 broadcast_in_dim.10.weight_ref
  40.7 2.0 %shard_map.89 = (f32[256,128]{1,0:T(8,128)S(1)}, f32[24,128]{1,0:T(8,128)S(1)}) custom-call(s32[1,32]{1,0:T(1,128)S(1)} %copy-done.1, s32[32,128]{1,0:T(8,128)S(1)} %get-tuple-element.15.tiles_ref, f32[8,128]{1,0:T(8,128)S(1)} %broadcast_in_dim.10.weight_ref), custom_call_target="tpu_custom_call" | custom-call | bytes 6000000 | tf_op jit(solution)/shard_map/pallas_call | solution.py:492
  42.7 1.4 %shard_map.88 = bf16[32,16,1024]{2,1,0:T(8,128)(2,1)} custom-call(bf16[32,16,1152]{2,1,0:T(8,128)(2,1)S(1)} %all-to-all-done.data_ref, bf16[512,96]{1,0:T(8,128)(2,1)S(1)} %maximum_bitcast_fusion.basis_t_ref, bf16[96,1024]{1,0:T(8,128)(2,1)S(1)} %get-tuple-element.16.both_ref), custom_call_target="tpu_custom_call" | custom-call | bytes 6000000 | tf_op jit(solution)/shard_map/pallas_call | solution.py:488
  44.1 5.3 %all-to-all-done.1.sums_ref = bf16[32,32,128]{2,1,0:T(8,128)(2,1)S(1)} async-done(((bf16[32,32,128]{2,1,0:T(8,128)(2,1)}), bf16[32,32,128]{2,1,0:T(8,128)(2,1)S(1)}, u32[]{:S(2)}, u32[]{:S(2)}) %all-to-all-start.1) | async-done | bytes 262176 | tf_op jit(solution)/shard_map/all_to_all | solution.py:491
  49.4 4.0 %all-to-all-start.2 = ((bf16[32,16,1024]{2,1,0:T(8,128)(2,1)}), bf16[32,16,1024]{2,1,0:T(8,128)(2,1)S(1)}, u32[]{:S(2)}, u32[]{:S(2)}) async-start(bf16[32,16,1024]{2,1,0:T(8,128)(2,1)} %shard_map.88), calls=%async_computation.2 | async-start | bytes 2097152 | tf_op jit(solution)/shard_map/all_to_all | solution.py:500
  53.4 1.2 %shard_map.90.a_ref = f32[88,128]{1,0:T(8,128)S(1)} custom-call(s32[32,128]{1,0:T(8,128)S(1)} %get-tuple-element.15.tiles_ref, bf16[32,32,128]{2,1,0:T(8,128)(2,1)S(1)} %all-to-all-done.1.sums_ref, f32[24,128]{1,0:T(8,128)S(1)} %get-tuple-element.22.scan_ref), custom_call_target="tpu_custom_call" | custom-call | bytes 6000000 | tf_op jit(solution)/shard_map/pallas_call | solution.py:502
  54.6 3.8 %collective-permute-start.2 = (f32[88,128]{1,0:T(8,128)S(1)}, f32[88,128]{1,0:T(8,128)S(1)}, u32[]{:S(2)}, u32[]{:S(2)}) collective-permute-start(f32[88,128]{1,0:T(8,128)S(1)} %shard_map.90.a_ref), channel_id=1, source_target_pairs={{0,96},{32,0},{64,32},{96,64},{1,97},{33,1},{65,33},{97,65},{2,98}... | collective-permute-start | bytes 135176 | tf_op jit(solution)/shard_map/ppermute | solution.py:436
  58.4 0.0 collective-permute-start.1
  58.4 0.7 collective-permute-start
  59.1 0.4 collective-permute-done.2.d_ref
  59.6 3.6 %collective-permute-done.1.c_ref = f32[88,128]{1,0:T(8,128)S(1)} collective-permute-done((f32[88,128]{1,0:T(8,128)S(1)}, f32[88,128]{1,0:T(8,128)S(1)}, u32[]{:S(2)}, u32[]{:S(2)}) %collective-permute-start.1) | collective-permute-done | bytes 45088 | tf_op jit(solution)/shard_map/ppermute | solution.py:436
  63.1 0.2 collective-permute-done.b_ref
  63.3 2.8 %collective-permute-start.5 = (bf16[64,128]{1,0:T(8,128)(2,1)S(1)}, bf16[64,128]{1,0:T(8,128)(2,1)S(1)}, u32[]{:S(2)}, u32[]{:S(2)}) collective-permute-start(bf16[64,128]{1,0:T(8,128)(2,1)S(1)} %get-tuple-element.26), channel_id=1, source_target_pairs={{0,24},{8,0},{16,8},{24,16},{1,25},{9,1},{17,9},{25,17},{2,26},{10... | collective-permute-start | bytes 49160 | tf_op jit(solution)/shard_map/ppermute | solution.py:436
  66.2 0.5 collective-permute-start.4
  66.6 0.6 collective-permute-start.3
  67.3 1.1 %collective-permute-done.5 = bf16[64,128]{1,0:T(8,128)(2,1)S(1)} collective-permute-done((bf16[64,128]{1,0:T(8,128)(2,1)S(1)}, bf16[64,128]{1,0:T(8,128)(2,1)S(1)}, u32[]{:S(2)}, u32[]{:S(2)}) %collective-permute-start.5) | collective-permute-done | bytes 16416 | tf_op jit(solution)/shard_map/ppermute | solution.py:436
  68.4 2.3 %collective-permute-done.4 = bf16[64,128]{1,0:T(8,128)(2,1)S(1)} collective-permute-done((bf16[64,128]{1,0:T(8,128)(2,1)S(1)}, bf16[64,128]{1,0:T(8,128)(2,1)S(1)}, u32[]{:S(2)}, u32[]{:S(2)}) %collective-permute-start.4) | collective-permute-done | bytes 16416 | tf_op jit(solution)/shard_map/ppermute | solution.py:436
  70.7 0.0 collective-permute-done.3
  70.7 0.1 pad_maximum_fusion
  70.8 0.0 all-to-all-done.2.data_ref
  70.8 4.0 %collective-permute-start.6 = (f32[16,1,128]{2,1,0:T(1,128)S(1)}, f32[16,1,128]{2,1,0:T(1,128)S(1)}, u32[]{:S(2)}, u32[]{:S(2)}) collective-permute-start(f32[16,1,128]{2,1,0:T(1,128)S(1)} %constant_dynamic-slice_fusion), channel_id=1, source_target_pairs={{0,4},{1,26},{2,36},{3,57},{4,67},{5,92},{6,99},{7,127},{8,12},{9,... | collective-permute-start | bytes 24584 | tf_op jit(solution)/shard_map/ppermute | solution.py:532
  74.9 0.1 pad_maximum_fusion.1
  75.0 6.1 %shard_map.92 = f32[1,16,32768]{2,1,0:T(8,128)} custom-call(s32[32,128]{1,0:T(8,128)S(1)} %get-tuple-element.15.tiles_ref, f32[256,128]{1,0:T(8,128)S(1)} %get-tuple-element.20.flags_ref, bf16[32,16,1024]{2,1,0:T(8,128)(2,1)S(1)} %all-to-all-done.2.data_ref, bf16[16,16,128]{2,1,0:T(8,128)(2,1)S(1)} %bitcast.34, bf16[16,8,129]{2,1,0:T(8,128)(2,1)S(1)} %bitcast.33), custom_call_target="tpu_custom_call" | custom-call | bytes 27000000 | tf_op jit(solution)/shard_map/pallas_call | solution.py:533
  81.1 0.0 collective-permute-done.6
  81.1 0.6 copy.16
  (20 shorter events, 0.3 us)
Async XLA Ops:
  6.4 8.8 %copy-start.2 = (f32[2,512]{1,0:T(2,128)S(1)}, f32[2,512]{1,0:T(2,128)}, u32[]{:S(2)}) copy-start(f32[2,512]{1,0:T(2,128)} %param.12) | copy-start | bytes 12292
  6.4 8.8 %copy-start.3 = (s32[512]{0:T(512)S(1)}, s32[512]{0:T(512)}, u32[]{:S(2)}) copy-start(s32[512]{0:T(512)} %param.13) | copy-start | bytes 6148
  6.4 13.7 %copy-start.4 = (bf16[1,512]{1,0:T(2,128)(2,1)S(1)}, bf16[1,512]{1,0:T(2,128)(2,1)}, u32[]{:S(2)}) copy-start(bf16[1,512]{1,0:T(2,128)(2,1)} %param.11) | copy-start | bytes 3076
  6.4 18.8 %copy-start.1 = (s32[1,32]{1,0:T(1,128)S(1)}, s32[1,32]{1,0:T(1,128)}, u32[]{:S(2)}) copy-start(s32[1,32]{1,0:T(1,128)} %bounds_ref.1) | copy-start | bytes 388
  6.4 26.4 %all-to-all-start = ((bf16[32,16,1152]{2,1,0:T(8,128)(2,1)}), bf16[32,16,1152]{2,1,0:T(8,128)(2,1)S(1)}, u32[]{:S(2)}, u32[]{:S(2)}) async-start(bf16[32,16,1152]{2,1,0:T(8,128)(2,1)} %shard_map.86), calls=%async_computation | async-start | bytes 2359296 | tf_op jit(solution)/shard_map/all_to_all | solution.py:468
  35.3 14.1 %all-to-all-start.1 = ((bf16[32,32,128]{2,1,0:T(8,128)(2,1)}), bf16[32,32,128]{2,1,0:T(8,128)(2,1)S(1)}, u32[]{:S(2)}, u32[]{:S(2)}) async-start(bf16[32,32,128]{2,1,0:T(8,128)(2,1)} %get-tuple-element.17), calls=%async_computation.1 | async-start | bytes 524288 | tf_op jit(solution)/shard_map/all_to_all | solution.py:491
  49.4 25.5 %copy-start = (bf16[1,16,8,129]{3,2,1,0:T(8,128)(2,1)S(1)}, bf16[1,16,8,129]{3,2,1,0:T(8,128)(2,1)}, u32[]{:S(2)}) copy-start(bf16[1,16,8,129]{3,2,1,0:T(8,128)(2,1)} %param.8) | copy-start | bytes 99076
  49.4 21.4 %all-to-all-start.2 = ((bf16[32,16,1024]{2,1,0:T(8,128)(2,1)}), bf16[32,16,1024]{2,1,0:T(8,128)(2,1)S(1)}, u32[]{:S(2)}, u32[]{:S(2)}) async-start(bf16[32,16,1024]{2,1,0:T(8,128)(2,1)} %shard_map.88), calls=%async_computation.2 | async-start | bytes 2097152 | tf_op jit(solution)/shard_map/all_to_all | solution.py:500
  54.6 5.0 %collective-permute-start.2 = (f32[88,128]{1,0:T(8,128)S(1)}, f32[88,128]{1,0:T(8,128)S(1)}, u32[]{:S(2)}, u32[]{:S(2)}) collective-permute-start(f32[88,128]{1,0:T(8,128)S(1)} %shard_map.90.a_ref), channel_id=1, source_target_pairs={{0,96},{32,0},{64,32},{96,64},{1,97},{33,1},{65,33},{97,65},{2,98}... | collective-permute-start | bytes 135176 | tf_op jit(solution)/shard_map/ppermute | solution.py:436
  58.4 4.7 %collective-permute-start.1 = (f32[88,128]{1,0:T(8,128)S(1)}, f32[88,128]{1,0:T(8,128)S(1)}, u32[]{:S(2)}, u32[]{:S(2)}) collective-permute-start(f32[88,128]{1,0:T(8,128)S(1)} %shard_map.90.a_ref), channel_id=1, source_target_pairs={{0,64},{32,96},{64,0},{96,32},{1,65},{33,97},{65,1},{97,33},{2,66}... | collective-permute-start | bytes 135176 | tf_op jit(solution)/shard_map/ppermute | solution.py:436
  58.4 4.9 %collective-permute-start = (f32[88,128]{1,0:T(8,128)S(1)}, f32[88,128]{1,0:T(8,128)S(1)}, u32[]{:S(2)}, u32[]{:S(2)}) collective-permute-start(f32[88,128]{1,0:T(8,128)S(1)} %shard_map.90.a_ref), channel_id=1, source_target_pairs={{0,32},{32,64},{64,96},{96,0},{1,33},{33,65},{65,97},{97,1},{2,34}... | collective-permute-start | bytes 135176 | tf_op jit(solution)/shard_map/ppermute | solution.py:436
  63.3 5.0 %collective-permute-start.5 = (bf16[64,128]{1,0:T(8,128)(2,1)S(1)}, bf16[64,128]{1,0:T(8,128)(2,1)S(1)}, u32[]{:S(2)}, u32[]{:S(2)}) collective-permute-start(bf16[64,128]{1,0:T(8,128)(2,1)S(1)} %get-tuple-element.26), channel_id=1, source_target_pairs={{0,24},{8,0},{16,8},{24,16},{1,25},{9,1},{17,9},{25,17},{2,26},{10... | collective-permute-start | bytes 49160 | tf_op jit(solution)/shard_map/ppermute | solution.py:436
  66.2 4.5 %collective-permute-start.4 = (bf16[64,128]{1,0:T(8,128)(2,1)S(1)}, bf16[64,128]{1,0:T(8,128)(2,1)S(1)}, u32[]{:S(2)}, u32[]{:S(2)}) collective-permute-start(bf16[64,128]{1,0:T(8,128)(2,1)S(1)} %get-tuple-element.26), channel_id=1, source_target_pairs={{0,16},{8,24},{16,0},{24,8},{1,17},{9,25},{17,1},{25,9},{2,18},{10... | collective-permute-start | bytes 49160 | tf_op jit(solution)/shard_map/ppermute | solution.py:436
  66.6 4.1 %collective-permute-start.3 = (bf16[64,128]{1,0:T(8,128)(2,1)S(1)}, bf16[64,128]{1,0:T(8,128)(2,1)S(1)}, u32[]{:S(2)}, u32[]{:S(2)}) collective-permute-start(bf16[64,128]{1,0:T(8,128)(2,1)S(1)} %get-tuple-element.26), channel_id=1, source_target_pairs={{0,8},{8,16},{16,24},{24,0},{1,9},{9,17},{17,25},{25,1},{2,10},{10... | collective-permute-start | bytes 49160 | tf_op jit(solution)/shard_map/ppermute | solution.py:436
  70.8 10.3 %collective-permute-start.6 = (f32[16,1,128]{2,1,0:T(1,128)S(1)}, f32[16,1,128]{2,1,0:T(1,128)S(1)}, u32[]{:S(2)}, u32[]{:S(2)}) collective-permute-start(f32[16,1,128]{2,1,0:T(1,128)S(1)} %constant_dynamic-slice_fusion), channel_id=1, source_target_pairs={{0,4},{1,26},{2,36},{3,57},{4,67},{5,92},{6,99},{7,127},{8,12},{9,... | collective-permute-start | bytes 24584 | tf_op jit(solution)/shard_map/ppermute | solution.py:532
